TPU v7x, 512 devices: a whole 4x4x16 slice. The times are simulated.
512 devices in a mesh: group: 8 (over y, core), slot: 16 (over z), ctx: 4 (over x).
Axes of the slice: x: 4, y: 4, z: 16, core: 2. Of those that a mesh axis runs over, the one named last changes fastest.
Arguments:
- queries: bfloat16 [8, 16, 512, 4096], P('group', 'slot', 'ctx'), may hold values from -0.5 to 0.5
- keys: bfloat16 [8, 16, 512, 4096], P('group', 'slot', 'ctx'), may hold values from -0.5 to 0.5
- values: bfloat16 [8, 16, 512, 4096], P('group', 'slot', 'ctx'), may hold values from -6 to 6
- lengths: int32 [8, 16], P('group', 'slot'), may hold values from 1 to 512
- rewards: float32 [8, 16], P('group', 'slot'), may hold values from 0 to 4
- decay_rate: float32 [32], replicated, may hold values from 0.0002 to 0.03
- prompt_state: float32 [8, 4096, 128], P('group', ('slot', 'ctx')), may hold values from -6 to 6
Outputs:
- key_grad: bfloat16 [8, 16, 512, 4096], P('group', 'slot', 'ctx')
- prompt_grad: float32 [8, 4096, 128], P('group', ('slot', 'ctx'))
All inputs are finite; a program needn't handle non-finite values.
Results may differ from a plain program's by a relative error of at most 0.0039.
Values sent between devices are 32-bit elements; how exact they have to be, the bound alone decides.
No kernel may reach another device: no remote copies, remote signals or barrier semaphores. Data moves between devices by JAX's collectives and lax.ppermute only.
A program may use at most 64 MiB of HBM per device.

v0:
```python
import jax
import jax.numpy as jnp
from jax import lax
from jax.sharding import PartitionSpec as P

loss_scale = 16.0
highest = lax.Precision.HIGHEST


def prefix(part, axis, combine, identity, reverse):
    count = lax.axis_size(axis)
    place = lax.axis_index(axis)
    ahead = count - 1 - place if reverse else place
    gathered = jax.tree.map(lambda a: lax.all_gather(a, axis), part)
    state = jax.tree.map(lambda a, e: jnp.zeros_like(a) + jnp.asarray(e, a.dtype), part, identity)

    def one(turn, state):
        source = count - 1 - turn if reverse else turn
        return combine(
            state, jax.tree.map(lambda a: lax.dynamic_index_in_dim(a, source, 0, False), gathered)
        )

    return lax.fori_loop(0, ahead, one, state)


def carry_forward(earlier, latter):
    return (earlier[0] * latter[0], latter[0][:, None, None] * earlier[1] + latter[1])


def carry_backward(earlier, latter):
    return (earlier[0] * latter[0], latter[1] + latter[0][:, None, None] * earlier[1])


def shards(queries, keys, values, lengths, rewards, decay_rate, prompt_state):
    block_len = queries.shape[2]
    width_all = queries.shape[3]
    head_count = decay_rate.shape[0]
    head_dim = width_all // head_count
    ctx_index = lax.axis_index("ctx")
    length = lengths[0, 0]
    reward = rewards[0, 0]
    token_total = lax.psum(length.astype(jnp.float32), ("group", "slot"))
    reward_total = lax.psum(reward, "slot")
    advantage = reward - reward_total / lax.axis_size("slot")
    factor = loss_scale * advantage * (lax.axis_size("group") * lax.axis_size("slot")) / token_total
    positions = ctx_index * block_len + jnp.arange(block_len, dtype=jnp.int32)
    keep_mask = (positions < length).astype(jnp.float32)
    keep_low = keep_mask.astype(jnp.bfloat16)[:, None, None]
    query_rows = queries[0, 0].reshape(block_len, head_count, head_dim)
    key_rows = keys[0, 0].reshape(block_len, head_count, head_dim) * keep_low
    value_rows = values[0, 0].reshape(block_len, head_count, head_dim) * keep_low
    query_f = query_rows.astype(jnp.float32)
    value_f = value_rows.astype(jnp.float32)
    place_f = jnp.arange(block_len, dtype=jnp.float32)
    offset = place_f[:, None] - place_f[None, :]
    decay_grid = jnp.where(
        offset[None] >= 0.0,
        jnp.exp(-decay_rate[:, None, None] * jnp.maximum(offset, 0.0)[None]),
        0.0,
    )
    scores = (
        jnp.einsum("phd,shd->hps", query_rows, key_rows, preferred_element_type=jnp.float32)
        * decay_grid
    ).astype(jnp.bfloat16)
    outward = jnp.exp(-(block_len - 1.0 - place_f)[:, None] * decay_rate[None, :])
    inward = jnp.exp(-(place_f[:, None] + 1.0) * decay_rate[None, :])
    local_state = jnp.einsum(
        "shd,she->hde",
        key_rows.astype(jnp.float32) * outward[:, :, None],
        value_f,
        precision=highest,
    )
    block_decay = jnp.exp(-decay_rate * block_len)
    carried_decay, carried_state = prefix(
        (block_decay, local_state),
        "ctx",
        carry_forward,
        (jnp.ones_like(block_decay), jnp.zeros_like(local_state)),
        False,
    )
    prompt = lax.all_gather(prompt_state, ("slot", "ctx"), axis=1, tiled=True)[0].reshape(
        head_count, head_dim, head_dim
    )
    entry_state = carried_decay[:, None, None] * prompt + carried_state
    output = jnp.einsum("hps,shd->phd", scores, value_rows, preferred_element_type=jnp.float32)
    output = output + inward[:, :, None] * jnp.einsum(
        "phd,hde->phe", query_f, entry_state, precision=highest
    )
    cotangent = ((factor * keep_mask)[:, None, None] * output).astype(jnp.bfloat16)
    cotangent_f = cotangent.astype(jnp.float32)
    back_state = jnp.einsum(
        "phd,phe->hde", query_f * inward[:, :, None], cotangent_f, precision=highest
    )
    later_decay, later_state = prefix(
        (block_decay, back_state),
        "ctx",
        carry_backward,
        (jnp.ones_like(block_decay), jnp.zeros_like(back_state)),
        True,
    )
    weights = (
        jnp.einsum("phe,she->hps", cotangent, value_rows, preferred_element_type=jnp.float32)
        * decay_grid
    ).astype(jnp.bfloat16)
    key_grads = jnp.einsum("hps,phd->shd", weights, query_rows, preferred_element_type=jnp.float32)
    key_grads = key_grads + outward[:, :, None] * jnp.einsum(
        "hde,she->shd", later_state, value_f, precision=highest
    )
    key_grad = (
        (keep_mask[:, None, None] * key_grads)
        .astype(jnp.bfloat16)
        .reshape(1, 1, block_len, width_all)
    )
    prompt_term = jnp.where(
        ctx_index == 0, back_state + block_decay[:, None, None] * later_state, 0.0
    )
    prompt_grad = lax.psum_scatter(
        prompt_term.reshape(1, width_all, head_dim),
        ("slot", "ctx"),
        scatter_dimension=1,
        tiled=True,
    )
    return (key_grad, prompt_grad)


def solution(mesh):
    placed = (
        P("group", "slot", "ctx", None),
        P("group", "slot", "ctx", None),
        P("group", "slot", "ctx", None),
        P("group", "slot"),
        P("group", "slot"),
        P(),
        P("group", ("slot", "ctx"), None),
    )
    return jax.shard_map(
        shards,
        mesh=mesh,
        in_specs=placed,
        out_specs=(P("group", "slot", "ctx", None), P("group", ("slot", "ctx"), None)),
        check_vma=False,
    )
```

profile of v0, /device:TPU:6, one launch (start us, length us, event | category | flops | bytes accessed | tf_op | source)
XLA Modules:
  0.0 1123.3 jit_solution(4120618526955762635)
XLA Ops:
  7.2 0.0 copy-start.2
  7.2 0.0 all-gather.9.cloned.1.call-start
  8.0 0.0 copy-start.5
  8.0 1.6 copy.18
  9.6 0.0 copy-done.2
  9.6 0.7 copy.19
  10.3 0.0 copy-start.1
  10.3 0.0 copy-done.5
  10.3 0.1 multiply_exponential_fusion.1
  10.4 3.5 fusion.13
  13.9 0.0 copy-done.1
  13.9 0.0 copy-start.3
  13.9 0.0 all-gather.9.cloned.1.call-update
  14.0 0.0 all-gather.7.cloned.1.call-start
  14.0 0.7 all-gather.7.cloned.1.call-update
  14.7 0.0 all-gather.11.cloned.1.call-start
  14.8 258.9 %psum.15 = f32[]{:T(128)} all-reduce(f32[]{:T(128)S(6)} %convert_element_type.41), channel_id=1, replica_groups=mesh['group'=8,'slot'=16,'ctx'=4] {'group','slot'}, use_global_device_ids=true, to_apply=%region_1.0 | all-reduce | flops 1 | bytes 8 | tf_op jit(solution)/shard_map/psum | solution.py:42
  273.6 27.7 %psum.14 = f32[]{:T(128)} all-reduce(f32[]{:T(128)} %bitcast.5), channel_id=1, replica_groups=mesh['group'=8,'slot'=16,'ctx'=4] {'slot'}, use_global_device_ids=true, to_apply=%region_0.0 | all-reduce | flops 1 | bytes 8 | tf_op jit(solution)/shard_map/psum | solution.py:43
  302.0 1.3 dynamic-slice
  303.9 0.1 multiply_exponential_fusion.2
  304.0 7.5 all-reduce
  311.5 0.1 reshape.121
  311.6 0.0 copy-done.3
  311.6 1.3 copy.20
  314.2 0.0 all-gather.9.cloned.1.call-done
  314.3 0.2 broadcast_in_dim.15.clone
  314.5 6.1 while.26
  314.6 2.0 bitcast_add_fusion.4
  316.6 2.0 bitcast_add_fusion.4
  318.6 2.0 bitcast_add_fusion.4
  320.6 0.0 all-gather.7.cloned.1.call-done
  320.6 5.1 fusion.10
  325.7 0.0 copy-start
  325.7 3.7 fusion.5
  329.4 0.0 copy-done
  329.4 0.0 copy-start.4
  329.4 3.7 fusion.7
  333.0 0.0 copy-done.4
  333.0 0.0 all-gather.11.cloned.1.call-update
  333.1 0.0 reduce-scatter.2.cloned.1.call-start
  333.1 80.0 %all-gather.11.cloned.1.call-done = f32[128,128,128]{2,1,0:T(8,128)} async-done(((f32[32,128,128]{2,1,0:T(8,128)}), f32[128,128,128]{2,1,0:T(8,128)}) %all-gather.11.cloned.1.call-update) | async-done | bytes 8388624 | tf_op jit(solution)/shard_map/all_gather | solution.py:14
  413.1 0.2 broadcast_in_dim.15
  413.4 0.2 while.27
  413.6 3.2 add_select_fusion
  416.8 0.0 reduce-scatter.2.cloned.1.call-update
  416.8 2.5 fusion.30
  419.3 3.3 fusion.2
  422.6 1.3 copy.26
  423.9 692.8 %reduce-scatter.2.cloned.1.call-done = f32[1,64,128]{2,1,0:T(8,128)} async-done(((f32[1,4096,128]{2,1,0:T(8,128)}), f32[1,64,128]{2,1,0:T(8,128)}) %reduce-scatter.2.cloned.1.call-update) | async-done | bytes 32784 | tf_op jit(solution)/shard_map/reduce_scatter | solution.py:117
  (10 shorter events, 0.1 us)
Async XLA Ops:
  7.2 2.4 copy-start.2
  7.2 307.1 %all-gather.9.cloned.1.call-start = ((), (), s32[]{:S(2)}) async-start(), calls=%async_computation.3 | async-start | bytes 10485760 | tf_op jit(solution)/shard_map/all_gather | solution.py:14
  8.0 2.3 copy-start.5
  10.3 3.7 copy-start.1
  13.9 297.6 %copy-start.3 = (bf16[1,1,128,4096]{3,2,1,0:T(8,128)(2,1)S(1)}, bf16[1,1,128,4096]{3,2,1,0:T(8,128)(2,1)}, u32[]{:S(2)}) copy-start(bf16[1,1,128,4096]{3,2,1,0:T(8,128)(2,1)} %param.11) | copy-start | bytes 3145732
  14.0 306.7 %all-gather.7.cloned.1.call-start = ((), (), s32[]{:S(2)}) async-start(), calls=%async_computation.1 | async-start | bytes 2129920 | tf_op jit(solution)/shard_map/all_gather | solution.py:81
  14.7 398.4 %all-gather.11.cloned.1.call-start = ((), (), s32[]{:S(2)}) async-start(), calls=%async_computation.4 | async-start | bytes 10485760 | tf_op jit(solution)/shard_map/all_gather | solution.py:14
  325.7 3.7 copy-start
  329.4 3.7 copy-start.4
  333.1 783.7 %reduce-scatter.2.cloned.1.call-start = ((), (), s32[]{:S(2)}) async-start(), calls=%async_computation.2 | async-start | bytes 2129920 | tf_op jit(solution)/shard_map/reduce_scatter | solution.py:117
Sparse Core Ops, SparseCore 0:
  14.1 94.0 all-gather.8
  111.1 141.8 all-gather.6
  333.2 79.9 all-gather.10
  417.9 698.7 reduce-scatter.1
where the time goes:
time: 1120 us
  waiting for transfers between devices  774 us (69%)
  blocking collectives  294 us (26%)
  matrix products  21.7 us (2%)
  between operations  17.3 us (2%)
    reduce_scatter x1, waiting for transfers between devices, shards(): lax.psum_scatter(prompt_term.reshape(1, width_all, head_dim), ('slot', 'c...  693 us
    psum x1, blocking collectives, shards(): token_total = lax.psum(length.astype(jnp.float32), ('group', 'slot'))  259 us
    all_gather x2, waiting for transfers between devices, prefix(): gathered = jax.tree.map(lambda a: lax.all_gather(a, axis), part)  80.1 us
    psum x1, blocking collectives, shards(): reward_total = lax.psum(reward, 'slot')  27.7 us
  transfers between devices with their start and end apart: 4, of which 2 were waited for; matrix products, arithmetic and copies ran while one was open for 1% of the time, Pallas kernels for 0%

commit v1 on v0

v1 whole, which is shorter than its diff:
```python
import functools

import jax
import jax.numpy as jnp
from jax import lax
from jax.experimental import pallas as pl
from jax.experimental.pallas import tpu as pltpu
from jax.sharding import PartitionSpec as P

loss_scale = 16.0
f32 = jnp.float32
bf16 = jnp.bfloat16
chunk_heads = (4, 4)
lane = 128
vmem_bytes = 40 * 1024 * 1024


def dot(a, b, dims):
    return lax.dot_general(a, b, ((dims[0], dims[1]), ((), ())), preferred_element_type=f32)


def halves(x):
    hi = x.astype(bf16)
    return hi, (x - hi.astype(f32)).astype(bf16)


def pack_body(place, *refs):
    sources, sends = refs[:9], refs[9:]
    for turn in range(3):
        for which in range(3):
            sends[turn][which, 0] = sources[3 * turn + which][...].astype(f32)


def pack(place, arrays, block_len, start, count):
    def column(turn):
        return lambda m, place: (0, lax.rem(place[0] + turn, 4) + 4 * (start + m))

    in_specs = [
        pl.BlockSpec((block_len, lane), column(turn)) for turn in (1, 2, 3) for _ in arrays
    ]
    shape = (3, count, block_len, lane)
    return pl.pallas_call(
        pack_body,
        grid_spec=pltpu.PrefetchScalarGridSpec(
            num_scalar_prefetch=1,
            grid=(count,),
            in_specs=in_specs,
            out_specs=[
                pl.BlockSpec((3, 1, block_len, lane), lambda m, place: (0, m, 0, 0))
            ]
            * 3,
        ),
        out_shape=[jax.ShapeDtypeStruct(shape, f32)] * 3,
        compiler_params=pltpu.CompilerParams(vmem_limit_bytes=vmem_bytes),
        cost_estimate=pl.CostEstimate(
            flops=0, bytes_accessed=18 * count * block_len * lane * 3 // 3, transcendentals=0
        ),
    )(place, *(list(arrays) * 3))


def main_body(start, place, rates, factor_ref, *refs):
    local, moved, prompt_ref = refs[:3], refs[3:6], refs[6]
    refs = refs[7:] if start == 0 else refs[8:]
    outs, prompt_grad_ref = refs[:4], refs[4]
    rows_q, rows_k, rows_v, grads = refs[5:]
    me, length = place[0], place[1]
    factor = factor_ref[0]
    rate = rates[me + 4 * (start + pl.program_id(0))]
    row = lax.broadcasted_iota(jnp.int32, (lane, lane), 0)
    col = lax.broadcasted_iota(jnp.int32, (lane, lane), 1)
    row_f, offset = row.astype(f32), (row - col).astype(f32)
    decay = jnp.where(offset >= 0.0, jnp.exp(-rate * jnp.maximum(offset, 0.0)), 0.0)
    inward = jnp.exp(-(row_f + 1.0) * rate)
    outward = jnp.exp(-(lane - 1.0 - row_f) * rate)
    block_decay = jnp.exp(jnp.full((lane, lane), -float(lane), f32) * rate)

    def live(block):
        return (row + lane * block < length).astype(f32)

    for turn in range(4):
        block = lax.rem(me + 4 - turn, 4)
        if turn == 0:
            q, k, v = (r[...].astype(f32) for r in local)
        else:
            q, k, v = (moved[turn - 1][which, 0] for which in range(3))
        keep = live(block)
        rows_q[block] = q.astype(bf16)
        rows_k[block] = (k * keep).astype(bf16)
        rows_v[block] = (v * keep).astype(bf16)

    state = jnp.concatenate([prompt_ref[0, :64], prompt_ref[1, :64]], 0)
    cotangents = []
    for block in range(4):
        q, k, v = rows_q[block], rows_k[block], rows_v[block]
        scores = (dot(q, k, ((1,), (1,))) * decay).astype(bf16)
        state_hi, state_lo = halves(state)
        carried = dot(q, state_hi, ((1,), (0,))) + dot(q, state_lo, ((1,), (0,)))
        output = dot(scores, v, ((1,), (0,))) + inward * carried
        cotangents.append((factor * live(block) * output).astype(bf16))
        if block < 3:
            k_hi, k_lo = halves(k.astype(f32) * outward)
            state = block_decay * state + dot(k_hi, v, ((0,), (0,))) + dot(k_lo, v, ((0,), (0,)))
    state = None
    for block in (3, 2, 1, 0):
        q, v, cotangent = rows_q[block], rows_v[block], cotangents[block]
        weights = (dot(cotangent, v, ((1,), (1,))) * decay).astype(bf16)
        grad = dot(weights, q, ((0,), (0,)))
        q_hi, q_lo = halves(q.astype(f32) * inward)
        gained = dot(q_hi, cotangent, ((0,), (0,))) + dot(q_lo, cotangent, ((0,), (0,)))
        if state is None:
            state = gained
        else:
            state_hi, state_lo = halves(state)
            carried = dot(v, state_hi, ((1,), (1,))) + dot(v, state_lo, ((1,), (1,)))
            grad = grad + outward * carried
            state = block_decay * state + gained
        grads[block] = live(block) * grad
    prompt_grad_ref[0] = state
    for turn in range(4):
        outs[turn][0] = grads[lax.rem(me + turn, 4)]


def main(place, rates, factor, arrays, moved, prompt, so_far, block_len, start, count):
    assert block_len == lane
    head_block = lambda m, place: (0, place[0] + 4 * (start + m))
    in_specs = [
        pl.BlockSpec(memory_space=pltpu.SMEM),
        pl.BlockSpec(memory_space=pltpu.SMEM),
    ]
    in_specs += [pl.BlockSpec((block_len, lane), head_block)] * 3
    in_specs += [pl.BlockSpec((3, 1, block_len, lane), lambda m, place: (0, m, 0, 0))] * 3
    in_specs += [pl.BlockSpec((2,) + prompt.shape[1:], lambda m, place: (start + m, 0, 0))]
    args = [place, rates, factor, *arrays, *moved, prompt]
    aliases = {}
    if so_far is not None:
        in_specs.append(pl.BlockSpec(memory_space=pl.ANY))
        aliases = {len(args): 4}
        args.append(so_far)
    one = pl.BlockSpec((1, block_len, lane), lambda m, place: (m, 0, 0))
    return pl.pallas_call(
        functools.partial(main_body, start),
        grid_spec=pltpu.PrefetchScalarGridSpec(
            num_scalar_prefetch=1,
            grid=(count,),
            in_specs=in_specs,
            out_specs=[one] * 4
            + [pl.BlockSpec((1, lane, lane), lambda m, place: (start + m, 0, 0))],
            scratch_shapes=[pltpu.VMEM((4, lane, lane), bf16)] * 3
            + [pltpu.VMEM((4, lane, lane), f32)],
        ),
        out_shape=[jax.ShapeDtypeStruct((count, block_len, lane), f32)] * 4
        + [jax.ShapeDtypeStruct((8, lane, lane), f32)],
        input_output_aliases=aliases,
        compiler_params=pltpu.CompilerParams(vmem_limit_bytes=vmem_bytes),
        cost_estimate=pl.CostEstimate(
            flops=count * 4 * 15 * 2 * lane**3,
            bytes_accessed=count * lane * lane * 4 * 20,
            transcendentals=0,
        ),
    )(*args)


def place_body(start, place, *refs):
    parts, out = refs[:4], refs[-1]
    for turn in range(4):
        owner = lax.rem(place[0] + 4 - turn, 4)
        out[:, pl.ds(pl.multiple_of(owner * lane, lane), lane)] = parts[turn][0].astype(bf16)


def put(place, parts, so_far, block_len, start, count, width):
    in_specs = [pl.BlockSpec((1, block_len, lane), lambda m, place: (m, 0, 0))] * 4
    args = [place, *parts]
    aliases = {}
    if so_far is not None:
        in_specs.append(pl.BlockSpec(memory_space=pl.ANY))
        aliases = {len(args): 0}
        args.append(so_far)
    return pl.pallas_call(
        functools.partial(place_body, start),
        grid_spec=pltpu.PrefetchScalarGridSpec(
            num_scalar_prefetch=1,
            grid=(count,),
            in_specs=in_specs,
            out_specs=pl.BlockSpec((block_len, 4 * lane), lambda m, place: (0, start + m)),
        ),
        out_shape=jax.ShapeDtypeStruct((block_len, width), bf16),
        input_output_aliases=aliases,
        compiler_params=pltpu.CompilerParams(vmem_limit_bytes=vmem_bytes),
        cost_estimate=pl.CostEstimate(
            flops=0, bytes_accessed=count * block_len * lane * 24, transcendentals=0
        ),
    )(*args)


def piece_moves():
    moves = []
    for ctx in range(4):
        for slot in range(16):
            home = 4 * (2 * (slot // 2) + ctx // 2) + 2 * (ctx % 2) + slot % 2
            moves.append((home, 4 * slot + ctx))
    return moves


def shards(queries, keys, values, lengths, rewards, decay_rate, prompt_state):
    block_len, width = queries.shape[2], queries.shape[3]
    arrays = [a.reshape(block_len, width) for a in (queries, keys, values)]
    ctx_index = lax.axis_index("ctx").astype(jnp.int32)
    length, reward = lengths[0, 0], rewards[0, 0]
    place = jnp.stack([ctx_index, length])
    moves = piece_moves()

    piece = lax.ppermute(prompt_state[0], ("slot", "ctx"), moves)
    by_group = lax.all_gather(jnp.full((8, lane), length.astype(f32)), "group", tiled=True)
    slot_tokens = jnp.sum(by_group.reshape(-1, 8, lane)[:, 0], 0, keepdims=True)
    scalars = jnp.concatenate(
        [slot_tokens, jnp.full((1, lane), reward), jnp.zeros((6, lane), f32)], 0
    )
    prompt = lax.all_gather(jnp.concatenate([piece, scalars], 0), "slot")
    rows = piece.shape[0]
    token_total = jnp.sum(prompt[:, rows, 0])
    reward_total = jnp.sum(prompt[:, rows + 1, 0])
    slots, groups = lax.axis_size("slot"), lax.axis_size("group")
    advantage = reward - reward_total / slots
    factor = (loss_scale * advantage * (groups * slots) / token_total).reshape(1)

    starts = [sum(chunk_heads[:n]) for n in range(len(chunk_heads))]
    rings = [[(i, (i + turn) % 4) for i in range(4)] for turn in range(4)]

    def turned(parts):
        return [lax.ppermute(parts[turn - 1], "ctx", rings[turn]) for turn in (1, 2, 3)]

    moved = [
        turned(pack(place, arrays, block_len, start, count))
        for start, count in zip(starts, chunk_heads)
    ]
    prompt_grad, key_parts = None, []
    for start, count, parts in zip(starts, chunk_heads, moved):
        *out, prompt_grad = main(
            place, decay_rate, factor, arrays, parts, prompt, prompt_grad, block_len, start, count
        )
        key_parts.append([out[0], *turned(out[1:])])
    summed = lax.psum_scatter(prompt_grad.reshape(-1, rows, lane), "slot", tiled=True)
    summed = lax.ppermute(summed, ("slot", "ctx"), [(there, home) for home, there in moves])
    key_grad = None
    for start, count, parts in zip(starts, chunk_heads, key_parts):
        key_grad = put(place, parts, key_grad, block_len, start, count, width)
    return (key_grad.reshape(1, 1, block_len, width), summed)


def solution(mesh):
    placed = (
        P("group", "slot", "ctx", None),
        P("group", "slot", "ctx", None),
        P("group", "slot", "ctx", None),
        P("group", "slot"),
        P("group", "slot"),
        P(),
        P("group", ("slot", "ctx"), None),
    )
    return jax.shard_map(
        shards,
        mesh=mesh,
        in_specs=placed,
        out_specs=(P("group", "slot", "ctx", None), P("group", ("slot", "ctx"), None)),
        check_vma=False,
    )
```

time: 1120 us -> 212 us (0.19)
  waiting for transfers between devices: 774 us -> 48.4 us
  blocking collectives: 294 us -> 50.6 us
  starting transfers between devices: 0.16 us -> 50.6 us
  Pallas kernels: 0 us -> 27 us
  matrix products: 21.7 us -> 0 us
    reduce_scatter x1, waiting for transfers between devices: 693 us -> 47.2 us  [shards(): lax.psum_scatter(prompt_grad.reshape(-1, rows, lane), 'slot', tiled=True)]
    psum x2 -> x0, blocking collectives: 287 us -> none  [the longest x1 259 us: shards(): token_total = lax.psum(length.astype(jnp.float32), ('group', 'slot'))]
    all_gather x3 -> x0, waiting for transfers between devices: 80.1 us -> none  [the longest x2 80.1 us: prefix(): gathered = jax.tree.map(lambda a: lax.all_gather(a, axis), part)]
    ppermute x0 -> x14, starting transfers between devices: none -> 50.6 us  [the longest x12 44.7 us: turned(): lax.ppermute(parts[turn - 1], 'ctx', rings[turn])]
    all_gather x0 -> x1, blocking collectives: none -> 36.3 us  [shards(): prompt = lax.all_gather(jnp.concatenate([piece, scalars], 0), 'slot')]
    pallas_call x0 -> x6, Pallas kernels: none -> 27 us  [the longest x2 18 us: main(): pl.pallas_call(functools.partial(main_body, start), grid_spec=pltpu.Prefe...]
    dot_general x6 -> x0, matrix products: 21.7 us -> none  [the longest x1 5.07 us: shards(): jnp.einsum('phd,hde->phe', query_f, entry_state, precision=highest)]
  transfers between devices with their start and end apart: 4 -> 15, of which waited for: 2 -> 2; matrix products, arithmetic and copies ran while one was open for 1% -> 1% of each run, Pallas kernels for 0% -> 7%
where the time goes in v1:
time: 212 us; the launch traced here: 211 us
  starting transfers between devices  50.6 us (24%)
  blocking collectives  50.6 us (24%)
  waiting for transfers between devices  48.4 us (23%)
  Pallas kernels  27 us (13%)
  between operations  16.9 us (8%)
  local copies, waits for them, and re-layouts  16.7 us (8%)
    reduce_scatter x1, waiting for transfers between devices, shards(): lax.psum_scatter(prompt_grad.reshape(-1, rows, lane), 'slot', tiled=True)  47.2 us
    ppermute x12, starting transfers between devices, turned(): lax.ppermute(parts[turn - 1], 'ctx', rings[turn])  44.7 us
    all_gather x1, blocking collectives, shards(): prompt = lax.all_gather(jnp.concatenate([piece, scalars], 0), 'slot')  36.3 us
    pallas_call x2, Pallas kernels, main(): pl.pallas_call(functools.partial(main_body, start), grid_spec=pltpu.Prefe...  18 us
    unnamed x54, local copies, waits for them, and re-layouts  16.5 us
    unnamed x1, blocking collectives  14.2 us
    pallas_call x2, Pallas kernels, pack(): pl.pallas_call(pack_body, grid_spec=pltpu.PrefetchScalarGridSpec(num_scal...  5.04 us
  transfers between devices with their start and end apart: 15, of which 2 were waited for; matrix products, arithmetic and copies ran while one was open for 1% of the time, Pallas kernels for 7%

profile of v1, /device:TPU:6, one launch (start us, length us, event | category | flops | bytes accessed | tf_op | source)
XLA Modules:
  0.0 211.0 jit_solution(573715076824879431)
XLA Ops:
  7.2 0.0 reduce-scatter.2.cloned.1.call-start
  7.9 0.1 pad_add_fusion.place
  7.9 1.2 copy-done
  9.2 1.2 copy-done.2
  10.4 1.2 copy-done.4
  11.6 3.2 %shard_map.87 = (f32[3,4,128,128]{3,2,1,0:T(8,128)}, f32[3,4,128,128]{3,2,1,0:T(8,128)}, f32[3,4,128,128]{3,2,1,0:T(8,128)}) custom-call(s32[2]{0:T(128)S(1)} %pad_add_fusion.place, bf16[128,4096]{1,0:T(8,128)(2,1)S(1)} %bitcast.20, bf16[128,4096]{1,0:T(8,128)(2,1)S(1)} %bitcast.28, bf16[128,4096]{1,0:T(8,128)(2,1)S(1)} %bitcast.36, ...), custom_call_target="tpu_custom_call" | custom-call | bytes 1179648 | tf_op jit(solution)/shard_map/pallas_call | solution.py:42
  14.8 7.7 %collective-permute-start.4 = (f32[3,4,128,128]{3,2,1,0:T(8,128)}, f32[3,4,128,128]{3,2,1,0:T(8,128)}, u32[]{:S(2)}, u32[]{:S(2)}) collective-permute-start(f32[3,4,128,128]{3,2,1,0:T(8,128)} %get-tuple-element.21), channel_id=1, source_target_pairs={{0,1},{1,2},{2,3},{3,0},{4,5},{5,6},{6,7},{7,4},{8,9},{9,10},{10,1... | collective-permute-start | bytes 2359304 | tf_op jit(solution)/shard_map/ppermute | solution.py:230
  22.5 1.9 collective-permute-start.5
  24.5 2.8 %collective-permute-start.6 = (f32[3,4,128,128]{3,2,1,0:T(8,128)}, f32[3,4,128,128]{3,2,1,0:T(8,128)}, u32[]{:S(2)}, u32[]{:S(2)}) collective-permute-start(f32[3,4,128,128]{3,2,1,0:T(8,128)} %get-tuple-element.23), channel_id=1, source_target_pairs={{0,3},{1,0},{2,1},{3,2},{4,7},{5,4},{6,5},{7,6},{8,11},{9,8},{10,9... | collective-permute-start | bytes 2359304 | tf_op jit(solution)/shard_map/ppermute | solution.py:230
  27.3 2.7 %collective-permute-start = (f32[64,128]{1,0:T(8,128)S(1)}, f32[64,128]{1,0:T(8,128)S(1)}, u32[]{:S(2)}, u32[]{:S(2)}) collective-permute-start(f32[64,128]{1,0:T(8,128)S(1)} %bitcast.50), channel_id=1, source_target_pairs={{0,0},{1,4},{8,8},{9,12},{16,16},{17,20},{24,24},{25,28},{32,32},{... | collective-permute-start | bytes 98312 | tf_op jit(solution)/shard_map/ppermute | solution.py:212
  30.0 0.0 copy-start.1
  30.0 0.0 copy-start.3
  30.0 0.0 copy-start.5
  30.0 1.9 shard_map.86
  31.9 0.9 copy-done.13
  32.8 0.9 copy-done.14
  33.7 0.9 copy-done.15
  34.6 1.3 dynamic-slice
  35.8 0.7 bitcast_dynamic-update-slice_fusion
  36.5 2.2 %collective-permute-start.1 = (f32[3,4,128,128]{3,2,1,0:T(8,128)}, f32[3,4,128,128]{3,2,1,0:T(8,128)}, u32[]{:S(2)}, u32[]{:S(2)}) collective-permute-start(f32[3,4,128,128]{3,2,1,0:T(8,128)} %copy-done.15), channel_id=1, source_target_pairs={{0,1},{1,2},{2,3},{3,0},{4,5},{5,6},{6,7},{7,4},{8,9},{9,10},{10,1... | collective-permute-start | bytes 2359304 | tf_op jit(solution)/shard_map/ppermute | solution.py:230
  38.8 14.2 %all-reduce = f32[8]{0:T(128)S(1)} all-reduce(f32[8]{0:T(128)S(1)} %bitcast_dynamic-update-slice_fusion), channel_id=3, replica_groups=mesh['group'=8,'slot'=16,'ctx'=4] {'group'}, use_global_device_ids=true, to_apply=%add | all-reduce | flops 8 | bytes 64
  53.7 0.1 pad.2.clone
  53.7 0.1 pad.3.clone
  53.8 0.0 collective-permute-done
  53.8 7.8 %collective-permute-start.2 = (f32[3,4,128,128]{3,2,1,0:T(8,128)}, f32[3,4,128,128]{3,2,1,0:T(8,128)}, u32[]{:S(2)}, u32[]{:S(2)}) collective-permute-start(f32[3,4,128,128]{3,2,1,0:T(8,128)} %copy-done.14), channel_id=1, source_target_pairs={{0,2},{1,3},{2,0},{3,1},{4,6},{5,7},{6,4},{7,5},{8,10},{9,11},{10,... | collective-permute-start | bytes 2359304 | tf_op jit(solution)/shard_map/ppermute | solution.py:230
  61.7 0.0 collective-permute-done.4.refs_3_
  61.7 1.9 collective-permute-start.3
  63.6 0.1 broadcast_reduce_fusion
  63.7 0.1 maximum_maximum_fusion
  63.8 36.3 %all-gather.1 = f32[1152,128]{1,0:T(8,128)S(1)} all-gather(f32[72,128]{1,0:T(8,128)S(1)} %maximum_maximum_fusion), channel_id=4, replica_groups=mesh['group'=8,'slot'=16,'ctx'=4] {'slot'}, dimensions={0}, use_global_device_ids=true | all-gather | bytes 626688 | tf_op jit(solution)/shard_map/all_gather | solution.py:218
  100.1 0.6 slice_reduce_fusion
  100.7 0.9 copy-done.6
  102.8 0.0 copy-start.12
  102.8 0.0 collective-permute-done.5.refs_4_
  102.8 0.0 collective-permute-done.6.refs_5_
  102.8 0.6 copy-done.12
  103.4 1.1 copy-done.7
  104.5 9.0 %shard_map.88 = (f32[4,128,128]{2,1,0:T(8,128)S(1)}, f32[4,128,128]{2,1,0:T(8,128)S(1)}, f32[4,128,128]{2,1,0:T(8,128)S(1)}, f32[4,128,128]{2,1,0:T(8,128)S(1)}, f32[8,128,128]{2,1,0:T(8,128)S(1)}) custom-call(s32[2]{0:T(128)S(1)} %pad_add_fusion.place, f32[32]{0:T(128)S(1)} %copy-done.12, f32[1]{0:T(128)} %bitcast.8.factor_ref, ...), custom_call_target="tpu_custom_call" | custom-call | flops 1006632960 | bytes 5242880 | tf_op jit(solution)/shard_map/pallas_call | solution.py:140
  113.5 0.7 copy-done.22
  114.2 0.7 copy-done.23
  114.9 0.0 collective-permute-done.1.refs_3_
  114.9 0.0 collective-permute-done.2.refs_4_
  114.9 9.0 %shard_map.89 = (f32[4,128,128]{2,1,0:T(8,128)S(1)}, f32[4,128,128]{2,1,0:T(8,128)S(1)}, f32[4,128,128]{2,1,0:T(8,128)S(1)}, f32[4,128,128]{2,1,0:T(8,128)S(1)}, f32[8,128,128]{2,1,0:T(8,128)S(1)}) custom-call(s32[2]{0:T(128)S(1)} %pad_add_fusion.place, f32[32]{0:T(128)S(1)} %copy-done.12, f32[1]{0:T(128)} %bitcast.8.factor_ref, ...), custom_call_target="tpu_custom_call", output_to_operand_aliasing={{4}: (10, {})} | custom-call | flops 1006632960 | bytes 5242880 | tf_op jit(solution)/shard_map/pallas_call | solution.py:140
  124.0 0.0 copy-start.9
  124.0 0.8 copy-done.9
  124.8 0.7 copy-done.10
  125.5 0.7 copy-done.18
  126.2 0.7 copy-done.20
  126.9 0.7 copy-done.21
  127.6 0.0 reduce-scatter.2.cloned.1.call-update
  127.6 5.2 %collective-permute-start.10 = (f32[4,128,128]{2,1,0:T(8,128)}, f32[4,128,128]{2,1,0:T(8,128)S(1)}, u32[]{:S(2)}, u32[]{:S(2)}) collective-permute-start(f32[4,128,128]{2,1,0:T(8,128)} %copy-done.23), channel_id=1, source_target_pairs={{0,1},{1,2},{2,3},{3,0},{4,5},{5,6},{6,7},{7,4},{8,9},{9,10},{10,1... | collective-permute-start | bytes 786440 | tf_op jit(solution)/shard_map/ppermute | solution.py:230
  132.8 1.9 collective-permute-start.11
  134.7 2.8 %collective-permute-start.12 = (f32[4,128,128]{2,1,0:T(8,128)S(1)}, f32[4,128,128]{2,1,0:T(8,128)S(1)}, u32[]{:S(2)}, u32[]{:S(2)}) collective-permute-start(f32[4,128,128]{2,1,0:T(8,128)S(1)} %copy-done.17), channel_id=1, source_target_pairs={{0,3},{1,0},{2,1},{3,2},{4,7},{5,4},{6,5},{7,6},{8,11},{9,8},{10,9... | collective-permute-start | bytes 786440 | tf_op jit(solution)/shard_map/ppermute | solution.py:230
  137.5 4.3 %collective-permute-start.7 = (f32[4,128,128]{2,1,0:T(8,128)}, f32[4,128,128]{2,1,0:T(8,128)S(1)}, u32[]{:S(2)}, u32[]{:S(2)}) collective-permute-start(f32[4,128,128]{2,1,0:T(8,128)} %copy-done.21), channel_id=1, source_target_pairs={{0,1},{1,2},{2,3},{3,0},{4,5},{5,6},{6,7},{7,4},{8,9},{9,10},{10,1... | collective-permute-start | bytes 786440 | tf_op jit(solution)/shard_map/ppermute | solution.py:230
  141.8 4.2 %collective-permute-start.8 = (f32[4,128,128]{2,1,0:T(8,128)}, f32[4,128,128]{2,1,0:T(8,128)S(1)}, u32[]{:S(2)}, u32[]{:S(2)}) collective-permute-start(f32[4,128,128]{2,1,0:T(8,128)} %copy-done.20), channel_id=1, source_target_pairs={{0,2},{1,3},{2,0},{3,1},{4,6},{5,7},{6,4},{7,5},{8,10},{9,11},{10,... | collective-permute-start | bytes 786440 | tf_op jit(solution)/shard_map/ppermute | solution.py:230
  146.0 0.0 collective-permute-done.10.refs_1_
  146.1 1.9 collective-permute-start.9
  148.0 47.2 %reduce-scatter.2.cloned.1.call-done = f32[1,64,128]{2,1,0:T(8,128)} async-done(((f32[16,64,128]{2,1,0:T(8,128)}), f32[1,64,128]{2,1,0:T(8,128)}) %reduce-scatter.2.cloned.1.call-update) | async-done | bytes 32784 | tf_op jit(solution)/shard_map/reduce_scatter | solution.py:242
  195.1 3.2 %collective-permute-start.13 = (f32[1,64,128]{2,1,0:T(8,128)}, f32[1,64,128]{2,1,0:T(8,128)S(1)}, u32[]{:S(2)}, u32[]{:S(2)}) collective-permute-start(f32[1,64,128]{2,1,0:T(8,128)} %reduce-scatter.2.cloned.1.call-done), channel_id=1, source_target_pairs={{0,0},{4,1},{8,8},{12,9},{16,16},{20,17},{24,24},{28,25},{32,32},{... | collective-permute-start | bytes 98312 | tf_op jit(solution)/shard_map/ppermute | solution.py:243
  198.3 0.0 collective-permute-done.12.refs_3_
  198.3 2.0 shard_map.90.refs_4_
  200.3 2.0 shard_map.91
  202.3 1.2 collective-permute-done.13
  203.6 0.6 copy.17
  (36 shorter events, 0.1 us)
Async XLA Ops:
  7.2 188.0 %reduce-scatter.2.cloned.1.call-start = ((), (), s32[]{:S(2)}) async-start(), calls=%async_computation.1 | async-start | bytes 557056 | tf_op jit(solution)/shard_map/reduce_scatter | solution.py:242
  7.9 1.2 copy-start
  9.2 1.2 copy-start.2
  10.4 1.2 copy-start.4
  11.6 15.6 %copy-start.24 = (f32[1,64,128]{2,1,0:T(8,128)S(1)}, f32[1,64,128]{2,1,0:T(8,128)}, u32[]{:S(2)}) copy-start(f32[1,64,128]{2,1,0:T(8,128)} %param.13) | copy-start | bytes 98308
  14.8 46.9 %collective-permute-start.4 = (f32[3,4,128,128]{3,2,1,0:T(8,128)}, f32[3,4,128,128]{3,2,1,0:T(8,128)}, u32[]{:S(2)}, u32[]{:S(2)}) collective-permute-start(f32[3,4,128,128]{3,2,1,0:T(8,128)} %get-tuple-element.21), channel_id=1, source_target_pairs={{0,1},{1,2},{2,3},{3,0},{4,5},{5,6},{6,7},{7,4},{8,9},{9,10},{10,1... | collective-permute-start | bytes 2359304 | tf_op jit(solution)/shard_map/ppermute | solution.py:230
  22.5 80.2 %collective-permute-start.5 = (f32[3,4,128,128]{3,2,1,0:T(8,128)}, f32[3,4,128,128]{3,2,1,0:T(8,128)}, u32[]{:S(2)}, u32[]{:S(2)}) collective-permute-start(f32[3,4,128,128]{3,2,1,0:T(8,128)} %get-tuple-element.22), channel_id=1, source_target_pairs={{0,2},{1,3},{2,0},{3,1},{4,6},{5,7},{6,4},{7,5},{8,10},{9,11},{10,... | collective-permute-start | bytes 2359304 | tf_op jit(solution)/shard_map/ppermute | solution.py:230
  24.5 78.3 %collective-permute-start.6 = (f32[3,4,128,128]{3,2,1,0:T(8,128)}, f32[3,4,128,128]{3,2,1,0:T(8,128)}, u32[]{:S(2)}, u32[]{:S(2)}) collective-permute-start(f32[3,4,128,128]{3,2,1,0:T(8,128)} %get-tuple-element.23), channel_id=1, source_target_pairs={{0,3},{1,0},{2,1},{3,2},{4,7},{5,4},{6,5},{7,6},{8,11},{9,8},{10,9... | collective-permute-start | bytes 2359304 | tf_op jit(solution)/shard_map/ppermute | solution.py:230
  27.3 26.6 %collective-permute-start = (f32[64,128]{1,0:T(8,128)S(1)}, f32[64,128]{1,0:T(8,128)S(1)}, u32[]{:S(2)}, u32[]{:S(2)}) collective-permute-start(f32[64,128]{1,0:T(8,128)S(1)} %bitcast.50), channel_id=1, source_target_pairs={{0,0},{1,4},{8,8},{9,12},{16,16},{17,20},{24,24},{25,28},{32,32},{... | collective-permute-start | bytes 98312 | tf_op jit(solution)/shard_map/ppermute | solution.py:212
  30.0 72.8 %copy-start.1 = (bf16[1,1,128,4096]{3,2,1,0:T(8,128)(2,1)S(1)}, bf16[1,1,128,4096]{3,2,1,0:T(8,128)(2,1)}, u32[]{:S(2)}) copy-start(bf16[1,1,128,4096]{3,2,1,0:T(8,128)(2,1)} %param.7) | copy-start | bytes 3145732
  30.0 72.8 %copy-start.3 = (bf16[1,1,128,4096]{3,2,1,0:T(8,128)(2,1)S(1)}, bf16[1,1,128,4096]{3,2,1,0:T(8,128)(2,1)}, u32[]{:S(2)}) copy-start(bf16[1,1,128,4096]{3,2,1,0:T(8,128)(2,1)} %param.8) | copy-start | bytes 3145732
  30.0 72.8 %copy-start.5 = (bf16[1,1,128,4096]{3,2,1,0:T(8,128)(2,1)S(1)}, bf16[1,1,128,4096]{3,2,1,0:T(8,128)(2,1)}, u32[]{:S(2)}) copy-start(bf16[1,1,128,4096]{3,2,1,0:T(8,128)(2,1)} %param.9) | copy-start | bytes 3145732
  31.9 0.9 copy-start.13
  32.8 0.9 copy-start.14
  33.7 0.9 copy-start.15
  36.5 78.4 %collective-permute-start.1 = (f32[3,4,128,128]{3,2,1,0:T(8,128)}, f32[3,4,128,128]{3,2,1,0:T(8,128)}, u32[]{:S(2)}, u32[]{:S(2)}) collective-permute-start(f32[3,4,128,128]{3,2,1,0:T(8,128)} %copy-done.15), channel_id=1, source_target_pairs={{0,1},{1,2},{2,3},{3,0},{4,5},{5,6},{6,7},{7,4},{8,9},{9,10},{10,1... | collective-permute-start | bytes 2359304 | tf_op jit(solution)/shard_map/ppermute | solution.py:230
  53.8 61.1 %collective-permute-start.2 = (f32[3,4,128,128]{3,2,1,0:T(8,128)}, f32[3,4,128,128]{3,2,1,0:T(8,128)}, u32[]{:S(2)}, u32[]{:S(2)}) collective-permute-start(f32[3,4,128,128]{3,2,1,0:T(8,128)} %copy-done.14), channel_id=1, source_target_pairs={{0,2},{1,3},{2,0},{3,1},{4,6},{5,7},{6,4},{7,5},{8,10},{9,11},{10,... | collective-permute-start | bytes 2359304 | tf_op jit(solution)/shard_map/ppermute | solution.py:230
  61.7 53.2 %collective-permute-start.3 = (f32[3,4,128,128]{3,2,1,0:T(8,128)}, f32[3,4,128,128]{3,2,1,0:T(8,128)}, u32[]{:S(2)}, u32[]{:S(2)}) collective-permute-start(f32[3,4,128,128]{3,2,1,0:T(8,128)} %copy-done.13), channel_id=1, source_target_pairs={{0,3},{1,0},{2,1},{3,2},{4,7},{5,4},{6,5},{7,6},{8,11},{9,8},{10,9... | collective-permute-start | bytes 2359304 | tf_op jit(solution)/shard_map/ppermute | solution.py:230
  100.7 0.9 copy-start.6
  102.8 0.7 copy-start.12
  103.4 1.1 copy-start.7
  104.5 10.4 %copy-start.8 = (f32[1152,128]{1,0:T(8,128)S(1)}, f32[1152,128]{1,0:T(8,128)}, u32[]{:S(2)}) copy-start(f32[1152,128]{1,0:T(8,128)} %copy-done.6) | copy-start | bytes 1769476
  113.5 0.7 copy-start.22
  114.2 0.7 copy-start.23
  114.9 9.0 %copy-start.16 = (f32[4,128,128]{2,1,0:T(8,128)}, f32[4,128,128]{2,1,0:T(8,128)S(1)}, u32[]{:S(2)}) copy-start(f32[4,128,128]{2,1,0:T(8,128)S(1)} %get-tuple-element.32) | copy-start | bytes 786436
  124.0 0.8 copy-start.9
  124.8 0.7 copy-start.10
  125.5 0.7 copy-start.18
  126.2 0.7 copy-start.20
  126.9 0.7 copy-start.21
  127.6 7.1 %copy-start.17 = (f32[4,128,128]{2,1,0:T(8,128)S(1)}, f32[4,128,128]{2,1,0:T(8,128)}, u32[]{:S(2)}) copy-start(f32[4,128,128]{2,1,0:T(8,128)} %copy-done.16) | copy-start | bytes 786436
  127.6 18.5 %copy-start.19 = (f32[4,128,128]{2,1,0:T(8,128)S(1)}, f32[4,128,128]{2,1,0:T(8,128)}, u32[]{:S(2)}) copy-start(f32[4,128,128]{2,1,0:T(8,128)} %copy-done.18) | copy-start | bytes 786436
  127.6 18.4 %collective-permute-start.10 = (f32[4,128,128]{2,1,0:T(8,128)}, f32[4,128,128]{2,1,0:T(8,128)S(1)}, u32[]{:S(2)}, u32[]{:S(2)}) collective-permute-start(f32[4,128,128]{2,1,0:T(8,128)} %copy-done.23), channel_id=1, source_target_pairs={{0,1},{1,2},{2,3},{3,0},{4,5},{5,6},{6,7},{7,4},{8,9},{9,10},{10,1... | collective-permute-start | bytes 786440 | tf_op jit(solution)/shard_map/ppermute | solution.py:230
  132.8 15.2 %collective-permute-start.11 = (f32[4,128,128]{2,1,0:T(8,128)}, f32[4,128,128]{2,1,0:T(8,128)S(1)}, u32[]{:S(2)}, u32[]{:S(2)}) collective-permute-start(f32[4,128,128]{2,1,0:T(8,128)} %copy-done.22), channel_id=1, source_target_pairs={{0,2},{1,3},{2,0},{3,1},{4,6},{5,7},{6,4},{7,5},{8,10},{9,11},{10,... | collective-permute-start | bytes 786440 | tf_op jit(solution)/shard_map/ppermute | solution.py:230
  134.7 63.6 %collective-permute-start.12 = (f32[4,128,128]{2,1,0:T(8,128)S(1)}, f32[4,128,128]{2,1,0:T(8,128)S(1)}, u32[]{:S(2)}, u32[]{:S(2)}) collective-permute-start(f32[4,128,128]{2,1,0:T(8,128)S(1)} %copy-done.17), channel_id=1, source_target_pairs={{0,3},{1,0},{2,1},{3,2},{4,7},{5,4},{6,5},{7,6},{8,11},{9,8},{10,9... | collective-permute-start | bytes 786440 | tf_op jit(solution)/shard_map/ppermute | solution.py:230
  137.5 62.8 %collective-permute-start.7 = (f32[4,128,128]{2,1,0:T(8,128)}, f32[4,128,128]{2,1,0:T(8,128)S(1)}, u32[]{:S(2)}, u32[]{:S(2)}) collective-permute-start(f32[4,128,128]{2,1,0:T(8,128)} %copy-done.21), channel_id=1, source_target_pairs={{0,1},{1,2},{2,3},{3,0},{4,5},{5,6},{6,7},{7,4},{8,9},{9,10},{10,1... | collective-permute-start | bytes 786440 | tf_op jit(solution)/shard_map/ppermute | solution.py:230
  141.8 58.5 %collective-permute-start.8 = (f32[4,128,128]{2,1,0:T(8,128)}, f32[4,128,128]{2,1,0:T(8,128)S(1)}, u32[]{:S(2)}, u32[]{:S(2)}) collective-permute-start(f32[4,128,128]{2,1,0:T(8,128)} %copy-done.20), channel_id=1, source_target_pairs={{0,2},{1,3},{2,0},{3,1},{4,6},{5,7},{6,4},{7,5},{8,10},{9,11},{10,... | collective-permute-start | bytes 786440 | tf_op jit(solution)/shard_map/ppermute | solution.py:230
  146.1 54.3 %collective-permute-start.9 = (f32[4,128,128]{2,1,0:T(8,128)S(1)}, f32[4,128,128]{2,1,0:T(8,128)S(1)}, u32[]{:S(2)}, u32[]{:S(2)}) collective-permute-start(f32[4,128,128]{2,1,0:T(8,128)S(1)} %copy-done.19), channel_id=1, source_target_pairs={{0,3},{1,0},{2,1},{3,2},{4,7},{5,4},{6,5},{7,6},{8,11},{9,8},{10,9... | collective-permute-start | bytes 786440 | tf_op jit(solution)/shard_map/ppermute | solution.py:230
  195.1 8.4 %collective-permute-start.13 = (f32[1,64,128]{2,1,0:T(8,128)}, f32[1,64,128]{2,1,0:T(8,128)S(1)}, u32[]{:S(2)}, u32[]{:S(2)}) collective-permute-start(f32[1,64,128]{2,1,0:T(8,128)} %reduce-scatter.2.cloned.1.call-done), channel_id=1, source_target_pairs={{0,0},{4,1},{8,8},{12,9},{16,16},{20,17},{24,24},{28,25},{32,32},{... | collective-permute-start | bytes 98312 | tf_op jit(solution)/shard_map/ppermute | solution.py:243
  198.3 2.0 copy-start.11
Sparse Core Ops, SparseCore 0:
  127.7 67.3 reduce-scatter.1

commit v2 on v1

v2 whole, which is shorter than its diff:
```python
import functools

import jax
import jax.numpy as jnp
from jax import lax
from jax.experimental import pallas as pl
from jax.experimental.pallas import tpu as pltpu
from jax.sharding import PartitionSpec as P

loss_scale = 16.0
f32 = jnp.float32
bf16 = jnp.bfloat16
chunk_heads = (8,)
lane = 128


def dot(a, b, dims):
    return lax.dot_general(a, b, ((dims[0], dims[1]), ((), ())), preferred_element_type=f32)


def halves(x):
    hi = x.astype(bf16)
    return hi, (x - hi.astype(f32)).astype(bf16)


def pack_body(heads, place, *refs):
    sources, sends = refs[:3], refs[3:]
    for turn in range(3):
        owner = lax.rem(place[0] + turn + 1, 4)
        for which in range(3):
            for step in range(heads):
                column = pl.multiple_of((owner + 4 * step) * lane, lane)
                sends[turn][which, step] = sources[which][:, pl.ds(column, lane)].astype(f32)


def pack(place, arrays, block_len, start, count, heads=4):
    first = start // heads
    return pl.pallas_call(
        functools.partial(pack_body, heads),
        grid_spec=pltpu.PrefetchScalarGridSpec(
            num_scalar_prefetch=1,
            grid=(count // heads,),
            in_specs=[
                pl.BlockSpec((block_len, 4 * heads * lane), lambda m, place: (0, first + m))
            ]
            * 3,
            out_specs=[
                pl.BlockSpec((3, heads, block_len, lane), lambda m, place: (0, m, 0, 0))
            ]
            * 3,
        ),
        out_shape=[jax.ShapeDtypeStruct((3, count, block_len, lane), f32)] * 3,
        cost_estimate=pl.CostEstimate(
            flops=0, bytes_accessed=60 * count * block_len * lane, transcendentals=0
        ),
    )(place, *arrays)


def head_grads(rates, factor, length, rows, states):
    row = lax.broadcasted_iota(jnp.int32, (lane, lane), 0)
    col = lax.broadcasted_iota(jnp.int32, (lane, lane), 1)
    row_f, offset = row.astype(f32), (row - col).astype(f32)
    keep = [(row + lane * block < length).astype(f32) for block in range(4)]
    heads = range(len(rates))
    decay = [
        jnp.where(offset >= 0.0, jnp.exp(-rate * jnp.maximum(offset, 0.0)), 0.0) for rate in rates
    ]
    inward = [jnp.exp(-(row_f + 1.0) * rate) for rate in rates]
    outward = [jnp.exp(-(lane - 1.0 - row_f) * rate) for rate in rates]
    block_decay = [jnp.exp(jnp.full((lane, lane), -float(lane), f32) * rate) for rate in rates]
    q, k, v = ({(h, b): rows[h][n][b] for h in heads for b in range(4)} for n in range(3))
    forward = [(h, b) for b in range(4) for h in heads]
    backward = forward[::-1]

    def two(a, b, dims):
        a, b = jnp.concatenate(a, dims[0][0]), jnp.concatenate(b, dims[1][0])
        return dot(a, b, dims)

    scores, gained, states_at = {}, {}, {}
    for at in forward:
        scores[at] = (dot(q[at], k[at], ((1,), (1,))) * decay[at[0]]).astype(bf16)
    for at in forward:
        if at[1] < 3:
            scaled = halves(k[at].astype(f32) * outward[at[0]])
            gained[at] = two(scaled, (v[at], v[at]), ((0,), (0,)))
    for h in heads:
        state = states[h]
        for b in range(4):
            states_at[h, b] = halves(state)
            if b < 3:
                state = block_decay[h] * state + gained[h, b]
    cotangents = {}
    for at in forward:
        carried = two((q[at], q[at]), states_at[at], ((1,), (0,)))
        output = dot(scores[at], v[at], ((1,), (0,))) + inward[at[0]] * carried
        cotangents[at] = (factor * keep[at[1]] * output).astype(bf16)
    for at in backward:
        scaled = halves(q[at].astype(f32) * inward[at[0]])
        gained[at] = two(scaled, (cotangents[at], cotangents[at]), ((0,), (0,)))
    ends = []
    for h in heads:
        state = gained[h, 3]
        for b in (2, 1, 0):
            states_at[h, b] = halves(state)
            state = block_decay[h] * state + gained[h, b]
        ends.append(state)
    weights, grads = {}, {}
    for at in backward:
        weights[at] = (dot(cotangents[at], v[at], ((1,), (1,))) * decay[at[0]]).astype(bf16)
    for at in backward:
        grad = dot(weights[at], q[at], ((0,), (0,)))
        if at[1] < 3:
            carried = two((v[at], v[at]), states_at[at], ((1,), (1,)))
            grad = grad + outward[at[0]] * carried
        grads[at] = keep[at[1]] * grad
    return grads, ends


def main_body(start, heads, aliased, place, rates, factor_ref, *refs):
    local, moved, prompt_ref = refs[:3], refs[3:6], refs[6]
    refs = refs[7 + aliased :]
    outs, prompt_grad_ref = refs[:4], refs[4]
    rows_q, rows_k, rows_v, grads_ref = refs[5:]
    me, length = place[0], place[1]
    row = lax.broadcasted_iota(jnp.int32, (lane, lane), 0)
    for step in range(heads):
        for turn in range(4):
            block = lax.rem(me + 4 - turn, 4)
            if turn == 0:
                column = pl.ds(pl.multiple_of((me + 4 * step) * lane, lane), lane)
                q, k, v = (r[:, column].astype(f32) for r in local)
            else:
                q, k, v = (moved[turn - 1][which, step] for which in range(3))
            keep = (row + lane * block < length).astype(f32)
            rows_q[step, block] = q.astype(bf16)
            rows_k[step, block] = (k * keep).astype(bf16)
            rows_v[step, block] = (v * keep).astype(bf16)
    half, steps = lane // 2, range(heads)
    head = me + 4 * (start + pl.program_id(0) * heads)
    prompts = [
        jnp.concatenate([prompt_ref[2 * step, :half], prompt_ref[2 * step + 1, :half]], 0)
        for step in steps
    ]
    rows = [
        [[r[step, block] for block in range(4)] for r in (rows_q, rows_k, rows_v)]
        for step in steps
    ]
    grads, ends = head_grads(
        [rates[head + 4 * step] for step in steps], factor_ref[0], length, rows, prompts
    )
    for step in steps:
        for block in range(4):
            grads_ref[step, block] = grads[step, block]
        prompt_grad_ref[step] = ends[step]
    for step in range(heads):
        for turn in range(4):
            outs[turn][step] = grads_ref[step, lax.rem(me + turn, 4)]


def main(place, rates, factor, arrays, moved, prompt, so_far, block_len, start, count, heads=2):
    assert block_len == lane
    first, total = start // heads, prompt.shape[0] // 2
    in_specs = [pl.BlockSpec(memory_space=pltpu.SMEM)] * 2
    in_specs += [
        pl.BlockSpec((block_len, 4 * heads * lane), lambda m, place: (0, first + m))
    ] * 3
    in_specs += [pl.BlockSpec((3, heads, block_len, lane), lambda m, place: (0, m, 0, 0))] * 3
    in_specs += [
        pl.BlockSpec((2 * heads,) + prompt.shape[1:], lambda m, place: (first + m, 0, 0))
    ]
    args = [place, rates, factor, *arrays, *moved, prompt]
    aliases = {len(args) + n: n for n in range(len(so_far))}
    in_specs += [pl.BlockSpec(memory_space=pl.ANY)] * len(so_far)
    one = pl.BlockSpec((heads, block_len, lane), lambda m, place: (first + m, 0, 0))
    return pl.pallas_call(
        functools.partial(main_body, start, heads, len(so_far)),
        grid_spec=pltpu.PrefetchScalarGridSpec(
            num_scalar_prefetch=1,
            grid=(count // heads,),
            in_specs=in_specs,
            out_specs=[one] * 5,
            scratch_shapes=[pltpu.VMEM((heads, 4, lane, lane), bf16)] * 3
            + [pltpu.VMEM((heads, 4, lane, lane), f32)],
        ),
        out_shape=[jax.ShapeDtypeStruct((total, block_len, lane), f32)] * 5,
        input_output_aliases=aliases,
        cost_estimate=pl.CostEstimate(
            flops=count * 4 * 15 * 2 * lane**3,
            bytes_accessed=count * lane * lane * 4 * 20,
            transcendentals=0,
        ),
    )(*args, *so_far)


def put_body(heads, place, *refs):
    parts, out = refs[:4], refs[4]
    for turn in range(4):
        owner = lax.rem(place[0] + 4 - turn, 4)
        for step in range(heads):
            column = pl.multiple_of((owner + 4 * step) * lane, lane)
            out[:, pl.ds(column, lane)] = parts[turn][step].astype(bf16)


def put(place, parts, block_len, width, heads=4):
    return pl.pallas_call(
        functools.partial(put_body, heads),
        grid_spec=pltpu.PrefetchScalarGridSpec(
            num_scalar_prefetch=1,
            grid=(parts[0].shape[0] // heads,),
            in_specs=[pl.BlockSpec((heads, block_len, lane), lambda m, place: (m, 0, 0))] * 4,
            out_specs=pl.BlockSpec((block_len, 4 * heads * lane), lambda m, place: (0, m)),
        ),
        out_shape=jax.ShapeDtypeStruct((block_len, width), bf16),
        cost_estimate=pl.CostEstimate(
            flops=0, bytes_accessed=parts[0].size * 24, transcendentals=0
        ),
    )(place, *parts)


def piece_moves():
    moves = []
    for ctx in range(4):
        for slot in range(16):
            home = 4 * (2 * (slot // 2) + ctx // 2) + 2 * (ctx % 2) + slot % 2
            moves.append((home, 4 * slot + ctx))
    return moves


def shards(queries, keys, values, lengths, rewards, decay_rate, prompt_state):
    block_len, width = queries.shape[2], queries.shape[3]
    arrays = [a.reshape(block_len, width) for a in (queries, keys, values)]
    ctx_index = lax.axis_index("ctx").astype(jnp.int32)
    length, reward = lengths[0, 0], rewards[0, 0]
    place = jnp.stack([ctx_index, length])
    moves = piece_moves()

    piece = lax.ppermute(prompt_state[0], ("slot", "ctx"), moves)
    rings = [[(i, (i + turn) % 4) for i in range(4)] for turn in range(4)]
    starts = [sum(chunk_heads[:n]) for n in range(len(chunk_heads))]

    def turned(parts):
        return [lax.ppermute(parts[turn - 1], "ctx", rings[turn]) for turn in (1, 2, 3)]

    sends = [
        pack(place, arrays, block_len, start, count) for start, count in zip(starts, chunk_heads)
    ]
    piece, sends = lax.optimization_barrier((piece, sends))
    moved = [turned(parts) for parts in sends]

    by_group = lax.all_gather(jnp.full((8, lane), length.astype(f32)), "group", tiled=True)
    slot_tokens = jnp.sum(by_group.reshape(-1, 8, lane)[:, 0], 0, keepdims=True)
    scalars = jnp.concatenate(
        [slot_tokens, jnp.full((1, lane), reward), jnp.zeros((6, lane), f32)], 0
    )
    prompt = lax.all_gather(jnp.concatenate([piece, scalars], 0), "slot")
    rows = piece.shape[0]
    token_total = jnp.sum(prompt[:, rows, 0])
    reward_total = jnp.sum(prompt[:, rows + 1, 0])
    slots, groups = lax.axis_size("slot"), lax.axis_size("group")
    advantage = reward - reward_total / slots
    factor = (loss_scale * advantage * (groups * slots) / token_total).reshape(1)

    out = ()
    for start, count, parts in zip(starts, chunk_heads, moved):
        out = main(
            place, decay_rate, factor, arrays, parts, prompt, out, block_len, start, count
        )
    back = turned(out[1:4])
    terms = lax.all_to_all(out[4].reshape(slots, rows, lane), "slot", 0, 0, tiled=True)
    summed = jnp.sum(terms, 0, keepdims=True)
    summed = lax.ppermute(summed, ("slot", "ctx"), [(there, home) for home, there in moves])
    key_grad = put(place, [out[0], *back], block_len, width)
    return (key_grad.reshape(1, 1, block_len, width), summed)


def solution(mesh):
    placed = (
        P("group", "slot", "ctx", None),
        P("group", "slot", "ctx", None),
        P("group", "slot", "ctx", None),
        P("group", "slot"),
        P("group", "slot"),
        P(),
        P("group", ("slot", "ctx"), None),
    )
    return jax.shard_map(
        shards,
        mesh=mesh,
        in_specs=placed,
        out_specs=(P("group", "slot", "ctx", None), P("group", ("slot", "ctx"), None)),
        check_vma=False,
    )
```

time: 212 us -> 150 us (0.71)
  waiting for transfers between devices: 48.4 us -> 32.3 us
  between operations: 16.9 us -> 3.48 us
  local copies, waits for them, and re-layouts: 16.7 us -> 3.84 us
  starting transfers between devices: 50.6 us -> 39.2 us
  Pallas kernels: 27 us -> 17.1 us
    reduce_scatter x1 -> x0, waiting for transfers between devices: 47.2 us -> none  [shards(): lax.psum_scatter(prompt_grad.reshape(-1, rows, lane), 'slot', tiled=True)]
    ppermute x12 -> x6, starting transfers between devices: 44.7 us -> 16.9 us  [turned(): lax.ppermute(parts[turn - 1], 'ctx', rings[turn])]
    all_to_all x0 -> x1, waiting for transfers between devices: none -> 21.4 us  [shards(): lax.all_to_all(out[4].reshape(slots, rows, lane), 'slot', 0, 0, tiled=True)]
    all_to_all x0 -> x1, starting transfers between devices: none -> 15.6 us  [shards(): lax.all_to_all(out[4].reshape(slots, rows, lane), 'slot', 0, 0, tiled=True)]
    unnamed x54 -> x14, local copies, waits for them, and re-layouts: 16.5 us -> 3.69 us
    pallas_call x6 -> x3, Pallas kernels: 27 us -> 17.1 us  [the longest x1 9.57 us: main(): pl.pallas_call(functools.partial(main_body, start, heads, len(so_far)), g...]
    ppermute x12 -> x6, waiting for transfers between devices: 0.03 us -> 8.91 us  [turned(): lax.ppermute(parts[turn - 1], 'ctx', rings[turn])]
    all_gather x1, blocking collectives: 36.3 us -> 38.6 us  [shards(): prompt = lax.all_gather(jnp.concatenate([piece, scalars], 0), 'slot')]
  transfers between devices with their start and end apart: 15 -> 9, of which waited for: 2 -> 3; matrix products, arithmetic and copies ran while one was open for 1% -> 2% of each run, Pallas kernels for 7% -> 5%
where the time goes in v2:
time: 150 us
  blocking collectives  52 us (35%)
  starting transfers between devices  39.2 us (26%)
  waiting for transfers between devices  32.3 us (22%)
  Pallas kernels  17.1 us (11%)
  local copies, waits for them, and re-layouts  3.84 us (3%)
  between operations  3.48 us (2%)
  other arithmetic  1.64 us (1%)
    all_gather x1, blocking collectives, shards(): prompt = lax.all_gather(jnp.concatenate([piece, scalars], 0), 'slot')  38.6 us
    all_to_all x1, waiting for transfers between devices, shards(): lax.all_to_all(out[4].reshape(slots, rows, lane), 'slot', 0, 0, tiled=True)  21.4 us
    ppermute x6, starting transfers between devices, turned(): lax.ppermute(parts[turn - 1], 'ctx', rings[turn])  16.9 us
    all_to_all x1, starting transfers between devices, shards(): lax.all_to_all(out[4].reshape(slots, rows, lane), 'slot', 0, 0, tiled=True)  15.6 us
    unnamed x1, blocking collectives  13.4 us
    pallas_call x1, Pallas kernels, main(): pl.pallas_call(functools.partial(main_body, start, heads, len(so_far)), g...  9.57 us
    ppermute x6, waiting for transfers between devices, turned(): lax.ppermute(parts[turn - 1], 'ctx', rings[turn])  8.91 us
    ppermute x1, starting transfers between devices, shards(): piece = lax.ppermute(prompt_state[0], ('slot', 'ctx'), moves)  4.67 us
  transfers between devices with their start and end apart: 9, of which 3 were waited for; matrix products, arithmetic and copies ran while one was open for 2% of the time, Pallas kernels for 5%

profile of v2, /device:TPU:6, one launch (start us, length us, event | category | flops | bytes accessed | tf_op | source)
XLA Modules:
  0.0 149.5 jit_solution(7038827110632107139)
XLA Ops:
  0.6 4.7 %collective-permute-start = (f32[64,128]{1,0:T(8,128)}, f32[64,128]{1,0:T(8,128)S(1)}, u32[]{:S(2)}, u32[]{:S(2)}) collective-permute-start(f32[64,128]{1,0:T(8,128)} %bitcast.33), channel_id=1, source_target_pairs={{0,0},{1,4},{8,8},{9,12},{16,16},{17,20},{24,24},{25,28},{32,32},{... | collective-permute-start | bytes 98312 | tf_op jit(solution)/shard_map/ppermute | solution.py:237
  6.0 0.7 pad_add_fusion.place
  6.6 4.5 %shard_map.86 = (f32[3,8,128,128]{3,2,1,0:T(8,128)}, f32[3,8,128,128]{3,2,1,0:T(8,128)}, f32[3,8,128,128]{3,2,1,0:T(8,128)}) custom-call(s32[2]{0:T(128)} %pad_add_fusion.place, bf16[128,4096]{1,0:T(8,128)(2,1)} %bitcast.21, bf16[128,4096]{1,0:T(8,128)(2,1)} %bitcast.23, bf16[128,4096]{1,0:T(8,128)(2,1)} %bitcast.25), custom_call_target="tpu_custom_call" | custom-call | bytes 7864320 | tf_op jit(solution)/shard_map/pallas_call | solution.py:38
  11.1 0.0 collective-permute-done
  11.1 4.5 %collective-permute-start.1 = (f32[3,8,128,128]{3,2,1,0:T(8,128)}, f32[3,8,128,128]{3,2,1,0:T(8,128)S(1)}, u32[]{:S(2)}, u32[]{:S(2)}) collective-permute-start(f32[3,8,128,128]{3,2,1,0:T(8,128)} %get-tuple-element.18), channel_id=1, source_target_pairs={{0,1},{1,2},{2,3},{3,0},{4,5},{5,6},{6,7},{7,4},{8,9},{9,10},{10,1... | collective-permute-start | bytes 4718600 | tf_op jit(solution)/shard_map/ppermute | solution.py:242
  15.6 1.9 %collective-permute-start.2 = (f32[3,8,128,128]{3,2,1,0:T(8,128)}, f32[3,8,128,128]{3,2,1,0:T(8,128)}, u32[]{:S(2)}, u32[]{:S(2)}) collective-permute-start(f32[3,8,128,128]{3,2,1,0:T(8,128)} %get-tuple-element.19), channel_id=1, source_target_pairs={{0,2},{1,3},{2,0},{3,1},{4,6},{5,7},{6,4},{7,5},{8,10},{9,11},{10,... | collective-permute-start | bytes 4718600 | tf_op jit(solution)/shard_map/ppermute | solution.py:242
  17.5 2.8 %collective-permute-start.3 = (f32[3,8,128,128]{3,2,1,0:T(8,128)}, f32[3,8,128,128]{3,2,1,0:T(8,128)}, u32[]{:S(2)}, u32[]{:S(2)}) collective-permute-start(f32[3,8,128,128]{3,2,1,0:T(8,128)} %get-tuple-element.20), channel_id=1, source_target_pairs={{0,3},{1,0},{2,1},{3,2},{4,7},{5,4},{6,5},{7,6},{8,11},{9,8},{10,9... | collective-permute-start | bytes 4718600 | tf_op jit(solution)/shard_map/ppermute | solution.py:242
  20.3 1.3 dynamic-slice
  21.6 0.7 bitcast_dynamic-update-slice_fusion
  22.2 13.4 %all-reduce = f32[8]{0:T(128)S(1)} all-reduce(f32[8]{0:T(128)S(1)} %bitcast_dynamic-update-slice_fusion), channel_id=3, replica_groups=mesh['group'=8,'slot'=16,'ctx'=4] {'group'}, use_global_device_ids=true, to_apply=%add | all-reduce | flops 8 | bytes 64
  36.3 0.1 pad.2.clone
  36.4 0.1 pad.3.clone
  36.4 0.1 broadcast_reduce_fusion
  36.5 0.1 maximum_maximum_fusion
  36.6 38.6 %all-gather.1 = f32[1152,128]{1,0:T(8,128)S(1)} all-gather(f32[72,128]{1,0:T(8,128)S(1)} %maximum_maximum_fusion), channel_id=4, replica_groups=mesh['group'=8,'slot'=16,'ctx'=4] {'slot'}, dimensions={0}, use_global_device_ids=true | all-gather | bytes 626688 | tf_op jit(solution)/shard_map/all_gather | solution.py:255
  75.2 0.0 copy-start
  75.2 0.8 slice_reduce_fusion
  77.3 0.0 collective-permute-done.1.refs_3_
  77.3 0.0 copy-start.1
  77.3 0.0 collective-permute-done.2.refs_4_
  77.4 8.9 %collective-permute-done.3.refs_5_ = f32[3,8,128,128]{3,2,1,0:T(8,128)} collective-permute-done((f32[3,8,128,128]{3,2,1,0:T(8,128)}, f32[3,8,128,128]{3,2,1,0:T(8,128)}, u32[]{:S(2)}, u32[]{:S(2)}) %collective-permute-start.3) | collective-permute-done | bytes 1572896 | tf_op jit(solution)/shard_map/ppermute | solution.py:242
  86.3 0.0 copy-done
  86.3 0.0 copy-done.1
  86.3 9.6 %shard_map.87 = (f32[8,128,128]{2,1,0:T(8,128)}, f32[8,128,128]{2,1,0:T(8,128)}, f32[8,128,128]{2,1,0:T(8,128)}, f32[8,128,128]{2,1,0:T(8,128)}, f32[8,128,128]{2,1,0:T(8,128)}) custom-call(s32[2]{0:T(128)} %pad_add_fusion.place, f32[32]{0:T(128)} %rates.1, f32[1]{0:T(128)} %bitcast.11.factor_ref, bf16[128,4096]{1,0:T(8,128)(2,1)} %bitcast.22, ...), custom_call_target="tpu_custom_call" | custom-call | flops 2013265920 | bytes 10485760 | tf_op jit(solution)/shard_map/pallas_call | solution.py:175
  95.8 15.6 %all-to-all-start = ((f32[16,64,128]{2,1,0:T(8,128)}), f32[16,64,128]{2,1,0:T(8,128)S(1)}, u32[]{:S(2)}, u32[]{:S(2)}) async-start(f32[16,64,128]{2,1,0:T(8,128)} %bitcast.30), calls=%async_computation | async-start | bytes 1048576 | tf_op jit(solution)/shard_map/all_to_all | solution.py:269
  111.5 2.5 %collective-permute-start.4 = (f32[8,128,128]{2,1,0:T(8,128)}, f32[8,128,128]{2,1,0:T(8,128)S(1)}, u32[]{:S(2)}, u32[]{:S(2)}) collective-permute-start(f32[8,128,128]{2,1,0:T(8,128)} %get-tuple-element.22), channel_id=1, source_target_pairs={{0,1},{1,2},{2,3},{3,0},{4,5},{5,6},{6,7},{7,4},{8,9},{9,10},{10,1... | collective-permute-start | bytes 1572872 | tf_op jit(solution)/shard_map/ppermute | solution.py:242
  114.0 2.5 %collective-permute-start.5 = (f32[8,128,128]{2,1,0:T(8,128)}, f32[8,128,128]{2,1,0:T(8,128)S(1)}, u32[]{:S(2)}, u32[]{:S(2)}) collective-permute-start(f32[8,128,128]{2,1,0:T(8,128)} %get-tuple-element.23), channel_id=1, source_target_pairs={{0,2},{1,3},{2,0},{3,1},{4,6},{5,7},{6,4},{7,5},{8,10},{9,11},{10,... | collective-permute-start | bytes 1572872 | tf_op jit(solution)/shard_map/ppermute | solution.py:242
  116.5 2.8 %collective-permute-start.6 = (f32[8,128,128]{2,1,0:T(8,128)}, f32[8,128,128]{2,1,0:T(8,128)S(1)}, u32[]{:S(2)}, u32[]{:S(2)}) collective-permute-start(f32[8,128,128]{2,1,0:T(8,128)} %get-tuple-element.24), channel_id=1, source_target_pairs={{0,3},{1,0},{2,1},{3,2},{4,7},{5,4},{6,5},{7,6},{8,11},{9,8},{10,9... | collective-permute-start | bytes 1572872 | tf_op jit(solution)/shard_map/ppermute | solution.py:242
  119.3 21.4 %all-to-all-done = f32[16,64,128]{2,1,0:T(8,128)S(1)} async-done(((f32[16,64,128]{2,1,0:T(8,128)}), f32[16,64,128]{2,1,0:T(8,128)S(1)}, u32[]{:S(2)}, u32[]{:S(2)}) %all-to-all-start) | async-done | bytes 524320 | tf_op jit(solution)/shard_map/all_to_all | solution.py:269
  140.7 1.9 %collective-permute-start.7 = (f32[1,64,128]{2,1,0:T(8,128)S(1)}, f32[1,64,128]{2,1,0:T(8,128)S(1)}, u32[]{:S(2)}, u32[]{:S(2)}) collective-permute-start(f32[1,64,128]{2,1,0:T(8,128)S(1)} %bitcast.31), channel_id=1, source_target_pairs={{0,0},{4,1},{8,8},{12,9},{16,16},{20,17},{24,24},{28,25},{32,32},{... | collective-permute-start | bytes 98312 | tf_op jit(solution)/shard_map/ppermute | solution.py:271
  142.6 0.0 collective-permute-done.4.refs_1_
  142.6 0.0 copy-start.2
  142.7 0.0 collective-permute-done.5.refs_2_
  142.7 0.0 copy-start.3
  142.7 0.0 collective-permute-done.6.refs_3_
  142.7 0.0 copy-start.4
  142.7 0.7 copy-done.2
  143.4 0.2 copy-done.3
  143.6 0.2 copy-done.4
  143.8 3.1 %shard_map.88 = bf16[128,4096]{1,0:T(8,128)(2,1)} custom-call(s32[2]{0:T(128)} %pad_add_fusion.place, f32[8,128,128]{2,1,0:T(8,128)} %get-tuple-element.21.refs_0_, f32[8,128,128]{2,1,0:T(8,128)} %copy-done.2, f32[8,128,128]{2,1,0:T(8,128)} %copy-done.3, f32[8,128,128]{2,1,0:T(8,128)} %copy-done.4), custom_call_target="tpu_custom_call" | custom-call | bytes 3145728 | tf_op jit(solution)/shard_map/pallas_call | solution.py:205
  146.9 2.0 %collective-permute-done.7 = f32[1,64,128]{2,1,0:T(8,128)S(1)} collective-permute-done((f32[1,64,128]{2,1,0:T(8,128)S(1)}, f32[1,64,128]{2,1,0:T(8,128)S(1)}, u32[]{:S(2)}, u32[]{:S(2)}) %collective-permute-start.7) | collective-permute-done | bytes 32800 | tf_op jit(solution)/shard_map/ppermute | solution.py:271
  148.9 0.6 copy.13
  (3 shorter events, 0.0 us)
Async XLA Ops:
  0.6 10.4 %collective-permute-start = (f32[64,128]{1,0:T(8,128)}, f32[64,128]{1,0:T(8,128)S(1)}, u32[]{:S(2)}, u32[]{:S(2)}) collective-permute-start(f32[64,128]{1,0:T(8,128)} %bitcast.33), channel_id=1, source_target_pairs={{0,0},{1,4},{8,8},{9,12},{16,16},{17,20},{24,24},{25,28},{32,32},{... | collective-permute-start | bytes 98312 | tf_op jit(solution)/shard_map/ppermute | solution.py:237
  11.1 66.3 %collective-permute-start.1 = (f32[3,8,128,128]{3,2,1,0:T(8,128)}, f32[3,8,128,128]{3,2,1,0:T(8,128)S(1)}, u32[]{:S(2)}, u32[]{:S(2)}) collective-permute-start(f32[3,8,128,128]{3,2,1,0:T(8,128)} %get-tuple-element.18), channel_id=1, source_target_pairs={{0,1},{1,2},{2,3},{3,0},{4,5},{5,6},{6,7},{7,4},{8,9},{9,10},{10,1... | collective-permute-start | bytes 4718600 | tf_op jit(solution)/shard_map/ppermute | solution.py:242
  15.6 61.8 %collective-permute-start.2 = (f32[3,8,128,128]{3,2,1,0:T(8,128)}, f32[3,8,128,128]{3,2,1,0:T(8,128)}, u32[]{:S(2)}, u32[]{:S(2)}) collective-permute-start(f32[3,8,128,128]{3,2,1,0:T(8,128)} %get-tuple-element.19), channel_id=1, source_target_pairs={{0,2},{1,3},{2,0},{3,1},{4,6},{5,7},{6,4},{7,5},{8,10},{9,11},{10,... | collective-permute-start | bytes 4718600 | tf_op jit(solution)/shard_map/ppermute | solution.py:242
  17.5 68.8 %collective-permute-start.3 = (f32[3,8,128,128]{3,2,1,0:T(8,128)}, f32[3,8,128,128]{3,2,1,0:T(8,128)}, u32[]{:S(2)}, u32[]{:S(2)}) collective-permute-start(f32[3,8,128,128]{3,2,1,0:T(8,128)} %get-tuple-element.20), channel_id=1, source_target_pairs={{0,3},{1,0},{2,1},{3,2},{4,7},{5,4},{6,5},{7,6},{8,11},{9,8},{10,9... | collective-permute-start | bytes 4718600 | tf_op jit(solution)/shard_map/ppermute | solution.py:242
  75.2 11.1 %copy-start = (f32[1152,128]{1,0:T(8,128)}, f32[1152,128]{1,0:T(8,128)S(1)}, u32[]{:S(2)}) copy-start(f32[1152,128]{1,0:T(8,128)S(1)} %all-gather.1) | copy-start | bytes 1769476
  77.3 8.9 %copy-start.1 = (f32[3,8,128,128]{3,2,1,0:T(8,128)}, f32[3,8,128,128]{3,2,1,0:T(8,128)S(1)}, u32[]{:S(2)}) copy-start(f32[3,8,128,128]{3,2,1,0:T(8,128)S(1)} %collective-permute-done.1.refs_3_) | copy-start | bytes 4718596
  95.8 44.8 %all-to-all-start = ((f32[16,64,128]{2,1,0:T(8,128)}), f32[16,64,128]{2,1,0:T(8,128)S(1)}, u32[]{:S(2)}, u32[]{:S(2)}) async-start(f32[16,64,128]{2,1,0:T(8,128)} %bitcast.30), calls=%async_computation | async-start | bytes 1048576 | tf_op jit(solution)/shard_map/all_to_all | solution.py:269
  111.5 31.1 %collective-permute-start.4 = (f32[8,128,128]{2,1,0:T(8,128)}, f32[8,128,128]{2,1,0:T(8,128)S(1)}, u32[]{:S(2)}, u32[]{:S(2)}) collective-permute-start(f32[8,128,128]{2,1,0:T(8,128)} %get-tuple-element.22), channel_id=1, source_target_pairs={{0,1},{1,2},{2,3},{3,0},{4,5},{5,6},{6,7},{7,4},{8,9},{9,10},{10,1... | collective-permute-start | bytes 1572872 | tf_op jit(solution)/shard_map/ppermute | solution.py:242
  114.0 28.7 %collective-permute-start.5 = (f32[8,128,128]{2,1,0:T(8,128)}, f32[8,128,128]{2,1,0:T(8,128)S(1)}, u32[]{:S(2)}, u32[]{:S(2)}) collective-permute-start(f32[8,128,128]{2,1,0:T(8,128)} %get-tuple-element.23), channel_id=1, source_target_pairs={{0,2},{1,3},{2,0},{3,1},{4,6},{5,7},{6,4},{7,5},{8,10},{9,11},{10,... | collective-permute-start | bytes 1572872 | tf_op jit(solution)/shard_map/ppermute | solution.py:242
  116.5 26.2 %collective-permute-start.6 = (f32[8,128,128]{2,1,0:T(8,128)}, f32[8,128,128]{2,1,0:T(8,128)S(1)}, u32[]{:S(2)}, u32[]{:S(2)}) collective-permute-start(f32[8,128,128]{2,1,0:T(8,128)} %get-tuple-element.24), channel_id=1, source_target_pairs={{0,3},{1,0},{2,1},{3,2},{4,7},{5,4},{6,5},{7,6},{8,11},{9,8},{10,9... | collective-permute-start | bytes 1572872 | tf_op jit(solution)/shard_map/ppermute | solution.py:242
  140.7 8.2 %collective-permute-start.7 = (f32[1,64,128]{2,1,0:T(8,128)S(1)}, f32[1,64,128]{2,1,0:T(8,128)S(1)}, u32[]{:S(2)}, u32[]{:S(2)}) collective-permute-start(f32[1,64,128]{2,1,0:T(8,128)S(1)} %bitcast.31), channel_id=1, source_target_pairs={{0,0},{4,1},{8,8},{12,9},{16,16},{20,17},{24,24},{28,25},{32,32},{... | collective-permute-start | bytes 98312 | tf_op jit(solution)/shard_map/ppermute | solution.py:271
  142.6 0.8 copy-start.2
  142.7 0.9 copy-start.3
  142.7 1.1 copy-start.4

commit v3 on v2

--- a/solution.py
+++ b/solution.py
@@ -10,7 +10,7 @@
 loss_scale = 16.0
 f32 = jnp.float32
 bf16 = jnp.bfloat16
-chunk_heads = (8,)
+early, late = 6, 2
 lane = 128
 
 
@@ -23,37 +23,49 @@
     return hi, (x - hi.astype(f32)).astype(bf16)
 
 
-def pack_body(heads, place, *refs):
-    sources, sends = refs[:3], refs[3:]
-    for turn in range(3):
-        owner = lax.rem(place[0] + turn + 1, 4)
+def residue(device):
+    return 2 * lax.rem(device, 2) + lax.div(device, 2)
+
+
+def pack_body(heads, *refs):
+    sources, across, soon, later = refs[:3], refs[3], refs[4:6], refs[6:8]
+
+    def move(turn, send):
+        owner = residue(lax.rem(lax.axis_index("ctx") + turn, 4))
         for which in range(3):
             for step in range(heads):
                 column = pl.multiple_of((owner + 4 * step) * lane, lane)
-                sends[turn][which, step] = sources[which][:, pl.ds(column, lane)].astype(f32)
-
-
-def pack(place, arrays, block_len, start, count, heads=4):
-    first = start // heads
+                send[which, step] = sources[which][:, pl.ds(column, lane)].astype(f32)
+
+    move(2, across)
+
+    @pl.when(pl.program_id(0) < early // heads)
+    def _():
+        move(1, soon[0])
+        move(3, soon[1])
+
+    @pl.when(pl.program_id(0) >= early // heads)
+    def _():
+        move(1, later[0])
+        move(3, later[1])
+
+
+def pack(arrays, block_len, heads=2):
+    turns = early // heads
+    block = (3, heads, block_len, lane)
+    soon = pl.BlockSpec(block, lambda m: (0, lax.min(m, turns - 1), 0, 0))
+    later = pl.BlockSpec(block, lambda m: (0, lax.max(m - turns, 0), 0, 0))
+    counts = (early + late, early, early, late, late)
     return pl.pallas_call(
         functools.partial(pack_body, heads),
-        grid_spec=pltpu.PrefetchScalarGridSpec(
-            num_scalar_prefetch=1,
-            grid=(count // heads,),
-            in_specs=[
-                pl.BlockSpec((block_len, 4 * heads * lane), lambda m, place: (0, first + m))
-            ]
-            * 3,
-            out_specs=[
-                pl.BlockSpec((3, heads, block_len, lane), lambda m, place: (0, m, 0, 0))
-            ]
-            * 3,
-        ),
-        out_shape=[jax.ShapeDtypeStruct((3, count, block_len, lane), f32)] * 3,
+        grid=((early + late) // heads,),
+        in_specs=[pl.BlockSpec((block_len, 4 * heads * lane), lambda m: (0, m))] * 3,
+        out_specs=[pl.BlockSpec(block, lambda m: (0, m, 0, 0)), soon, soon, later, later],
+        out_shape=[jax.ShapeDtypeStruct((3, count, block_len, lane), f32) for count in counts],
         cost_estimate=pl.CostEstimate(
-            flops=0, bytes_accessed=60 * count * block_len * lane, transcendentals=0
-        ),
-    )(place, *arrays)
+            flops=0, bytes_accessed=60 * (early + late) * block_len * lane, transcendentals=0
+        ),
+    )(*arrays)
 
 
 def head_grads(rates, factor, length, rows, states):
@@ -117,8 +129,8 @@
 
 
 def main_body(start, heads, aliased, place, rates, factor_ref, *refs):
-    local, moved, prompt_ref = refs[:3], refs[3:6], refs[6]
-    refs = refs[7 + aliased :]
+    local, refs = refs[: 3 * heads], refs[3 * heads :]
+    moved, prompt_ref, refs = refs[:3], refs[3], refs[4 + aliased :]
     outs, prompt_grad_ref = refs[:4], refs[4]
     rows_q, rows_k, rows_v, grads_ref = refs[5:]
     me, length = place[0], place[1]
@@ -127,8 +139,7 @@
         for turn in range(4):
             block = lax.rem(me + 4 - turn, 4)
             if turn == 0:
-                column = pl.ds(pl.multiple_of((me + 4 * step) * lane, lane), lane)
-                q, k, v = (r[:, column].astype(f32) for r in local)
+                q, k, v = (r[...].astype(f32) for r in local[3 * step : 3 * step + 3])
             else:
                 q, k, v = (moved[turn - 1][which, step] for which in range(3))
             keep = (row + lane * block < length).astype(f32)
@@ -136,7 +147,7 @@
             rows_k[step, block] = (k * keep).astype(bf16)
             rows_v[step, block] = (v * keep).astype(bf16)
     half, steps = lane // 2, range(heads)
-    head = me + 4 * (start + pl.program_id(0) * heads)
+    head = residue(me) + 4 * (start + pl.program_id(0) * heads)
     prompts = [
         jnp.concatenate([prompt_ref[2 * step, :half], prompt_ref[2 * step + 1, :half]], 0)
         for step in steps
@@ -161,14 +172,22 @@
     assert block_len == lane
     first, total = start // heads, prompt.shape[0] // 2
     in_specs = [pl.BlockSpec(memory_space=pltpu.SMEM)] * 2
+
+    def column(step):
+        return lambda m, place: (0, residue(place[0]) + 4 * (start + m * heads + step))
+
+    def rest(part):
+        skipped = 0 if part.shape[1] == count else first
+        return lambda m, place: (0, m + skipped, 0, 0)
+
     in_specs += [
-        pl.BlockSpec((block_len, 4 * heads * lane), lambda m, place: (0, first + m))
-    ] * 3
-    in_specs += [pl.BlockSpec((3, heads, block_len, lane), lambda m, place: (0, m, 0, 0))] * 3
+        pl.BlockSpec((block_len, lane), column(step)) for step in range(heads) for _ in arrays
+    ]
+    in_specs += [pl.BlockSpec((3, heads, block_len, lane), rest(part)) for part in moved]
     in_specs += [
         pl.BlockSpec((2 * heads,) + prompt.shape[1:], lambda m, place: (first + m, 0, 0))
     ]
-    args = [place, rates, factor, *arrays, *moved, prompt]
+    args = [place, rates, factor, *(list(arrays) * heads), *moved, prompt]
     aliases = {len(args) + n: n for n in range(len(so_far))}
     in_specs += [pl.BlockSpec(memory_space=pl.ANY)] * len(so_far)
     one = pl.BlockSpec((heads, block_len, lane), lambda m, place: (first + m, 0, 0))
@@ -195,7 +214,7 @@
 def put_body(heads, place, *refs):
     parts, out = refs[:4], refs[4]
     for turn in range(4):
-        owner = lax.rem(place[0] + 4 - turn, 4)
+        owner = residue(lax.rem(place[0] + 4 - turn, 4))
         for step in range(heads):
             column = pl.multiple_of((owner + 4 * step) * lane, lane)
             out[:, pl.ds(column, lane)] = parts[turn][step].astype(bf16)
@@ -217,13 +236,8 @@
     )(place, *parts)
 
 
-def piece_moves():
-    moves = []
-    for ctx in range(4):
-        for slot in range(16):
-            home = 4 * (2 * (slot // 2) + ctx // 2) + 2 * (ctx % 2) + slot % 2
-            moves.append((home, 4 * slot + ctx))
-    return moves
+def home(ctx, piece):
+    return 4 * (2 * (piece // 2) + ctx % 2) + 2 * (ctx // 2) + piece % 2
 
 
 def shards(queries, keys, values, lengths, rewards, decay_rate, prompt_state):
@@ -232,23 +246,19 @@
     ctx_index = lax.axis_index("ctx").astype(jnp.int32)
     length, reward = lengths[0, 0], rewards[0, 0]
     place = jnp.stack([ctx_index, length])
-    moves = piece_moves()
+    moves = [(home(ctx, slot), 4 * slot + ctx) for slot in range(16) for ctx in range(4)]
 
     piece = lax.ppermute(prompt_state[0], ("slot", "ctx"), moves)
     rings = [[(i, (i + turn) % 4) for i in range(4)] for turn in range(4)]
-    starts = [sum(chunk_heads[:n]) for n in range(len(chunk_heads))]
-
-    def turned(parts):
-        return [lax.ppermute(parts[turn - 1], "ctx", rings[turn]) for turn in (1, 2, 3)]
-
-    sends = [
-        pack(place, arrays, block_len, start, count) for start, count in zip(starts, chunk_heads)
-    ]
-    piece, sends = lax.optimization_barrier((piece, sends))
-    moved = [turned(parts) for parts in sends]
-
-    by_group = lax.all_gather(jnp.full((8, lane), length.astype(f32)), "group", tiled=True)
-    slot_tokens = jnp.sum(by_group.reshape(-1, 8, lane)[:, 0], 0, keepdims=True)
+
+    def turned(part, turn):
+        return lax.ppermute(part, "ctx", rings[turn])
+
+    piece, sends = lax.optimization_barrier((piece, pack(arrays, block_len)))
+    across = turned(sends[0], 2)
+    moved = [(turned(sends[n], 1), across, turned(sends[n + 1], 3)) for n in (1, 3)]
+
+    slot_tokens = jnp.full((1, lane), lax.psum(length.astype(f32), "group"))
     scalars = jnp.concatenate(
         [slot_tokens, jnp.full((1, lane), reward), jnp.zeros((6, lane), f32)], 0
     )
@@ -261,11 +271,11 @@
     factor = (loss_scale * advantage * (groups * slots) / token_total).reshape(1)
 
     out = ()
-    for start, count, parts in zip(starts, chunk_heads, moved):
+    for start, count, parts in ((0, early, moved[0]), (early, late, moved[1])):
         out = main(
             place, decay_rate, factor, arrays, parts, prompt, out, block_len, start, count
         )
-    back = turned(out[1:4])
+    back = [turned(out[turn], turn) for turn in (1, 2, 3)]
     terms = lax.all_to_all(out[4].reshape(slots, rows, lane), "slot", 0, 0, tiled=True)
     summed = jnp.sum(terms, 0, keepdims=True)
     summed = lax.ppermute(summed, ("slot", "ctx"), [(there, home) for home, there in moves])

time: 150 us -> 141 us (0.940)
  waiting for transfers between devices: 32.3 us -> 15.6 us
  Pallas kernels: 17.1 us -> 20.5 us
  blocking collectives: 52 us -> 54.2 us
  starting transfers between devices: 39.2 us -> 41.3 us
    psum x0 -> x1, blocking collectives: none -> 14.6 us  [shards(): slot_tokens = jnp.full((1, lane), lax.psum(length.astype(f32), 'group'))]
    unnamed x1 -> x0, blocking collectives: 13.4 us -> none
    all_to_all x1, starting transfers between devices: 15.6 us -> 6.73 us  [shards(): lax.all_to_all(out[4].reshape(slots, rows, lane), 'slot', 0, 0, tiled=True)]
    ppermute x6 -> x8, waiting for transfers between devices: 8.91 us -> 0.02 us  [turned(): return lax.ppermute(part, 'ctx', rings[turn])]
    ppermute x6 -> x8, starting transfers between devices: 16.9 us -> 25.5 us  [turned(): return lax.ppermute(part, 'ctx', rings[turn])]
    all_to_all x1, waiting for transfers between devices: 21.4 us -> 15.6 us  [shards(): lax.all_to_all(out[4].reshape(slots, rows, lane), 'slot', 0, 0, tiled=True)]
    ppermute x1, starting transfers between devices: 1.92 us -> 5.03 us  [shards(): lax.ppermute(summed, ('slot', 'ctx'), [(there, home) for home, there in m...]
    pallas_call x1 -> x2, Pallas kernels: 9.57 us -> 12.3 us  [main(): pl.pallas_call(functools.partial(main_body, start, heads, len(so_far)), g...]
  transfers between devices with their start and end apart: 9 -> 11, of which waited for: 3 -> 1; matrix products, arithmetic and copies ran while one was open for 2% -> 2% of each run, Pallas kernels for 5% -> 11%
where the time goes in v3:
time: 141 us
  blocking collectives  54.2 us (38%)
  starting transfers between devices  41.3 us (29%)
  Pallas kernels  20.5 us (15%)
  waiting for transfers between devices  15.6 us (11%)
  local copies, waits for them, and re-layouts  4.04 us (3%)
  between operations  3.45 us (2%)
  other arithmetic  1.45 us (1%)
    all_gather x1, blocking collectives, shards(): prompt = lax.all_gather(jnp.concatenate([piece, scalars], 0), 'slot')  39.6 us
    ppermute x8, starting transfers between devices, turned(): return lax.ppermute(part, 'ctx', rings[turn])  25.5 us
    all_to_all x1, waiting for transfers between devices, shards(): lax.all_to_all(out[4].reshape(slots, rows, lane), 'slot', 0, 0, tiled=True)  15.6 us
    psum x1, blocking collectives, shards(): slot_tokens = jnp.full((1, lane), lax.psum(length.astype(f32), 'group'))  14.6 us
    pallas_call x2, Pallas kernels, main(): pl.pallas_call(functools.partial(main_body, start, heads, len(so_far)), g...  12.3 us
    all_to_all x1, starting transfers between devices, shards(): lax.all_to_all(out[4].reshape(slots, rows, lane), 'slot', 0, 0, tiled=True)  6.73 us
    pallas_call x1, Pallas kernels, pack(): pl.pallas_call(functools.partial(pack_body, heads), grid=((early + late)...  5.05 us
    ppermute x1, starting transfers between devices, shards(): lax.ppermute(summed, ('slot', 'ctx'), [(there, home) for home, there in m...  5.03 us
  transfers between devices with their start and end apart: 11, of which 1 were waited for; matrix products, arithmetic and copies ran while one was open for 2% of the time, Pallas kernels for 11%

profile of v3, /device:TPU:6, one launch (start us, length us, event | category | flops | bytes accessed | tf_op | source)
XLA Modules:
  0.0 140.6 jit_solution(3795179080109042207)
XLA Ops:
  0.6 4.1 %collective-permute-start = (f32[64,128]{1,0:T(8,128)}, f32[64,128]{1,0:T(8,128)S(1)}, u32[]{:S(2)}, u32[]{:S(2)}) collective-permute-start(f32[64,128]{1,0:T(8,128)} %bitcast.40), channel_id=1, source_target_pairs={{0,0},{4,1},{2,2},{6,3},{1,4},{5,5},{3,6},{7,7},{8,8},{12,9},{10,1... | collective-permute-start | bytes 98312 | tf_op jit(solution)/shard_map/ppermute | solution.py:251
  4.7 5.1 %shard_map.86 = (f32[3,8,128,128]{3,2,1,0:T(8,128)}, f32[3,6,128,128]{3,2,1,0:T(8,128)}, f32[3,6,128,128]{3,2,1,0:T(8,128)}, f32[3,2,128,128]{3,2,1,0:T(8,128)}, f32[3,2,128,128]{3,2,1,0:T(8,128)}) custom-call(bf16[128,4096]{1,0:T(8,128)(2,1)} %bitcast.19, bf16[128,4096]{1,0:T(8,128)(2,1)} %bitcast.24, bf16[128,4096]{1,0:T(8,128)(2,1)} %bitcast.29), custom_call_target="tpu_custom_call" | custom-call | bytes 7864320 | tf_op jit(solution)/shard_map/pallas_call | solution.py:59
  9.8 0.0 collective-permute-done
  9.8 3.0 %collective-permute-start.2 = (f32[3,8,128,128]{3,2,1,0:T(8,128)}, f32[3,8,128,128]{3,2,1,0:T(8,128)S(1)}, u32[]{:S(2)}, u32[]{:S(2)}) collective-permute-start(f32[3,8,128,128]{3,2,1,0:T(8,128)} %get-tuple-element.30), channel_id=1, source_target_pairs={{0,2},{1,3},{2,0},{3,1},{4,6},{5,7},{6,4},{7,5},{8,10},{9,11},{10,... | collective-permute-start | bytes 4718600 | tf_op jit(solution)/shard_map/ppermute | solution.py:255
  12.8 3.9 %collective-permute-start.4 = (f32[3,6,128,128]{3,2,1,0:T(8,128)}, f32[3,6,128,128]{3,2,1,0:T(8,128)S(1)}, u32[]{:S(2)}, u32[]{:S(2)}) collective-permute-start(f32[3,6,128,128]{3,2,1,0:T(8,128)} %get-tuple-element.32), channel_id=1, source_target_pairs={{0,1},{1,2},{2,3},{3,0},{4,5},{5,6},{6,7},{7,4},{8,9},{9,10},{10,1... | collective-permute-start | bytes 3538952 | tf_op jit(solution)/shard_map/ppermute | solution.py:255
  16.8 2.8 %collective-permute-start.5 = (f32[3,6,128,128]{3,2,1,0:T(8,128)}, f32[3,6,128,128]{3,2,1,0:T(8,128)}, u32[]{:S(2)}, u32[]{:S(2)}) collective-permute-start(f32[3,6,128,128]{3,2,1,0:T(8,128)} %get-tuple-element.33), channel_id=1, source_target_pairs={{0,3},{1,0},{2,1},{3,2},{4,7},{5,4},{6,5},{7,6},{8,11},{9,8},{10,9... | collective-permute-start | bytes 3538952 | tf_op jit(solution)/shard_map/ppermute | solution.py:255
  20.2 14.6 %psum.7 = f32[]{:T(128)} all-reduce(f32[]{:T(128)} %bitcast.7), channel_id=1, replica_groups=mesh['group'=8,'slot'=16,'ctx'=4] {'group'}, use_global_device_ids=true, to_apply=%region_0.0 | all-reduce | flops 1 | bytes 8 | tf_op jit(solution)/shard_map/psum | solution.py:261
  35.4 0.7 pad.1.clone
  36.1 0.1 pad.2.clone
  36.2 0.1 pad.3.clone
  36.3 0.6 pad_add_fusion.place
  36.9 3.8 %collective-permute-start.1 = (f32[3,2,128,128]{3,2,1,0:T(8,128)}, f32[3,2,128,128]{3,2,1,0:T(8,128)}, u32[]{:S(2)}, u32[]{:S(2)}) collective-permute-start(f32[3,2,128,128]{3,2,1,0:T(8,128)} %get-tuple-element.29), channel_id=1, source_target_pairs={{0,1},{1,2},{2,3},{3,0},{4,5},{5,6},{6,7},{7,4},{8,9},{9,10},{10,1... | collective-permute-start | bytes 1179656 | tf_op jit(solution)/shard_map/ppermute | solution.py:255
  40.7 2.0 %collective-permute-start.3 = (f32[3,2,128,128]{3,2,1,0:T(8,128)}, f32[3,2,128,128]{3,2,1,0:T(8,128)}, u32[]{:S(2)}, u32[]{:S(2)}) collective-permute-start(f32[3,2,128,128]{3,2,1,0:T(8,128)} %get-tuple-element.31), channel_id=1, source_target_pairs={{0,3},{1,0},{2,1},{3,2},{4,7},{5,4},{6,5},{7,6},{8,11},{9,8},{10,9... | collective-permute-start | bytes 1179656 | tf_op jit(solution)/shard_map/ppermute | solution.py:255
  42.7 0.1 maximum_maximum_fusion
  42.8 39.6 %all-gather = f32[1152,128]{1,0:T(8,128)S(1)} all-gather(f32[72,128]{1,0:T(8,128)S(1)} %maximum_maximum_fusion), channel_id=2, replica_groups=mesh['group'=8,'slot'=16,'ctx'=4] {'slot'}, dimensions={0}, use_global_device_ids=true | all-gather | bytes 626688 | tf_op jit(solution)/shard_map/all_gather | solution.py:265
  82.4 0.0 copy-start.1
  82.4 0.7 slice_reduce_fusion
  84.4 0.0 collective-permute-done.4.refs_6_
  84.5 0.0 copy-start.2
  84.5 0.0 collective-permute-done.5.refs_8_
  84.5 0.0 collective-permute-done.2.refs_7_
  84.5 0.0 copy-start
  84.5 0.0 copy-done.1
  84.5 1.0 copy-done.2
  85.5 0.5 copy-done
  86.0 7.9 %shard_map.87 = (f32[8,128,128]{2,1,0:T(8,128)}, f32[8,128,128]{2,1,0:T(8,128)}, f32[8,128,128]{2,1,0:T(8,128)}, f32[8,128,128]{2,1,0:T(8,128)}, f32[8,128,128]{2,1,0:T(8,128)}) custom-call(s32[2]{0:T(128)} %pad_add_fusion.place, f32[32]{0:T(128)} %rates.3, f32[1]{0:T(128)} %bitcast.9.factor_ref, bf16[128,4096]{1,0:T(8,128)(2,1)} %bitcast.20, ...), custom_call_target="tpu_custom_call" | custom-call | flops 1509949440 | bytes 7864320 | tf_op jit(solution)/shard_map/pallas_call | solution.py:194
  93.8 0.0 collective-permute-done.1.refs_6_
  93.9 0.0 collective-permute-done.3.refs_8_
  93.9 4.5 %shard_map.88 = (f32[8,128,128]{2,1,0:T(8,128)}, f32[8,128,128]{2,1,0:T(8,128)}, f32[8,128,128]{2,1,0:T(8,128)}, f32[8,128,128]{2,1,0:T(8,128)}, f32[8,128,128]{2,1,0:T(8,128)}) custom-call(s32[2]{0:T(128)} %pad_add_fusion.place, f32[32]{0:T(128)} %rates.3, ...), custom_call_target="tpu_custom_call", output_to_operand_aliasing={{0}: (13, {}), {1}: (14, {}), {2}: (15, {}), {3}: (16, {}),... | custom-call | flops 503316480 | bytes 2621440 | tf_op jit(solution)/shard_map/pallas_call | solution.py:194
  98.3 6.7 %all-to-all-start = ((f32[16,64,128]{2,1,0:T(8,128)}), f32[16,64,128]{2,1,0:T(8,128)S(1)}, u32[]{:S(2)}, u32[]{:S(2)}) async-start(f32[16,64,128]{2,1,0:T(8,128)} %bitcast.37), calls=%async_computation | async-start | bytes 1048576 | tf_op jit(solution)/shard_map/all_to_all | solution.py:279
  105.1 5.2 %collective-permute-start.6 = (f32[8,128,128]{2,1,0:T(8,128)}, f32[8,128,128]{2,1,0:T(8,128)S(1)}, u32[]{:S(2)}, u32[]{:S(2)}) collective-permute-start(f32[8,128,128]{2,1,0:T(8,128)} %get-tuple-element.40), channel_id=1, source_target_pairs={{0,1},{1,2},{2,3},{3,0},{4,5},{5,6},{6,7},{7,4},{8,9},{9,10},{10,1... | collective-permute-start | bytes 1572872 | tf_op jit(solution)/shard_map/ppermute | solution.py:255
  110.3 1.9 %collective-permute-start.7 = (f32[8,128,128]{2,1,0:T(8,128)}, f32[8,128,128]{2,1,0:T(8,128)S(1)}, u32[]{:S(2)}, u32[]{:S(2)}) collective-permute-start(f32[8,128,128]{2,1,0:T(8,128)} %get-tuple-element.41), channel_id=1, source_target_pairs={{0,2},{1,3},{2,0},{3,1},{4,6},{5,7},{6,4},{7,5},{8,10},{9,11},{10,... | collective-permute-start | bytes 1572872 | tf_op jit(solution)/shard_map/ppermute | solution.py:255
  112.3 2.8 %collective-permute-start.8 = (f32[8,128,128]{2,1,0:T(8,128)}, f32[8,128,128]{2,1,0:T(8,128)S(1)}, u32[]{:S(2)}, u32[]{:S(2)}) collective-permute-start(f32[8,128,128]{2,1,0:T(8,128)} %get-tuple-element.42), channel_id=1, source_target_pairs={{0,3},{1,0},{2,1},{3,2},{4,7},{5,4},{6,5},{7,6},{8,11},{9,8},{10,9... | collective-permute-start | bytes 1572872 | tf_op jit(solution)/shard_map/ppermute | solution.py:255
  115.0 15.6 %all-to-all-done = f32[16,64,128]{2,1,0:T(8,128)S(1)} async-done(((f32[16,64,128]{2,1,0:T(8,128)}), f32[16,64,128]{2,1,0:T(8,128)S(1)}, u32[]{:S(2)}, u32[]{:S(2)}) %all-to-all-start) | async-done | bytes 524320 | tf_op jit(solution)/shard_map/all_to_all | solution.py:279
  130.6 5.0 %collective-permute-start.9 = (f32[1,64,128]{2,1,0:T(8,128)S(1)}, f32[1,64,128]{2,1,0:T(8,128)S(1)}, u32[]{:S(2)}, u32[]{:S(2)}) collective-permute-start(f32[1,64,128]{2,1,0:T(8,128)S(1)} %bitcast.39), channel_id=1, source_target_pairs={{0,0},{1,4},{2,2},{3,6},{4,1},{5,5},{6,3},{7,7},{8,8},{9,12},{10,1... | collective-permute-start | bytes 98312 | tf_op jit(solution)/shard_map/ppermute | solution.py:281
  135.7 0.0 collective-permute-done.6.refs_1_
  135.7 0.0 copy-start.3
  135.7 0.0 collective-permute-done.7.refs_2_
  135.7 0.0 copy-start.4
  135.7 0.0 collective-permute-done.8.refs_3_
  135.7 0.0 copy-start.5
  135.7 0.7 copy-done.3
  136.5 0.2 copy-done.4
  136.7 0.2 copy-done.5
  136.8 3.1 %shard_map.89 = bf16[128,4096]{1,0:T(8,128)(2,1)} custom-call(s32[2]{0:T(128)} %pad_add_fusion.place, f32[8,128,128]{2,1,0:T(8,128)} %get-tuple-element.39.refs_0_, f32[8,128,128]{2,1,0:T(8,128)} %copy-done.3, f32[8,128,128]{2,1,0:T(8,128)} %copy-done.4, f32[8,128,128]{2,1,0:T(8,128)} %copy-done.5), custom_call_target="tpu_custom_call" | custom-call | bytes 3145728 | tf_op jit(solution)/shard_map/pallas_call | solution.py:224
  139.9 0.0 collective-permute-done.9
  139.9 0.6 copy.22
  (2 shorter events, 0.0 us)
Async XLA Ops:
  0.6 9.2 %collective-permute-start = (f32[64,128]{1,0:T(8,128)}, f32[64,128]{1,0:T(8,128)S(1)}, u32[]{:S(2)}, u32[]{:S(2)}) collective-permute-start(f32[64,128]{1,0:T(8,128)} %bitcast.40), channel_id=1, source_target_pairs={{0,0},{4,1},{2,2},{6,3},{1,4},{5,5},{3,6},{7,7},{8,8},{12,9},{10,1... | collective-permute-start | bytes 98312 | tf_op jit(solution)/shard_map/ppermute | solution.py:251
  9.8 74.7 %collective-permute-start.2 = (f32[3,8,128,128]{3,2,1,0:T(8,128)}, f32[3,8,128,128]{3,2,1,0:T(8,128)S(1)}, u32[]{:S(2)}, u32[]{:S(2)}) collective-permute-start(f32[3,8,128,128]{3,2,1,0:T(8,128)} %get-tuple-element.30), channel_id=1, source_target_pairs={{0,2},{1,3},{2,0},{3,1},{4,6},{5,7},{6,4},{7,5},{8,10},{9,11},{10,... | collective-permute-start | bytes 4718600 | tf_op jit(solution)/shard_map/ppermute | solution.py:255
  12.8 71.6 %collective-permute-start.4 = (f32[3,6,128,128]{3,2,1,0:T(8,128)}, f32[3,6,128,128]{3,2,1,0:T(8,128)S(1)}, u32[]{:S(2)}, u32[]{:S(2)}) collective-permute-start(f32[3,6,128,128]{3,2,1,0:T(8,128)} %get-tuple-element.32), channel_id=1, source_target_pairs={{0,1},{1,2},{2,3},{3,0},{4,5},{5,6},{6,7},{7,4},{8,9},{9,10},{10,1... | collective-permute-start | bytes 3538952 | tf_op jit(solution)/shard_map/ppermute | solution.py:255
  16.8 67.7 %collective-permute-start.5 = (f32[3,6,128,128]{3,2,1,0:T(8,128)}, f32[3,6,128,128]{3,2,1,0:T(8,128)}, u32[]{:S(2)}, u32[]{:S(2)}) collective-permute-start(f32[3,6,128,128]{3,2,1,0:T(8,128)} %get-tuple-element.33), channel_id=1, source_target_pairs={{0,3},{1,0},{2,1},{3,2},{4,7},{5,4},{6,5},{7,6},{8,11},{9,8},{10,9... | collective-permute-start | bytes 3538952 | tf_op jit(solution)/shard_map/ppermute | solution.py:255
  36.9 57.0 %collective-permute-start.1 = (f32[3,2,128,128]{3,2,1,0:T(8,128)}, f32[3,2,128,128]{3,2,1,0:T(8,128)}, u32[]{:S(2)}, u32[]{:S(2)}) collective-permute-start(f32[3,2,128,128]{3,2,1,0:T(8,128)} %get-tuple-element.29), channel_id=1, source_target_pairs={{0,1},{1,2},{2,3},{3,0},{4,5},{5,6},{6,7},{7,4},{8,9},{9,10},{10,1... | collective-permute-start | bytes 1179656 | tf_op jit(solution)/shard_map/ppermute | solution.py:255
  40.7 53.2 %collective-permute-start.3 = (f32[3,2,128,128]{3,2,1,0:T(8,128)}, f32[3,2,128,128]{3,2,1,0:T(8,128)}, u32[]{:S(2)}, u32[]{:S(2)}) collective-permute-start(f32[3,2,128,128]{3,2,1,0:T(8,128)} %get-tuple-element.31), channel_id=1, source_target_pairs={{0,3},{1,0},{2,1},{3,2},{4,7},{5,4},{6,5},{7,6},{8,11},{9,8},{10,9... | collective-permute-start | bytes 1179656 | tf_op jit(solution)/shard_map/ppermute | solution.py:255
  82.4 2.1 %copy-start.1 = (f32[1152,128]{1,0:T(8,128)}, f32[1152,128]{1,0:T(8,128)S(1)}, u32[]{:S(2)}) copy-start(f32[1152,128]{1,0:T(8,128)S(1)} %all-gather) | copy-start | bytes 1769476
  84.5 1.0 copy-start.2
  84.5 1.5 %copy-start = (f32[3,8,128,128]{3,2,1,0:T(8,128)}, f32[3,8,128,128]{3,2,1,0:T(8,128)S(1)}, u32[]{:S(2)}) copy-start(f32[3,8,128,128]{3,2,1,0:T(8,128)S(1)} %collective-permute-done.2.refs_7_) | copy-start | bytes 4718596
  98.3 32.3 %all-to-all-start = ((f32[16,64,128]{2,1,0:T(8,128)}), f32[16,64,128]{2,1,0:T(8,128)S(1)}, u32[]{:S(2)}, u32[]{:S(2)}) async-start(f32[16,64,128]{2,1,0:T(8,128)} %bitcast.37), calls=%async_computation | async-start | bytes 1048576 | tf_op jit(solution)/shard_map/all_to_all | solution.py:279
  105.1 30.6 %collective-permute-start.6 = (f32[8,128,128]{2,1,0:T(8,128)}, f32[8,128,128]{2,1,0:T(8,128)S(1)}, u32[]{:S(2)}, u32[]{:S(2)}) collective-permute-start(f32[8,128,128]{2,1,0:T(8,128)} %get-tuple-element.40), channel_id=1, source_target_pairs={{0,1},{1,2},{2,3},{3,0},{4,5},{5,6},{6,7},{7,4},{8,9},{9,10},{10,1... | collective-permute-start | bytes 1572872 | tf_op jit(solution)/shard_map/ppermute | solution.py:255
  110.3 25.4 %collective-permute-start.7 = (f32[8,128,128]{2,1,0:T(8,128)}, f32[8,128,128]{2,1,0:T(8,128)S(1)}, u32[]{:S(2)}, u32[]{:S(2)}) collective-permute-start(f32[8,128,128]{2,1,0:T(8,128)} %get-tuple-element.41), channel_id=1, source_target_pairs={{0,2},{1,3},{2,0},{3,1},{4,6},{5,7},{6,4},{7,5},{8,10},{9,11},{10,... | collective-permute-start | bytes 1572872 | tf_op jit(solution)/shard_map/ppermute | solution.py:255
  112.3 23.5 %collective-permute-start.8 = (f32[8,128,128]{2,1,0:T(8,128)}, f32[8,128,128]{2,1,0:T(8,128)S(1)}, u32[]{:S(2)}, u32[]{:S(2)}) collective-permute-start(f32[8,128,128]{2,1,0:T(8,128)} %get-tuple-element.42), channel_id=1, source_target_pairs={{0,3},{1,0},{2,1},{3,2},{4,7},{5,4},{6,5},{7,6},{8,11},{9,8},{10,9... | collective-permute-start | bytes 1572872 | tf_op jit(solution)/shard_map/ppermute | solution.py:255
  130.6 9.3 %collective-permute-start.9 = (f32[1,64,128]{2,1,0:T(8,128)S(1)}, f32[1,64,128]{2,1,0:T(8,128)S(1)}, u32[]{:S(2)}, u32[]{:S(2)}) collective-permute-start(f32[1,64,128]{2,1,0:T(8,128)S(1)} %bitcast.39), channel_id=1, source_target_pairs={{0,0},{1,4},{2,2},{3,6},{4,1},{5,5},{6,3},{7,7},{8,8},{9,12},{10,1... | collective-permute-start | bytes 98312 | tf_op jit(solution)/shard_map/ppermute | solution.py:281
  135.7 0.8 copy-start.3
  135.7 1.0 copy-start.4
  135.7 1.1 copy-start.5

commit v4 on v3

--- a/solution.py
+++ b/solution.py
@@ -12,6 +12,7 @@
 bf16 = jnp.bfloat16
 early, late = 6, 2
 lane = 128
+vmem_bytes = 16 * 1024 * 1024
 
 
 def dot(a, b, dims):
@@ -27,43 +28,51 @@
     return 2 * lax.rem(device, 2) + lax.div(device, 2)
 
 
-def pack_body(heads, *refs):
-    sources, across, soon, later = refs[:3], refs[3], refs[4:6], refs[6:8]
-
-    def move(turn, send):
-        owner = residue(lax.rem(lax.axis_index("ctx") + turn, 4))
-        for which in range(3):
-            for step in range(heads):
-                column = pl.multiple_of((owner + 4 * step) * lane, lane)
-                send[which, step] = sources[which][:, pl.ds(column, lane)].astype(f32)
-
-    move(2, across)
-
-    @pl.when(pl.program_id(0) < early // heads)
+def widen(turn, sources, send, heads):
+    owner = residue(lax.rem(lax.axis_index("ctx") + turn, 4))
+    for which in range(3):
+        for step in range(heads):
+            column = pl.multiple_of((owner + 4 * step) * lane, lane)
+            send[which, step] = sources[which][:, pl.ds(column, lane)].astype(f32)
+
+
+def across_body(heads, *refs):
+    widen(2, refs[:3], refs[3], heads)
+
+
+def beside_body(heads, *refs):
+    sources, soon, later = refs[:3], refs[3:5], refs[5:7]
+    turns = early // heads
+
+    @pl.when(pl.program_id(0) < turns)
     def _():
-        move(1, soon[0])
-        move(3, soon[1])
-
-    @pl.when(pl.program_id(0) >= early // heads)
+        widen(1, sources, soon[0], heads)
+        widen(3, sources, soon[1], heads)
+
+    @pl.when(pl.program_id(0) >= turns)
     def _():
-        move(1, later[0])
-        move(3, later[1])
-
-
-def pack(arrays, block_len, heads=2):
+        widen(1, sources, later[0], heads)
+        widen(3, sources, later[1], heads)
+
+
+def pack(arrays, block_len, beside, heads):
     turns = early // heads
     block = (3, heads, block_len, lane)
-    soon = pl.BlockSpec(block, lambda m: (0, lax.min(m, turns - 1), 0, 0))
-    later = pl.BlockSpec(block, lambda m: (0, lax.max(m - turns, 0), 0, 0))
-    counts = (early + late, early, early, late, late)
+    if beside:
+        soon = pl.BlockSpec(block, lambda m: (0, lax.min(m, turns - 1), 0, 0))
+        later = pl.BlockSpec(block, lambda m: (0, lax.max(m - turns, 0), 0, 0))
+        specs, counts, body = [soon, soon, later, later], (early, early, late, late), beside_body
+    else:
+        specs, counts = [pl.BlockSpec(block, lambda m: (0, m, 0, 0))], (early + late,)
+        body = across_body
     return pl.pallas_call(
-        functools.partial(pack_body, heads),
+        functools.partial(body, heads),
         grid=((early + late) // heads,),
         in_specs=[pl.BlockSpec((block_len, 4 * heads * lane), lambda m: (0, m))] * 3,
-        out_specs=[pl.BlockSpec(block, lambda m: (0, m, 0, 0)), soon, soon, later, later],
+        out_specs=specs,
         out_shape=[jax.ShapeDtypeStruct((3, count, block_len, lane), f32) for count in counts],
         cost_estimate=pl.CostEstimate(
-            flops=0, bytes_accessed=60 * (early + late) * block_len * lane, transcendentals=0
+            flops=0, bytes_accessed=48 * (early + late) * block_len * lane, transcendentals=0
         ),
     )(*arrays)
 
@@ -128,9 +137,12 @@
     return grads, ends
 
 
-def main_body(start, heads, aliased, place, rates, factor_ref, *refs):
+def main_body(start, heads, scale, aliased, place, rates, reward, *refs):
     local, refs = refs[: 3 * heads], refs[3 * heads :]
-    moved, prompt_ref, refs = refs[:3], refs[3], refs[4 + aliased :]
+    moved, prompt_ref, sums_ref, refs = refs[:3], refs[3], refs[4], refs[5 + aliased :]
+    sums = jnp.sum(sums_ref[...], 0)
+    slots = sums_ref.shape[0]
+    factor = scale * (reward[0] - sums[1:2] / slots) / sums[0:1]
     outs, prompt_grad_ref = refs[:4], refs[4]
     rows_q, rows_k, rows_v, grads_ref = refs[5:]
     me, length = place[0], place[1]
@@ -157,7 +169,7 @@
         for step in steps
     ]
     grads, ends = head_grads(
-        [rates[head + 4 * step] for step in steps], factor_ref[0], length, rows, prompts
+        [rates[head + 4 * step] for step in steps], factor, length, rows, prompts
     )
     for step in steps:
         for block in range(4):
@@ -168,7 +180,7 @@
             outs[turn][step] = grads_ref[step, lax.rem(me + turn, 4)]
 
 
-def main(place, rates, factor, arrays, moved, prompt, so_far, block_len, start, count, heads=2):
+def main(place, rates, reward, scale, arrays, moved, prompt, so_far, block_len, start, count, heads=2):
     assert block_len == lane
     first, total = start // heads, prompt.shape[0] // 2
     in_specs = [pl.BlockSpec(memory_space=pltpu.SMEM)] * 2
@@ -185,14 +197,15 @@
     ]
     in_specs += [pl.BlockSpec((3, heads, block_len, lane), rest(part)) for part in moved]
     in_specs += [
-        pl.BlockSpec((2 * heads,) + prompt.shape[1:], lambda m, place: (first + m, 0, 0))
-    ]
-    args = [place, rates, factor, *(list(arrays) * heads), *moved, prompt]
+        pl.BlockSpec((2 * heads, lane // 2, lane), lambda m, place: (first + m, 0, 0)),
+        pl.BlockSpec((prompt.shape[0], 8, lane), lambda m, place: (0, lane // 16, 0)),
+    ]
+    args = [place, rates, reward, *(list(arrays) * heads), *moved, prompt, prompt]
     aliases = {len(args) + n: n for n in range(len(so_far))}
     in_specs += [pl.BlockSpec(memory_space=pl.ANY)] * len(so_far)
     one = pl.BlockSpec((heads, block_len, lane), lambda m, place: (first + m, 0, 0))
     return pl.pallas_call(
-        functools.partial(main_body, start, heads, len(so_far)),
+        functools.partial(main_body, start, heads, scale, len(so_far)),
         grid_spec=pltpu.PrefetchScalarGridSpec(
             num_scalar_prefetch=1,
             grid=(count // heads,),
@@ -201,8 +214,9 @@
             scratch_shapes=[pltpu.VMEM((heads, 4, lane, lane), bf16)] * 3
             + [pltpu.VMEM((heads, 4, lane, lane), f32)],
         ),
-        out_shape=[jax.ShapeDtypeStruct((total, block_len, lane), f32)] * 5,
+        out_shape=[pltpu.HBM((total, block_len, lane), f32)] * 5,
         input_output_aliases=aliases,
+        compiler_params=pltpu.CompilerParams(vmem_limit_bytes=vmem_bytes),
         cost_estimate=pl.CostEstimate(
             flops=count * 4 * 15 * 2 * lane**3,
             bytes_accessed=count * lane * lane * 4 * 20,
@@ -230,6 +244,7 @@
             out_specs=pl.BlockSpec((block_len, 4 * heads * lane), lambda m, place: (0, m)),
         ),
         out_shape=jax.ShapeDtypeStruct((block_len, width), bf16),
+        compiler_params=pltpu.CompilerParams(vmem_limit_bytes=vmem_bytes),
         cost_estimate=pl.CostEstimate(
             flops=0, bytes_accessed=parts[0].size * 24, transcendentals=0
         ),
@@ -254,26 +269,23 @@
     def turned(part, turn):
         return lax.ppermute(part, "ctx", rings[turn])
 
-    piece, sends = lax.optimization_barrier((piece, pack(arrays, block_len)))
-    across = turned(sends[0], 2)
-    moved = [(turned(sends[n], 1), across, turned(sends[n + 1], 3)) for n in (1, 3)]
+    piece, (wide,) = lax.optimization_barrier((piece, pack(arrays, block_len, False, 4)))
+    across = turned(wide, 2)
+    piece, sends = lax.optimization_barrier((piece, pack(arrays, block_len, True, 2)))
+    moved = [(turned(sends[n], 1), across, turned(sends[n + 1], 3)) for n in (0, 2)]
 
     slot_tokens = jnp.full((1, lane), lax.psum(length.astype(f32), "group"))
     scalars = jnp.concatenate(
         [slot_tokens, jnp.full((1, lane), reward), jnp.zeros((6, lane), f32)], 0
     )
     prompt = lax.all_gather(jnp.concatenate([piece, scalars], 0), "slot")
-    rows = piece.shape[0]
-    token_total = jnp.sum(prompt[:, rows, 0])
-    reward_total = jnp.sum(prompt[:, rows + 1, 0])
-    slots, groups = lax.axis_size("slot"), lax.axis_size("group")
-    advantage = reward - reward_total / slots
-    factor = (loss_scale * advantage * (groups * slots) / token_total).reshape(1)
+    rows, slots = piece.shape[0], lax.axis_size("slot")
+    scale = loss_scale * lax.axis_size("group") * slots
 
     out = ()
     for start, count, parts in ((0, early, moved[0]), (early, late, moved[1])):
         out = main(
-            place, decay_rate, factor, arrays, parts, prompt, out, block_len, start, count
+            place, decay_rate, rewards[0], scale, arrays, parts, prompt, out, block_len, start, count
         )
     back = [turned(out[turn], turn) for turn in (1, 2, 3)]
     terms = lax.all_to_all(out[4].reshape(slots, rows, lane), "slot", 0, 0, tiled=True)

time: 141 us -> 137 us (0.972)
  local copies, waits for them, and re-layouts: 4.04 us -> 1.5 us
  starting transfers between devices: 41.3 us -> 39.3 us
  waiting for transfers between devices: 15.6 us -> 17.5 us
    unnamed x13 -> x11, local copies, waits for them, and re-layouts: 3.21 us -> 0.64 us
    ppermute x1, starting transfers between devices: 5.03 us -> 2.78 us  [shards(): lax.ppermute(summed, ('slot', 'ctx'), [(there, home) for home, there in m...]
    ppermute x1, waiting for transfers between devices: 0.01 us -> 2.23 us  [shards(): lax.ppermute(summed, ('slot', 'ctx'), [(there, home) for home, there in m...]
    pallas_call x3 -> x4, Pallas kernels: 17.4 us -> 19.2 us  [the longest x2 11.7 us: main(): pl.pallas_call(functools.partial(main_body, start, heads, scale, len(so_f...]
    pallas_call x1, Pallas kernels: 3.09 us -> 1.65 us  [put(): pl.pallas_call(functools.partial(put_body, heads), grid_spec=pltpu.Prefet...]
  transfers between devices with their start and end apart: 11 -> 11, of which waited for: 1 -> 2; matrix products, arithmetic and copies ran while one was open for 2% -> 1% of each run, Pallas kernels for 11% -> 12%
where the time goes in v4:
time: 137 us; the launch traced here: 136 us
  blocking collectives  54.4 us (40%)
  starting transfers between devices  39.3 us (29%)
  Pallas kernels  20.9 us (15%)
  waiting for transfers between devices  17.5 us (13%)
  between operations  2.13 us (2%)
  local copies, waits for them, and re-layouts  1.5 us (1%)
    all_gather x1, blocking collectives, shards(): prompt = lax.all_gather(jnp.concatenate([piece, scalars], 0), 'slot')  39.6 us
    ppermute x8, starting transfers between devices, turned(): return lax.ppermute(part, 'ctx', rings[turn])  25.6 us
    all_to_all x1, waiting for transfers between devices, shards(): lax.all_to_all(out[4].reshape(slots, rows, lane), 'slot', 0, 0, tiled=True)  15.3 us
    psum x1, blocking collectives, shards(): slot_tokens = jnp.full((1, lane), lax.psum(length.astype(f32), 'group'))  14.8 us
    pallas_call x2, Pallas kernels, main(): pl.pallas_call(functools.partial(main_body, start, heads, scale, len(so_f...  11.7 us
    pallas_call x2, Pallas kernels, pack(): pl.pallas_call(functools.partial(body, heads), grid=((early + late) // he...  7.51 us
    all_to_all x1, starting transfers between devices, shards(): lax.all_to_all(out[4].reshape(slots, rows, lane), 'slot', 0, 0, tiled=True)  6.86 us
    ppermute x1, starting transfers between devices, shards(): piece = lax.ppermute(prompt_state[0], ('slot', 'ctx'), moves)  4.09 us
  transfers between devices with their start and end apart: 11, of which 2 were waited for; matrix products, arithmetic and copies ran while one was open for 1% of the time, Pallas kernels for 12%

profile of v4, /device:TPU:6, one launch (start us, length us, event | category | flops | bytes accessed | tf_op | source)
XLA Modules:
  0.0 136.0 jit_solution(6019992980941942027)
XLA Ops:
  0.6 4.1 %collective-permute-start = (f32[64,128]{1,0:T(8,128)}, f32[64,128]{1,0:T(8,128)S(1)}, u32[]{:S(2)}, u32[]{:S(2)}) collective-permute-start(f32[64,128]{1,0:T(8,128)} %bitcast.45), channel_id=1, source_target_pairs={{0,0},{4,1},{2,2},{6,3},{1,4},{5,5},{3,6},{7,7},{8,8},{12,9},{10,1... | collective-permute-start | bytes 98312 | tf_op jit(solution)/shard_map/ppermute | solution.py:266
  4.7 2.9 %shard_map.86 = f32[3,8,128,128]{3,2,1,0:T(8,128)} custom-call(bf16[128,4096]{1,0:T(8,128)(2,1)} %bitcast.20, bf16[128,4096]{1,0:T(8,128)(2,1)} %bitcast.26, bf16[128,4096]{1,0:T(8,128)(2,1)} %bitcast.32), custom_call_target="tpu_custom_call" | custom-call | bytes 6291456 | tf_op jit(solution)/shard_map/pallas_call | solution.py:68
  7.6 0.0 copy-start
  7.6 0.0 copy-start.1
  7.6 0.0 copy-start.2
  7.6 0.0 copy-start.4
  7.6 0.0 collective-permute-done
  7.6 3.4 %collective-permute-start.2 = (f32[3,8,128,128]{3,2,1,0:T(8,128)}, f32[3,8,128,128]{3,2,1,0:T(8,128)}, u32[]{:S(2)}, u32[]{:S(2)}) collective-permute-start(f32[3,8,128,128]{3,2,1,0:T(8,128)} %shard_map.86), channel_id=1, source_target_pairs={{0,2},{1,3},{2,0},{3,1},{4,6},{5,7},{6,4},{7,5},{8,10},{9,11},{10,... | collective-permute-start | bytes 4718600 | tf_op jit(solution)/shard_map/ppermute | solution.py:270
  11.0 4.7 %shard_map.87 = (f32[3,6,128,128]{3,2,1,0:T(8,128)}, f32[3,6,128,128]{3,2,1,0:T(8,128)}, f32[3,2,128,128]{3,2,1,0:T(8,128)}, f32[3,2,128,128]{3,2,1,0:T(8,128)}) custom-call(bf16[128,4096]{1,0:T(8,128)(2,1)} %bitcast.21, bf16[128,4096]{1,0:T(8,128)(2,1)} %bitcast.27, bf16[128,4096]{1,0:T(8,128)(2,1)} %bitcast.33), custom_call_target="tpu_custom_call" | custom-call | bytes 6291456 | tf_op jit(solution)/shard_map/pallas_call | solution.py:68
  15.6 3.9 %collective-permute-start.4 = (f32[3,6,128,128]{3,2,1,0:T(8,128)}, f32[3,6,128,128]{3,2,1,0:T(8,128)}, u32[]{:S(2)}, u32[]{:S(2)}) collective-permute-start(f32[3,6,128,128]{3,2,1,0:T(8,128)} %get-tuple-element.32), channel_id=1, source_target_pairs={{0,1},{1,2},{2,3},{3,0},{4,5},{5,6},{6,7},{7,4},{8,9},{9,10},{10,1... | collective-permute-start | bytes 3538952 | tf_op jit(solution)/shard_map/ppermute | solution.py:270
  19.5 2.8 %collective-permute-start.5 = (f32[3,6,128,128]{3,2,1,0:T(8,128)}, f32[3,6,128,128]{3,2,1,0:T(8,128)}, u32[]{:S(2)}, u32[]{:S(2)}) collective-permute-start(f32[3,6,128,128]{3,2,1,0:T(8,128)} %get-tuple-element.33), channel_id=1, source_target_pairs={{0,3},{1,0},{2,1},{3,2},{4,7},{5,4},{6,5},{7,6},{8,11},{9,8},{10,9... | collective-permute-start | bytes 3538952 | tf_op jit(solution)/shard_map/ppermute | solution.py:270
  22.9 14.8 %psum.7 = f32[]{:T(128)} all-reduce(f32[]{:T(128)} %bitcast.7), channel_id=1, replica_groups=mesh['group'=8,'slot'=16,'ctx'=4] {'group'}, use_global_device_ids=true, to_apply=%region_0.0 | all-reduce | flops 1 | bytes 8 | tf_op jit(solution)/shard_map/psum | solution.py:277
  38.4 0.7 pad.1.clone
  39.1 0.1 pad.2.clone
  39.2 0.1 pad.3.clone
  39.3 0.1 pad_add_fusion.place
  39.3 3.8 %collective-permute-start.1 = (f32[3,2,128,128]{3,2,1,0:T(8,128)}, f32[3,2,128,128]{3,2,1,0:T(8,128)S(1)}, u32[]{:S(2)}, u32[]{:S(2)}) collective-permute-start(f32[3,2,128,128]{3,2,1,0:T(8,128)} %get-tuple-element.28), channel_id=1, source_target_pairs={{0,1},{1,2},{2,3},{3,0},{4,5},{5,6},{6,7},{7,4},{8,9},{9,10},{10,1... | collective-permute-start | bytes 1179656 | tf_op jit(solution)/shard_map/ppermute | solution.py:270
  43.2 2.0 %collective-permute-start.3 = (f32[3,2,128,128]{3,2,1,0:T(8,128)}, f32[3,2,128,128]{3,2,1,0:T(8,128)S(1)}, u32[]{:S(2)}, u32[]{:S(2)}) collective-permute-start(f32[3,2,128,128]{3,2,1,0:T(8,128)} %get-tuple-element.30), channel_id=1, source_target_pairs={{0,3},{1,0},{2,1},{3,2},{4,7},{5,4},{6,5},{7,6},{8,11},{9,8},{10,9... | collective-permute-start | bytes 1179656 | tf_op jit(solution)/shard_map/ppermute | solution.py:270
  45.2 0.1 maximum_maximum_fusion
  45.3 39.6 %all-gather = f32[1152,128]{1,0:T(8,128)S(1)} all-gather(f32[72,128]{1,0:T(8,128)S(1)} %maximum_maximum_fusion), channel_id=2, replica_groups=mesh['group'=8,'slot'=16,'ctx'=4] {'slot'}, dimensions={0}, use_global_device_ids=true | all-gather | bytes 626688 | tf_op jit(solution)/shard_map/all_gather | solution.py:281
  84.9 0.0 collective-permute-done.4.refs_6_
  84.9 0.0 collective-permute-done.5.refs_8_
  84.9 0.0 collective-permute-done.2.refs_7_
  84.9 0.0 copy-done
  84.9 0.0 copy-done.1
  84.9 0.0 copy-done.2
  84.9 0.0 copy-done.4
  84.9 7.7 %shard_map.88 = (f32[8,128,128]{2,1,0:T(8,128)}, f32[8,128,128]{2,1,0:T(8,128)}, f32[8,128,128]{2,1,0:T(8,128)}, f32[8,128,128]{2,1,0:T(8,128)}, f32[8,128,128]{2,1,0:T(8,128)}) custom-call(s32[2]{0:T(128)S(1)} %pad_add_fusion.place, f32[32]{0:T(128)S(1)} %copy-done.4, f32[1]{0:T(128)} %bitcast.17.reward, bf16[128,4096]{1,0:T(8,128)(2,1)S(1)} %bitcast.22, ...), custom_call_target="tpu_custom_call" | custom-call | flops 1509949440 | bytes 7864320 | tf_op jit(solution)/shard_map/pallas_call | solution.py:207
  92.6 0.0 collective-permute-done.1.refs_6_
  92.6 0.0 collective-permute-done.3.refs_8_
  92.7 4.0 %shard_map.89 = (f32[8,128,128]{2,1,0:T(8,128)}, f32[8,128,128]{2,1,0:T(8,128)}, f32[8,128,128]{2,1,0:T(8,128)}, f32[8,128,128]{2,1,0:T(8,128)}, f32[8,128,128]{2,1,0:T(8,128)}) custom-call(s32[2]{0:T(128)S(1)} %pad_add_fusion.place, f32[32]{0:T(128)S(1)} %copy-done.4, ...), custom_call_target="tpu_custom_call", output_to_operand_aliasing={{0}: (14, {}), {1}: (15, {}), {2}: (16, {}), {3}: (17, {}),... | custom-call | flops 503316480 | bytes 2621440 | tf_op jit(solution)/shard_map/pallas_call | solution.py:207
  96.7 0.0 copy-start.3
  96.7 6.9 %all-to-all-start = ((f32[16,64,128]{2,1,0:T(8,128)}), f32[16,64,128]{2,1,0:T(8,128)S(1)}, u32[]{:S(2)}, u32[]{:S(2)}) async-start(f32[16,64,128]{2,1,0:T(8,128)} %bitcast.42), calls=%async_computation | async-start | bytes 1048576 | tf_op jit(solution)/shard_map/all_to_all | solution.py:291
  103.5 5.1 %collective-permute-start.6 = (f32[8,128,128]{2,1,0:T(8,128)}, f32[8,128,128]{2,1,0:T(8,128)S(1)}, u32[]{:S(2)}, u32[]{:S(2)}) collective-permute-start(f32[8,128,128]{2,1,0:T(8,128)} %get-tuple-element.40), channel_id=1, source_target_pairs={{0,1},{1,2},{2,3},{3,0},{4,5},{5,6},{6,7},{7,4},{8,9},{9,10},{10,1... | collective-permute-start | bytes 1572872 | tf_op jit(solution)/shard_map/ppermute | solution.py:270
  108.6 1.9 %collective-permute-start.7 = (f32[8,128,128]{2,1,0:T(8,128)}, f32[8,128,128]{2,1,0:T(8,128)S(1)}, u32[]{:S(2)}, u32[]{:S(2)}) collective-permute-start(f32[8,128,128]{2,1,0:T(8,128)} %get-tuple-element.41), channel_id=1, source_target_pairs={{0,2},{1,3},{2,0},{3,1},{4,6},{5,7},{6,4},{7,5},{8,10},{9,11},{10,... | collective-permute-start | bytes 1572872 | tf_op jit(solution)/shard_map/ppermute | solution.py:270
  110.5 2.8 %collective-permute-start.8 = (f32[8,128,128]{2,1,0:T(8,128)}, f32[8,128,128]{2,1,0:T(8,128)S(1)}, u32[]{:S(2)}, u32[]{:S(2)}) collective-permute-start(f32[8,128,128]{2,1,0:T(8,128)} %get-tuple-element.42), channel_id=1, source_target_pairs={{0,3},{1,0},{2,1},{3,2},{4,7},{5,4},{6,5},{7,6},{8,11},{9,8},{10,9... | collective-permute-start | bytes 1572872 | tf_op jit(solution)/shard_map/ppermute | solution.py:270
  113.3 15.3 %all-to-all-done = f32[16,64,128]{2,1,0:T(8,128)S(1)} async-done(((f32[16,64,128]{2,1,0:T(8,128)}), f32[16,64,128]{2,1,0:T(8,128)S(1)}, u32[]{:S(2)}, u32[]{:S(2)}) %all-to-all-start) | async-done | bytes 524320 | tf_op jit(solution)/shard_map/all_to_all | solution.py:291
  128.6 2.8 %collective-permute-start.9 = (f32[1,64,128]{2,1,0:T(8,128)S(1)}, f32[1,64,128]{2,1,0:T(8,128)S(1)}, u32[]{:S(2)}, u32[]{:S(2)}) collective-permute-start(f32[1,64,128]{2,1,0:T(8,128)S(1)} %bitcast.44), channel_id=1, source_target_pairs={{0,0},{1,4},{2,2},{3,6},{4,1},{5,5},{6,3},{7,7},{8,8},{9,12},{10,1... | collective-permute-start | bytes 98312 | tf_op jit(solution)/shard_map/ppermute | solution.py:293
  131.4 0.0 collective-permute-done.6.refs_1_
  131.4 0.0 collective-permute-done.7.refs_2_
  131.4 0.0 collective-permute-done.8.refs_3_
  131.4 0.0 copy-done.3
  131.5 1.7 %shard_map.90 = bf16[128,4096]{1,0:T(8,128)(2,1)} custom-call(s32[2]{0:T(128)S(1)} %pad_add_fusion.place, f32[8,128,128]{2,1,0:T(8,128)S(1)} %copy-done.3, f32[8,128,128]{2,1,0:T(8,128)S(1)} %collective-permute-done.6.refs_1_, f32[8,128,128]{2,1,0:T(8,128)S(1)} %collective-permute-done.7.refs_2_, f32[8,128,128]{2,1,0:T(8,128)S(1)} %collective-permute-done.8.refs_3_), custom_call_target="tpu_custom_call" | custom-call | bytes 3145728 | tf_op jit(solution)/shard_map/pallas_call | solution.py:238
  133.1 2.2 %collective-permute-done.9 = f32[1,64,128]{2,1,0:T(8,128)S(1)} collective-permute-done((f32[1,64,128]{2,1,0:T(8,128)S(1)}, f32[1,64,128]{2,1,0:T(8,128)S(1)}, u32[]{:S(2)}, u32[]{:S(2)}) %collective-permute-start.9) | collective-permute-done | bytes 32800 | tf_op jit(solution)/shard_map/ppermute | solution.py:293
  135.3 0.6 copy.22
  (2 shorter events, 0.0 us)
Async XLA Ops:
  0.6 7.0 %collective-permute-start = (f32[64,128]{1,0:T(8,128)}, f32[64,128]{1,0:T(8,128)S(1)}, u32[]{:S(2)}, u32[]{:S(2)}) collective-permute-start(f32[64,128]{1,0:T(8,128)} %bitcast.45), channel_id=1, source_target_pairs={{0,0},{4,1},{2,2},{6,3},{1,4},{5,5},{3,6},{7,7},{8,8},{12,9},{10,1... | collective-permute-start | bytes 98312 | tf_op jit(solution)/shard_map/ppermute | solution.py:266
  7.6 77.3 %copy-start = (bf16[1,1,128,4096]{3,2,1,0:T(8,128)(2,1)S(1)}, bf16[1,1,128,4096]{3,2,1,0:T(8,128)(2,1)}, u32[]{:S(2)}) copy-start(bf16[1,1,128,4096]{3,2,1,0:T(8,128)(2,1)} %param.7) | copy-start | bytes 3145732
  7.6 77.3 %copy-start.1 = (bf16[1,1,128,4096]{3,2,1,0:T(8,128)(2,1)S(1)}, bf16[1,1,128,4096]{3,2,1,0:T(8,128)(2,1)}, u32[]{:S(2)}) copy-start(bf16[1,1,128,4096]{3,2,1,0:T(8,128)(2,1)} %param.8) | copy-start | bytes 3145732
  7.6 77.3 %copy-start.2 = (bf16[1,1,128,4096]{3,2,1,0:T(8,128)(2,1)S(1)}, bf16[1,1,128,4096]{3,2,1,0:T(8,128)(2,1)}, u32[]{:S(2)}) copy-start(bf16[1,1,128,4096]{3,2,1,0:T(8,128)(2,1)} %param.9) | copy-start | bytes 3145732
  7.6 77.3 %copy-start.4 = (f32[32]{0:T(128)S(1)}, f32[32]{0:T(128)}, u32[]{:S(2)}) copy-start(f32[32]{0:T(128)} %rates.3) | copy-start | bytes 388
  7.6 77.3 %collective-permute-start.2 = (f32[3,8,128,128]{3,2,1,0:T(8,128)}, f32[3,8,128,128]{3,2,1,0:T(8,128)}, u32[]{:S(2)}, u32[]{:S(2)}) collective-permute-start(f32[3,8,128,128]{3,2,1,0:T(8,128)} %shard_map.86), channel_id=1, source_target_pairs={{0,2},{1,3},{2,0},{3,1},{4,6},{5,7},{6,4},{7,5},{8,10},{9,11},{10,... | collective-permute-start | bytes 4718600 | tf_op jit(solution)/shard_map/ppermute | solution.py:270
  15.6 69.2 %collective-permute-start.4 = (f32[3,6,128,128]{3,2,1,0:T(8,128)}, f32[3,6,128,128]{3,2,1,0:T(8,128)}, u32[]{:S(2)}, u32[]{:S(2)}) collective-permute-start(f32[3,6,128,128]{3,2,1,0:T(8,128)} %get-tuple-element.32), channel_id=1, source_target_pairs={{0,1},{1,2},{2,3},{3,0},{4,5},{5,6},{6,7},{7,4},{8,9},{9,10},{10,1... | collective-permute-start | bytes 3538952 | tf_op jit(solution)/shard_map/ppermute | solution.py:270
  19.5 65.4 %collective-permute-start.5 = (f32[3,6,128,128]{3,2,1,0:T(8,128)}, f32[3,6,128,128]{3,2,1,0:T(8,128)}, u32[]{:S(2)}, u32[]{:S(2)}) collective-permute-start(f32[3,6,128,128]{3,2,1,0:T(8,128)} %get-tuple-element.33), channel_id=1, source_target_pairs={{0,3},{1,0},{2,1},{3,2},{4,7},{5,4},{6,5},{7,6},{8,11},{9,8},{10,9... | collective-permute-start | bytes 3538952 | tf_op jit(solution)/shard_map/ppermute | solution.py:270
  39.3 53.3 %collective-permute-start.1 = (f32[3,2,128,128]{3,2,1,0:T(8,128)}, f32[3,2,128,128]{3,2,1,0:T(8,128)S(1)}, u32[]{:S(2)}, u32[]{:S(2)}) collective-permute-start(f32[3,2,128,128]{3,2,1,0:T(8,128)} %get-tuple-element.28), channel_id=1, source_target_pairs={{0,1},{1,2},{2,3},{3,0},{4,5},{5,6},{6,7},{7,4},{8,9},{9,10},{10,1... | collective-permute-start | bytes 1179656 | tf_op jit(solution)/shard_map/ppermute | solution.py:270
  43.2 49.5 %collective-permute-start.3 = (f32[3,2,128,128]{3,2,1,0:T(8,128)}, f32[3,2,128,128]{3,2,1,0:T(8,128)S(1)}, u32[]{:S(2)}, u32[]{:S(2)}) collective-permute-start(f32[3,2,128,128]{3,2,1,0:T(8,128)} %get-tuple-element.30), channel_id=1, source_target_pairs={{0,3},{1,0},{2,1},{3,2},{4,7},{5,4},{6,5},{7,6},{8,11},{9,8},{10,9... | collective-permute-start | bytes 1179656 | tf_op jit(solution)/shard_map/ppermute | solution.py:270
  96.7 34.8 %copy-start.3 = (f32[8,128,128]{2,1,0:T(8,128)S(1)}, f32[8,128,128]{2,1,0:T(8,128)}, u32[]{:S(2)}) copy-start(f32[8,128,128]{2,1,0:T(8,128)} %get-tuple-element.39.refs_0_) | copy-start | bytes 1572868
  96.7 31.9 %all-to-all-start = ((f32[16,64,128]{2,1,0:T(8,128)}), f32[16,64,128]{2,1,0:T(8,128)S(1)}, u32[]{:S(2)}, u32[]{:S(2)}) async-start(f32[16,64,128]{2,1,0:T(8,128)} %bitcast.42), calls=%async_computation | async-start | bytes 1048576 | tf_op jit(solution)/shard_map/all_to_all | solution.py:291
  103.5 27.9 %collective-permute-start.6 = (f32[8,128,128]{2,1,0:T(8,128)}, f32[8,128,128]{2,1,0:T(8,128)S(1)}, u32[]{:S(2)}, u32[]{:S(2)}) collective-permute-start(f32[8,128,128]{2,1,0:T(8,128)} %get-tuple-element.40), channel_id=1, source_target_pairs={{0,1},{1,2},{2,3},{3,0},{4,5},{5,6},{6,7},{7,4},{8,9},{9,10},{10,1... | collective-permute-start | bytes 1572872 | tf_op jit(solution)/shard_map/ppermute | solution.py:270
  108.6 22.8 %collective-permute-start.7 = (f32[8,128,128]{2,1,0:T(8,128)}, f32[8,128,128]{2,1,0:T(8,128)S(1)}, u32[]{:S(2)}, u32[]{:S(2)}) collective-permute-start(f32[8,128,128]{2,1,0:T(8,128)} %get-tuple-element.41), channel_id=1, source_target_pairs={{0,2},{1,3},{2,0},{3,1},{4,6},{5,7},{6,4},{7,5},{8,10},{9,11},{10,... | collective-permute-start | bytes 1572872 | tf_op jit(solution)/shard_map/ppermute | solution.py:270
  110.5 20.9 %collective-permute-start.8 = (f32[8,128,128]{2,1,0:T(8,128)}, f32[8,128,128]{2,1,0:T(8,128)S(1)}, u32[]{:S(2)}, u32[]{:S(2)}) collective-permute-start(f32[8,128,128]{2,1,0:T(8,128)} %get-tuple-element.42), channel_id=1, source_target_pairs={{0,3},{1,0},{2,1},{3,2},{4,7},{5,4},{6,5},{7,6},{8,11},{9,8},{10,9... | collective-permute-start | bytes 1572872 | tf_op jit(solution)/shard_map/ppermute | solution.py:270
  128.6 6.7 %collective-permute-start.9 = (f32[1,64,128]{2,1,0:T(8,128)S(1)}, f32[1,64,128]{2,1,0:T(8,128)S(1)}, u32[]{:S(2)}, u32[]{:S(2)}) collective-permute-start(f32[1,64,128]{2,1,0:T(8,128)S(1)} %bitcast.44), channel_id=1, source_target_pairs={{0,0},{1,4},{2,2},{3,6},{4,1},{5,5},{6,3},{7,7},{8,8},{9,12},{10,1... | collective-permute-start | bytes 98312 | tf_op jit(solution)/shard_map/ppermute | solution.py:293

commit v5 on v4

--- a/solution.py
+++ b/solution.py
@@ -28,53 +28,64 @@
     return 2 * lax.rem(device, 2) + lax.div(device, 2)
 
 
-def widen(turn, sources, send, heads):
-    owner = residue(lax.rem(lax.axis_index("ctx") + turn, 4))
-    for which in range(3):
-        for step in range(heads):
-            column = pl.multiple_of((owner + 4 * step) * lane, lane)
-            send[which, step] = sources[which][:, pl.ds(column, lane)].astype(f32)
-
-
-def across_body(heads, *refs):
-    widen(2, refs[:3], refs[3], heads)
-
-
-def beside_body(heads, *refs):
-    sources, soon, later = refs[:3], refs[3:5], refs[5:7]
-    turns = early // heads
+def widen(sources, send):
+    for n, source in enumerate(sources):
+        send[n % 3, n // 3] = source[...].astype(f32)
+
+
+def across_body(me, *refs):
+    widen(refs[:-1], refs[-1])
+
+
+def beside_body(me, *refs):
+    blocks = len(refs[:-4]) // 2
+    right, left, soon, later = refs[:blocks], refs[blocks:-4], refs[-4:-2], refs[-2:]
+    turns = early // (blocks // 3)
 
     @pl.when(pl.program_id(0) < turns)
     def _():
-        widen(1, sources, soon[0], heads)
-        widen(3, sources, soon[1], heads)
+        widen(right, soon[0])
+        widen(left, soon[1])
 
     @pl.when(pl.program_id(0) >= turns)
     def _():
-        widen(1, sources, later[0], heads)
-        widen(3, sources, later[1], heads)
-
-
-def pack(arrays, block_len, beside, heads):
+        widen(right, later[0])
+        widen(left, later[1])
+
+
+def pack(me, arrays, block_len, beside, heads):
     turns = early // heads
     block = (3, heads, block_len, lane)
+
+    def column(turn, step):
+        return lambda m, me: (0, residue(lax.rem(me[0] + turn, 4)) + 4 * (m * heads + step))
+
     if beside:
-        soon = pl.BlockSpec(block, lambda m: (0, lax.min(m, turns - 1), 0, 0))
-        later = pl.BlockSpec(block, lambda m: (0, lax.max(m - turns, 0), 0, 0))
+        soon = pl.BlockSpec(block, lambda m, me: (0, lax.min(m, turns - 1), 0, 0))
+        later = pl.BlockSpec(block, lambda m, me: (0, lax.max(m - turns, 0), 0, 0))
         specs, counts, body = [soon, soon, later, later], (early, early, late, late), beside_body
     else:
-        specs, counts = [pl.BlockSpec(block, lambda m: (0, m, 0, 0))], (early + late,)
+        specs, counts = [pl.BlockSpec(block, lambda m, me: (0, m, 0, 0))], (early + late,)
         body = across_body
+    in_specs = [
+        pl.BlockSpec((block_len, lane), column(turn, step))
+        for turn in ((1, 3) if beside else (2,))
+        for step in range(heads)
+        for _ in arrays
+    ]
     return pl.pallas_call(
-        functools.partial(body, heads),
-        grid=((early + late) // heads,),
-        in_specs=[pl.BlockSpec((block_len, 4 * heads * lane), lambda m: (0, m))] * 3,
-        out_specs=specs,
+        body,
+        grid_spec=pltpu.PrefetchScalarGridSpec(
+            num_scalar_prefetch=1,
+            grid=((early + late) // heads,),
+            in_specs=in_specs,
+            out_specs=specs,
+        ),
         out_shape=[jax.ShapeDtypeStruct((3, count, block_len, lane), f32) for count in counts],
         cost_estimate=pl.CostEstimate(
             flops=0, bytes_accessed=48 * (early + late) * block_len * lane, transcendentals=0
         ),
-    )(*arrays)
+    )(me, *(list(arrays) * (len(in_specs) // 3)))
 
 
 def head_grads(rates, factor, length, rows, states):
@@ -269,14 +280,17 @@
     def turned(part, turn):
         return lax.ppermute(part, "ctx", rings[turn])
 
-    piece, (wide,) = lax.optimization_barrier((piece, pack(arrays, block_len, False, 4)))
+    (wide,) = pack(ctx_index.reshape(1), arrays, block_len, False, 4)
     across = turned(wide, 2)
-    piece, sends = lax.optimization_barrier((piece, pack(arrays, block_len, True, 2)))
+    tokens = jnp.full((1, lane), length.astype(f32))
+    piece, sends, tokens = lax.optimization_barrier((piece, pack(ctx_index.reshape(1), arrays, block_len, True, 2), tokens))
     moved = [(turned(sends[n], 1), across, turned(sends[n + 1], 3)) for n in (0, 2)]
 
-    slot_tokens = jnp.full((1, lane), lax.psum(length.astype(f32), "group"))
+    groups = lax.axis_size("group")
+    for step in (1, 2, 4):
+        tokens = tokens + lax.ppermute(tokens, "group", [(i, i ^ step) for i in range(groups)])
     scalars = jnp.concatenate(
-        [slot_tokens, jnp.full((1, lane), reward), jnp.zeros((6, lane), f32)], 0
+        [tokens, jnp.full((1, lane), reward), jnp.zeros((6, lane), f32)], 0
     )
     prompt = lax.all_gather(jnp.concatenate([piece, scalars], 0), "slot")
     rows, slots = piece.shape[0], lax.axis_size("slot")

time: 137 us -> 133 us (0.971)
  blocking collectives: 54.4 us -> 39.4 us
  starting transfers between devices: 39.3 us -> 49.3 us
  waiting for transfers between devices: 17.5 us -> 20.4 us
    psum x1 -> x0, blocking collectives: 14.8 us -> none  [shards(): slot_tokens = jnp.full((1, lane), lax.psum(length.astype(f32), 'group'))]
    ppermute x0 -> x3, starting transfers between devices: none -> 8.96 us  [shards(): lax.ppermute(tokens, 'group', [(i, i ^ step) for i in range(groups)])]
    ppermute x0 -> x3, waiting for transfers between devices: none -> 3.71 us  [shards(): lax.ppermute(tokens, 'group', [(i, i ^ step) for i in range(groups)])]
    ppermute x1, starting transfers between devices: 2.78 us -> 4.55 us  [shards(): lax.ppermute(summed, ('slot', 'ctx'), [(there, home) for home, there in m...]
    ppermute x1, waiting for transfers between devices: 2.23 us -> 0.46 us  [shards(): lax.ppermute(summed, ('slot', 'ctx'), [(there, home) for home, there in m...]
  transfers between devices with their start and end apart: 11 -> 14, of which waited for: 2 -> 4; matrix products, arithmetic and copies ran while one was open for 1% -> 0% of each run, Pallas kernels for 12% -> 10%
where the time goes in v5:
time: 133 us; the launch traced here: 132 us
  starting transfers between devices  49.3 us (37%)
  blocking collectives  39.4 us (30%)
  waiting for transfers between devices  20.4 us (15%)
  Pallas kernels  19.8 us (15%)
  between operations  2.21 us (2%)
    all_gather x1, blocking collectives, shards(): prompt = lax.all_gather(jnp.concatenate([piece, scalars], 0), 'slot')  39.4 us
    ppermute x8, starting transfers between devices, turned(): return lax.ppermute(part, 'ctx', rings[turn])  25.5 us
    all_to_all x1, waiting for transfers between devices, shards(): lax.all_to_all(out[4].reshape(slots, rows, lane), 'slot', 0, 0, tiled=True)  16.2 us
    pallas_call x2, Pallas kernels, main(): pl.pallas_call(functools.partial(main_body, start, heads, scale, len(so_f...  11.5 us
    ppermute x3, starting transfers between devices, shards(): lax.ppermute(tokens, 'group', [(i, i ^ step) for i in range(groups)])  8.96 us
    all_to_all x1, starting transfers between devices, shards(): lax.all_to_all(out[4].reshape(slots, rows, lane), 'slot', 0, 0, tiled=True)  7.08 us
    pallas_call x2, Pallas kernels, pack(): pl.pallas_call(body, grid_spec=pltpu.PrefetchScalarGridSpec(num_scalar_pr...  6.66 us
    ppermute x1, starting transfers between devices, shards(): lax.ppermute(summed, ('slot', 'ctx'), [(there, home) for home, there in m...  4.55 us
  transfers between devices with their start and end apart: 14, of which 4 were waited for; matrix products, arithmetic and copies ran while one was open for 0% of the time, Pallas kernels for 10%

profile of v5, /device:TPU:6, one launch (start us, length us, event | category | flops | bytes accessed | tf_op | source)
XLA Modules:
  0.0 132.1 jit_solution(15977280185786048822)
XLA Ops:
  0.6 0.0 copy-start.5
  0.6 2.3 %shard_map.87 = f32[3,8,128,128]{3,2,1,0:T(8,128)} custom-call(s32[1]{0:T(128)} %bitcast.me, bf16[128,4096]{1,0:T(8,128)(2,1)} %bitcast.19, bf16[128,4096]{1,0:T(8,128)(2,1)} %bitcast.31, bf16[128,4096]{1,0:T(8,128)(2,1)} %bitcast.43, bf16[128,4096]{1,0:T(8,128)(2,1)} %bitcast.20, bf16[128,4096]{1,0:T(8,128)(2,1)} %bitcast.32, bf16[128,4096]{1,0:T(8,128)(2,1)} %bitcast.44, ...), custom_call_target="tpu_custom_call" | custom-call | bytes 6291456 | tf_op jit(solution)/shard_map/pallas_call | solution.py:76
  2.9 3.3 %collective-permute-start.2 = (f32[3,8,128,128]{3,2,1,0:T(8,128)}, f32[3,8,128,128]{3,2,1,0:T(8,128)}, u32[]{:S(2)}, u32[]{:S(2)}) collective-permute-start(f32[3,8,128,128]{3,2,1,0:T(8,128)} %shard_map.87), channel_id=1, source_target_pairs={{0,2},{1,3},{2,0},{3,1},{4,6},{5,7},{6,4},{7,5},{8,10},{9,11},{10,... | collective-permute-start | bytes 4718600 | tf_op jit(solution)/shard_map/ppermute | solution.py:281
  6.2 0.0 copy-done.5
  6.3 0.0 copy-start.4
  6.3 3.2 %collective-permute-start = (f32[64,128]{1,0:T(8,128)S(1)}, f32[64,128]{1,0:T(8,128)S(1)}, u32[]{:S(2)}, u32[]{:S(2)}) collective-permute-start(f32[64,128]{1,0:T(8,128)S(1)} %bitcast.62), channel_id=1, source_target_pairs={{0,0},{4,1},{2,2},{6,3},{1,4},{5,5},{3,6},{7,7},{8,8},{12,9},{10,1... | collective-permute-start | bytes 98312 | tf_op jit(solution)/shard_map/ppermute | solution.py:277
  9.5 0.0 copy-start
  9.5 0.0 copy-start.1
  9.5 0.0 copy-start.2
  9.5 4.4 %shard_map.86 = (f32[3,6,128,128]{3,2,1,0:T(8,128)}, f32[3,6,128,128]{3,2,1,0:T(8,128)}, f32[3,2,128,128]{3,2,1,0:T(8,128)}, f32[3,2,128,128]{3,2,1,0:T(8,128)}) custom-call(s32[1]{0:T(128)} %bitcast.me, bf16[128,4096]{1,0:T(8,128)(2,1)} %bitcast.23, bf16[128,4096]{1,0:T(8,128)(2,1)} %bitcast.35, bf16[128,4096]{1,0:T(8,128)(2,1)} %bitcast.47, ...), custom_call_target="tpu_custom_call" | custom-call | bytes 6291456 | tf_op jit(solution)/shard_map/pallas_call | solution.py:76
  14.5 0.0 collective-permute-done
  14.6 3.8 %collective-permute-start.7 = (f32[3,6,128,128]{3,2,1,0:T(8,128)}, f32[3,6,128,128]{3,2,1,0:T(8,128)S(1)}, u32[]{:S(2)}, u32[]{:S(2)}) collective-permute-start(f32[3,6,128,128]{3,2,1,0:T(8,128)} %get-tuple-element.30), channel_id=1, source_target_pairs={{0,1},{1,2},{2,3},{3,0},{4,5},{5,6},{6,7},{7,4},{8,9},{9,10},{10,1... | collective-permute-start | bytes 3538952 | tf_op jit(solution)/shard_map/ppermute | solution.py:281
  18.4 2.8 %collective-permute-start.8 = (f32[3,6,128,128]{3,2,1,0:T(8,128)}, f32[3,6,128,128]{3,2,1,0:T(8,128)S(1)}, u32[]{:S(2)}, u32[]{:S(2)}) collective-permute-start(f32[3,6,128,128]{3,2,1,0:T(8,128)} %get-tuple-element.31), channel_id=1, source_target_pairs={{0,3},{1,0},{2,1},{3,2},{4,7},{5,4},{6,5},{7,6},{8,11},{9,8},{10,9... | collective-permute-start | bytes 3538952 | tf_op jit(solution)/shard_map/ppermute | solution.py:281
  21.2 1.9 %collective-permute-start.4 = (f32[1,128]{1,0:T(1,128)S(1)}, f32[1,128]{1,0:T(1,128)S(1)}, u32[]{:S(2)}, u32[]{:S(2)}) collective-permute-start(f32[1,128]{1,0:T(1,128)S(1)} %broadcast_in_dim.12), channel_id=1, source_target_pairs={{0,64},{64,0},{128,192},{192,128},{256,320},{320,256},{384,448},{4... | collective-permute-start | bytes 1544 | tf_op jit(solution)/shard_map/ppermute | solution.py:291
  23.1 1.1 collective-permute-done.4
  24.2 2.7 %collective-permute-start.5 = (f32[1,128]{1,0:T(1,128)S(1)}, f32[1,128]{1,0:T(1,128)S(1)}, u32[]{:S(2)}, u32[]{:S(2)}) collective-permute-start(f32[1,128]{1,0:T(1,128)S(1)} %add.9), channel_id=1, source_target_pairs={{0,128},{64,192},{128,0},{192,64},{256,384},{320,448},{384,256},{4... | collective-permute-start | bytes 1544 | tf_op jit(solution)/shard_map/ppermute | solution.py:291
  26.9 0.1 pad_add_fusion.place
  27.0 2.6 %collective-permute-done.5 = f32[1,128]{1,0:T(1,128)S(1)} collective-permute-done((f32[1,128]{1,0:T(1,128)S(1)}, f32[1,128]{1,0:T(1,128)S(1)}, u32[]{:S(2)}, u32[]{:S(2)}) %collective-permute-start.5) | collective-permute-done | bytes 544 | tf_op jit(solution)/shard_map/ppermute | solution.py:291
  29.6 4.3 %collective-permute-start.6 = (f32[1,128]{1,0:T(1,128)S(1)}, f32[1,128]{1,0:T(1,128)S(1)}, u32[]{:S(2)}, u32[]{:S(2)}) collective-permute-start(f32[1,128]{1,0:T(1,128)S(1)} %add.10), channel_id=1, source_target_pairs={{0,256},{64,320},{128,384},{192,448},{256,0},{320,64},{384,128},{4... | collective-permute-start | bytes 1544 | tf_op jit(solution)/shard_map/ppermute | solution.py:291
  34.6 0.1 pad.2.clone
  34.7 0.1 pad.3.clone
  34.8 4.1 %collective-permute-start.1 = (f32[3,2,128,128]{3,2,1,0:T(8,128)}, f32[3,2,128,128]{3,2,1,0:T(8,128)S(1)}, u32[]{:S(2)}, u32[]{:S(2)}) collective-permute-start(f32[3,2,128,128]{3,2,1,0:T(8,128)} %get-tuple-element.26), channel_id=1, source_target_pairs={{0,1},{1,2},{2,3},{3,0},{4,5},{5,6},{6,7},{7,4},{8,9},{9,10},{10,1... | collective-permute-start | bytes 1179656 | tf_op jit(solution)/shard_map/ppermute | solution.py:281
  38.8 0.0 collective-permute-done.6
  38.9 1.9 %collective-permute-start.3 = (f32[3,2,128,128]{3,2,1,0:T(8,128)}, f32[3,2,128,128]{3,2,1,0:T(8,128)S(1)}, u32[]{:S(2)}, u32[]{:S(2)}) collective-permute-start(f32[3,2,128,128]{3,2,1,0:T(8,128)} %get-tuple-element.27), channel_id=1, source_target_pairs={{0,3},{1,0},{2,1},{3,2},{4,7},{5,4},{6,5},{7,6},{8,11},{9,8},{10,9... | collective-permute-start | bytes 1179656 | tf_op jit(solution)/shard_map/ppermute | solution.py:281
  40.8 0.1 maximum_maximum_fusion
  40.9 39.4 %all-gather = f32[1152,128]{1,0:T(8,128)S(1)} all-gather(f32[72,128]{1,0:T(8,128)S(1)} %maximum_maximum_fusion), channel_id=2, replica_groups=mesh['group'=8,'slot'=16,'ctx'=4] {'slot'}, dimensions={0}, use_global_device_ids=true | all-gather | bytes 626688 | tf_op jit(solution)/shard_map/all_gather | solution.py:295
  80.3 0.0 collective-permute-done.7.refs_6_
  80.3 0.0 collective-permute-done.8.refs_8_
  80.3 0.0 collective-permute-done.2.refs_7_
  80.3 0.0 copy-done.4
  80.3 0.0 copy-done
  80.3 0.0 copy-done.1
  80.3 0.0 copy-done.2
  80.4 7.5 %shard_map.88 = (f32[8,128,128]{2,1,0:T(8,128)}, f32[8,128,128]{2,1,0:T(8,128)}, f32[8,128,128]{2,1,0:T(8,128)}, f32[8,128,128]{2,1,0:T(8,128)}, f32[8,128,128]{2,1,0:T(8,128)}) custom-call(s32[2]{0:T(128)S(1)} %pad_add_fusion.place, f32[32]{0:T(128)S(1)} %copy-done.4, f32[1]{0:T(128)} %bitcast.16.reward, bf16[128,4096]{1,0:T(8,128)(2,1)S(1)} %bitcast.27, ...), custom_call_target="tpu_custom_call" | custom-call | flops 1509949440 | bytes 7864320 | tf_op jit(solution)/shard_map/pallas_call | solution.py:218
  87.9 0.0 collective-permute-done.1.refs_6_
  87.9 0.0 collective-permute-done.3.refs_8_
  87.9 4.0 %shard_map.89 = (f32[8,128,128]{2,1,0:T(8,128)}, f32[8,128,128]{2,1,0:T(8,128)}, f32[8,128,128]{2,1,0:T(8,128)}, f32[8,128,128]{2,1,0:T(8,128)}, f32[8,128,128]{2,1,0:T(8,128)}) custom-call(s32[2]{0:T(128)S(1)} %pad_add_fusion.place, f32[32]{0:T(128)S(1)} %copy-done.4, ...), custom_call_target="tpu_custom_call", output_to_operand_aliasing={{0}: (14, {}), {1}: (15, {}), {2}: (16, {}), {3}: (17, {}),... | custom-call | flops 503316480 | bytes 2621440 | tf_op jit(solution)/shard_map/pallas_call | solution.py:218
  91.9 0.0 copy-start.3
  91.9 7.1 %all-to-all-start = ((f32[16,64,128]{2,1,0:T(8,128)}), f32[16,64,128]{2,1,0:T(8,128)S(1)}, u32[]{:S(2)}, u32[]{:S(2)}) async-start(f32[16,64,128]{2,1,0:T(8,128)} %bitcast.59), calls=%async_computation | async-start | bytes 1048576 | tf_op jit(solution)/shard_map/all_to_all | solution.py:305
  99.0 4.9 %collective-permute-start.9 = (f32[8,128,128]{2,1,0:T(8,128)}, f32[8,128,128]{2,1,0:T(8,128)S(1)}, u32[]{:S(2)}, u32[]{:S(2)}) collective-permute-start(f32[8,128,128]{2,1,0:T(8,128)} %get-tuple-element.38), channel_id=1, source_target_pairs={{0,1},{1,2},{2,3},{3,0},{4,5},{5,6},{6,7},{7,4},{8,9},{9,10},{10,1... | collective-permute-start | bytes 1572872 | tf_op jit(solution)/shard_map/ppermute | solution.py:281
  103.9 1.9 %collective-permute-start.10 = (f32[8,128,128]{2,1,0:T(8,128)}, f32[8,128,128]{2,1,0:T(8,128)S(1)}, u32[]{:S(2)}, u32[]{:S(2)}) collective-permute-start(f32[8,128,128]{2,1,0:T(8,128)} %get-tuple-element.39), channel_id=1, source_target_pairs={{0,2},{1,3},{2,0},{3,1},{4,6},{5,7},{6,4},{7,5},{8,10},{9,11},{10,... | collective-permute-start | bytes 1572872 | tf_op jit(solution)/shard_map/ppermute | solution.py:281
  105.8 2.8 %collective-permute-start.11 = (f32[8,128,128]{2,1,0:T(8,128)}, f32[8,128,128]{2,1,0:T(8,128)S(1)}, u32[]{:S(2)}, u32[]{:S(2)}) collective-permute-start(f32[8,128,128]{2,1,0:T(8,128)} %get-tuple-element.40), channel_id=1, source_target_pairs={{0,3},{1,0},{2,1},{3,2},{4,7},{5,4},{6,5},{7,6},{8,11},{9,8},{10,9... | collective-permute-start | bytes 1572872 | tf_op jit(solution)/shard_map/ppermute | solution.py:281
  108.6 16.2 %all-to-all-done = f32[16,64,128]{2,1,0:T(8,128)S(1)} async-done(((f32[16,64,128]{2,1,0:T(8,128)}), f32[16,64,128]{2,1,0:T(8,128)S(1)}, u32[]{:S(2)}, u32[]{:S(2)}) %all-to-all-start) | async-done | bytes 524320 | tf_op jit(solution)/shard_map/all_to_all | solution.py:305
  124.8 4.5 %collective-permute-start.12 = (f32[1,64,128]{2,1,0:T(8,128)S(1)}, f32[1,64,128]{2,1,0:T(8,128)S(1)}, u32[]{:S(2)}, u32[]{:S(2)}) collective-permute-start(f32[1,64,128]{2,1,0:T(8,128)S(1)} %bitcast.61), channel_id=1, source_target_pairs={{0,0},{1,4},{2,2},{3,6},{4,1},{5,5},{6,3},{7,7},{8,8},{9,12},{10,1... | collective-permute-start | bytes 98312 | tf_op jit(solution)/shard_map/ppermute | solution.py:307
  129.3 0.0 collective-permute-done.9.refs_1_
  129.3 0.0 collective-permute-done.10.refs_2_
  129.3 0.0 collective-permute-done.11.refs_3_
  129.3 0.0 copy-done.3
  129.4 1.7 %shard_map.90 = bf16[128,4096]{1,0:T(8,128)(2,1)} custom-call(s32[2]{0:T(128)S(1)} %pad_add_fusion.place, f32[8,128,128]{2,1,0:T(8,128)S(1)} %copy-done.3, f32[8,128,128]{2,1,0:T(8,128)S(1)} %collective-permute-done.9.refs_1_, f32[8,128,128]{2,1,0:T(8,128)S(1)} %collective-permute-done.10.refs_2_, f32[8,128,128]{2,1,0:T(8,128)S(1)} %collective-permute-done.11.refs_3_), custom_call_target="tpu_custom_call" | custom-call | bytes 3145728 | tf_op jit(solution)/shard_map/pallas_call | solution.py:249
  131.0 0.5 collective-permute-done.12
  131.5 0.6 copy.22
  (6 shorter events, 0.0 us)
Async XLA Ops:
  0.6 5.6 %copy-start.5 = (f32[1,64,128]{2,1,0:T(8,128)S(1)}, f32[1,64,128]{2,1,0:T(8,128)}, u32[]{:S(2)}) copy-start(f32[1,64,128]{2,1,0:T(8,128)} %param.13) | copy-start | bytes 98308
  2.9 77.4 %collective-permute-start.2 = (f32[3,8,128,128]{3,2,1,0:T(8,128)}, f32[3,8,128,128]{3,2,1,0:T(8,128)}, u32[]{:S(2)}, u32[]{:S(2)}) collective-permute-start(f32[3,8,128,128]{3,2,1,0:T(8,128)} %shard_map.87), channel_id=1, source_target_pairs={{0,2},{1,3},{2,0},{3,1},{4,6},{5,7},{6,4},{7,5},{8,10},{9,11},{10,... | collective-permute-start | bytes 4718600 | tf_op jit(solution)/shard_map/ppermute | solution.py:281
  6.3 74.1 %copy-start.4 = (f32[32]{0:T(128)S(1)}, f32[32]{0:T(128)}, u32[]{:S(2)}) copy-start(f32[32]{0:T(128)} %rates.3) | copy-start | bytes 388
  6.3 8.3 %collective-permute-start = (f32[64,128]{1,0:T(8,128)S(1)}, f32[64,128]{1,0:T(8,128)S(1)}, u32[]{:S(2)}, u32[]{:S(2)}) collective-permute-start(f32[64,128]{1,0:T(8,128)S(1)} %bitcast.62), channel_id=1, source_target_pairs={{0,0},{4,1},{2,2},{6,3},{1,4},{5,5},{3,6},{7,7},{8,8},{12,9},{10,1... | collective-permute-start | bytes 98312 | tf_op jit(solution)/shard_map/ppermute | solution.py:277
  9.5 70.9 %copy-start = (bf16[1,1,128,4096]{3,2,1,0:T(8,128)(2,1)S(1)}, bf16[1,1,128,4096]{3,2,1,0:T(8,128)(2,1)}, u32[]{:S(2)}) copy-start(bf16[1,1,128,4096]{3,2,1,0:T(8,128)(2,1)} %param.7) | copy-start | bytes 3145732
  9.5 70.9 %copy-start.1 = (bf16[1,1,128,4096]{3,2,1,0:T(8,128)(2,1)S(1)}, bf16[1,1,128,4096]{3,2,1,0:T(8,128)(2,1)}, u32[]{:S(2)}) copy-start(bf16[1,1,128,4096]{3,2,1,0:T(8,128)(2,1)} %param.8) | copy-start | bytes 3145732
  9.5 70.9 %copy-start.2 = (bf16[1,1,128,4096]{3,2,1,0:T(8,128)(2,1)S(1)}, bf16[1,1,128,4096]{3,2,1,0:T(8,128)(2,1)}, u32[]{:S(2)}) copy-start(bf16[1,1,128,4096]{3,2,1,0:T(8,128)(2,1)} %param.9) | copy-start | bytes 3145732
  14.6 65.8 %collective-permute-start.7 = (f32[3,6,128,128]{3,2,1,0:T(8,128)}, f32[3,6,128,128]{3,2,1,0:T(8,128)S(1)}, u32[]{:S(2)}, u32[]{:S(2)}) collective-permute-start(f32[3,6,128,128]{3,2,1,0:T(8,128)} %get-tuple-element.30), channel_id=1, source_target_pairs={{0,1},{1,2},{2,3},{3,0},{4,5},{5,6},{6,7},{7,4},{8,9},{9,10},{10,1... | collective-permute-start | bytes 3538952 | tf_op jit(solution)/shard_map/ppermute | solution.py:281
  18.4 61.9 %collective-permute-start.8 = (f32[3,6,128,128]{3,2,1,0:T(8,128)}, f32[3,6,128,128]{3,2,1,0:T(8,128)S(1)}, u32[]{:S(2)}, u32[]{:S(2)}) collective-permute-start(f32[3,6,128,128]{3,2,1,0:T(8,128)} %get-tuple-element.31), channel_id=1, source_target_pairs={{0,3},{1,0},{2,1},{3,2},{4,7},{5,4},{6,5},{7,6},{8,11},{9,8},{10,9... | collective-permute-start | bytes 3538952 | tf_op jit(solution)/shard_map/ppermute | solution.py:281
  21.2 3.0 %collective-permute-start.4 = (f32[1,128]{1,0:T(1,128)S(1)}, f32[1,128]{1,0:T(1,128)S(1)}, u32[]{:S(2)}, u32[]{:S(2)}) collective-permute-start(f32[1,128]{1,0:T(1,128)S(1)} %broadcast_in_dim.12), channel_id=1, source_target_pairs={{0,64},{64,0},{128,192},{192,128},{256,320},{320,256},{384,448},{4... | collective-permute-start | bytes 1544 | tf_op jit(solution)/shard_map/ppermute | solution.py:291
  24.2 5.4 %collective-permute-start.5 = (f32[1,128]{1,0:T(1,128)S(1)}, f32[1,128]{1,0:T(1,128)S(1)}, u32[]{:S(2)}, u32[]{:S(2)}) collective-permute-start(f32[1,128]{1,0:T(1,128)S(1)} %add.9), channel_id=1, source_target_pairs={{0,128},{64,192},{128,0},{192,64},{256,384},{320,448},{384,256},{4... | collective-permute-start | bytes 1544 | tf_op jit(solution)/shard_map/ppermute | solution.py:291
  29.6 9.2 %collective-permute-start.6 = (f32[1,128]{1,0:T(1,128)S(1)}, f32[1,128]{1,0:T(1,128)S(1)}, u32[]{:S(2)}, u32[]{:S(2)}) collective-permute-start(f32[1,128]{1,0:T(1,128)S(1)} %add.10), channel_id=1, source_target_pairs={{0,256},{64,320},{128,384},{192,448},{256,0},{320,64},{384,128},{4... | collective-permute-start | bytes 1544 | tf_op jit(solution)/shard_map/ppermute | solution.py:291
  34.8 53.1 %collective-permute-start.1 = (f32[3,2,128,128]{3,2,1,0:T(8,128)}, f32[3,2,128,128]{3,2,1,0:T(8,128)S(1)}, u32[]{:S(2)}, u32[]{:S(2)}) collective-permute-start(f32[3,2,128,128]{3,2,1,0:T(8,128)} %get-tuple-element.26), channel_id=1, source_target_pairs={{0,1},{1,2},{2,3},{3,0},{4,5},{5,6},{6,7},{7,4},{8,9},{9,10},{10,1... | collective-permute-start | bytes 1179656 | tf_op jit(solution)/shard_map/ppermute | solution.py:281
  38.9 49.0 %collective-permute-start.3 = (f32[3,2,128,128]{3,2,1,0:T(8,128)}, f32[3,2,128,128]{3,2,1,0:T(8,128)S(1)}, u32[]{:S(2)}, u32[]{:S(2)}) collective-permute-start(f32[3,2,128,128]{3,2,1,0:T(8,128)} %get-tuple-element.27), channel_id=1, source_target_pairs={{0,3},{1,0},{2,1},{3,2},{4,7},{5,4},{6,5},{7,6},{8,11},{9,8},{10,9... | collective-permute-start | bytes 1179656 | tf_op jit(solution)/shard_map/ppermute | solution.py:281
  91.9 37.5 %copy-start.3 = (f32[8,128,128]{2,1,0:T(8,128)S(1)}, f32[8,128,128]{2,1,0:T(8,128)}, u32[]{:S(2)}) copy-start(f32[8,128,128]{2,1,0:T(8,128)} %get-tuple-element.37.refs_0_) | copy-start | bytes 1572868
  91.9 32.8 %all-to-all-start = ((f32[16,64,128]{2,1,0:T(8,128)}), f32[16,64,128]{2,1,0:T(8,128)S(1)}, u32[]{:S(2)}, u32[]{:S(2)}) async-start(f32[16,64,128]{2,1,0:T(8,128)} %bitcast.59), calls=%async_computation | async-start | bytes 1048576 | tf_op jit(solution)/shard_map/all_to_all | solution.py:305
  99.0 30.3 %collective-permute-start.9 = (f32[8,128,128]{2,1,0:T(8,128)}, f32[8,128,128]{2,1,0:T(8,128)S(1)}, u32[]{:S(2)}, u32[]{:S(2)}) collective-permute-start(f32[8,128,128]{2,1,0:T(8,128)} %get-tuple-element.38), channel_id=1, source_target_pairs={{0,1},{1,2},{2,3},{3,0},{4,5},{5,6},{6,7},{7,4},{8,9},{9,10},{10,1... | collective-permute-start | bytes 1572872 | tf_op jit(solution)/shard_map/ppermute | solution.py:281
  103.9 25.5 %collective-permute-start.10 = (f32[8,128,128]{2,1,0:T(8,128)}, f32[8,128,128]{2,1,0:T(8,128)S(1)}, u32[]{:S(2)}, u32[]{:S(2)}) collective-permute-start(f32[8,128,128]{2,1,0:T(8,128)} %get-tuple-element.39), channel_id=1, source_target_pairs={{0,2},{1,3},{2,0},{3,1},{4,6},{5,7},{6,4},{7,5},{8,10},{9,11},{10,... | collective-permute-start | bytes 1572872 | tf_op jit(solution)/shard_map/ppermute | solution.py:281
  105.8 23.6 %collective-permute-start.11 = (f32[8,128,128]{2,1,0:T(8,128)}, f32[8,128,128]{2,1,0:T(8,128)S(1)}, u32[]{:S(2)}, u32[]{:S(2)}) collective-permute-start(f32[8,128,128]{2,1,0:T(8,128)} %get-tuple-element.40), channel_id=1, source_target_pairs={{0,3},{1,0},{2,1},{3,2},{4,7},{5,4},{6,5},{7,6},{8,11},{9,8},{10,9... | collective-permute-start | bytes 1572872 | tf_op jit(solution)/shard_map/ppermute | solution.py:281
  124.8 6.7 %collective-permute-start.12 = (f32[1,64,128]{2,1,0:T(8,128)S(1)}, f32[1,64,128]{2,1,0:T(8,128)S(1)}, u32[]{:S(2)}, u32[]{:S(2)}) collective-permute-start(f32[1,64,128]{2,1,0:T(8,128)S(1)} %bitcast.61), channel_id=1, source_target_pairs={{0,0},{1,4},{2,2},{3,6},{4,1},{5,5},{6,3},{7,7},{8,8},{9,12},{10,1... | collective-permute-start | bytes 98312 | tf_op jit(solution)/shard_map/ppermute | solution.py:307

commit v6 on v5

--- a/solution.py
+++ b/solution.py
@@ -149,46 +149,48 @@
 
 
 def main_body(start, heads, scale, aliased, place, rates, reward, *refs):
+    me, length = place[0], place[1]
+    for device in range(4):
+
+        @pl.when(me == device)
+        def _(device=device):
+            main_at(device, length, start, heads, scale, aliased, rates, reward, *refs)
+
+
+def main_at(me, length, start, heads, scale, aliased, rates, reward, *refs):
     local, refs = refs[: 3 * heads], refs[3 * heads :]
     moved, prompt_ref, sums_ref, refs = refs[:3], refs[3], refs[4], refs[5 + aliased :]
     sums = jnp.sum(sums_ref[...], 0)
     slots = sums_ref.shape[0]
     factor = scale * (reward[0] - sums[1:2] / slots) / sums[0:1]
     outs, prompt_grad_ref = refs[:4], refs[4]
-    rows_q, rows_k, rows_v, grads_ref = refs[5:]
-    me, length = place[0], place[1]
     row = lax.broadcasted_iota(jnp.int32, (lane, lane), 0)
-    for step in range(heads):
-        for turn in range(4):
-            block = lax.rem(me + 4 - turn, 4)
+    half, steps = lane // 2, range(heads)
+    rows = []
+    for step in steps:
+        taken = ([], [], [])
+        for block in range(4):
+            turn = (me - block) % 4
             if turn == 0:
                 q, k, v = (r[...].astype(f32) for r in local[3 * step : 3 * step + 3])
             else:
                 q, k, v = (moved[turn - 1][which, step] for which in range(3))
             keep = (row + lane * block < length).astype(f32)
-            rows_q[step, block] = q.astype(bf16)
-            rows_k[step, block] = (k * keep).astype(bf16)
-            rows_v[step, block] = (v * keep).astype(bf16)
-    half, steps = lane // 2, range(heads)
-    head = residue(me) + 4 * (start + pl.program_id(0) * heads)
+            for rows_of, part in zip(taken, (q, k * keep, v * keep)):
+                rows_of.append(part.astype(bf16))
+        rows.append(taken)
+    head = 2 * (me % 2) + me // 2 + 4 * (start + pl.program_id(0) * heads)
     prompts = [
         jnp.concatenate([prompt_ref[2 * step, :half], prompt_ref[2 * step + 1, :half]], 0)
-        for step in steps
-    ]
-    rows = [
-        [[r[step, block] for block in range(4)] for r in (rows_q, rows_k, rows_v)]
         for step in steps
     ]
     grads, ends = head_grads(
         [rates[head + 4 * step] for step in steps], factor, length, rows, prompts
     )
     for step in steps:
-        for block in range(4):
-            grads_ref[step, block] = grads[step, block]
+        for turn in range(4):
+            outs[turn][step] = grads[step, (me + turn) % 4]
         prompt_grad_ref[step] = ends[step]
-    for step in range(heads):
-        for turn in range(4):
-            outs[turn][step] = grads_ref[step, lax.rem(me + turn, 4)]
 
 
 def main(place, rates, reward, scale, arrays, moved, prompt, so_far, block_len, start, count, heads=2):
@@ -222,8 +224,6 @@
             grid=(count // heads,),
             in_specs=in_specs,
             out_specs=[one] * 5,
-            scratch_shapes=[pltpu.VMEM((heads, 4, lane, lane), bf16)] * 3
-            + [pltpu.VMEM((heads, 4, lane, lane), f32)],
         ),
         out_shape=[pltpu.HBM((total, block_len, lane), f32)] * 5,
         input_output_aliases=aliases,
@@ -238,11 +238,11 @@
 
 def put_body(heads, place, *refs):
     parts, out = refs[:4], refs[4]
-    for turn in range(4):
+    for n, turn in enumerate((0, 2, 1, 3)):
         owner = residue(lax.rem(place[0] + 4 - turn, 4))
         for step in range(heads):
             column = pl.multiple_of((owner + 4 * step) * lane, lane)
-            out[:, pl.ds(column, lane)] = parts[turn][step].astype(bf16)
+            out[:, pl.ds(column, lane)] = parts[n][step].astype(bf16)
 
 
 def put(place, parts, block_len, width, heads=4):
@@ -301,11 +301,11 @@
         out = main(
             place, decay_rate, rewards[0], scale, arrays, parts, prompt, out, block_len, start, count
         )
-    back = [turned(out[turn], turn) for turn in (1, 2, 3)]
+    back = {turn: turned(out[turn], turn) for turn in (2, 1, 3)}
     terms = lax.all_to_all(out[4].reshape(slots, rows, lane), "slot", 0, 0, tiled=True)
     summed = jnp.sum(terms, 0, keepdims=True)
     summed = lax.ppermute(summed, ("slot", "ctx"), [(there, home) for home, there in moves])
-    key_grad = put(place, [out[0], *back], block_len, width)
+    key_grad = put(place, [out[0], back[2], back[1], back[3]], block_len, width)
     return (key_grad.reshape(1, 1, block_len, width), summed)
 
 

time: 133 us -> 133 us (level)
  no operation moved by 1% of the time
where the time goes in v6:
time: 133 us; the launch traced here: 132 us
  starting transfers between devices  50.2 us (38%)
  blocking collectives  39.4 us (30%)
  waiting for transfers between devices  19.8 us (15%)
  Pallas kernels  19.2 us (14%)
  between operations  2.21 us (2%)
    all_gather x1, blocking collectives, shards(): prompt = lax.all_gather(jnp.concatenate([piece, scalars], 0), 'slot')  39.4 us
    ppermute x8, starting transfers between devices, turned(): return lax.ppermute(part, 'ctx', rings[turn])  25.5 us
    all_to_all x1, waiting for transfers between devices, shards(): lax.all_to_all(out[4].reshape(slots, rows, lane), 'slot', 0, 0, tiled=True)  15.8 us
    pallas_call x2, Pallas kernels, main(): pl.pallas_call(functools.partial(main_body, start, heads, scale, len(so_f...  10.9 us
    ppermute x3, starting transfers between devices, shards(): lax.ppermute(tokens, 'group', [(i, i ^ step) for i in range(groups)])  8.96 us
    all_to_all x1, starting transfers between devices, shards(): lax.all_to_all(out[4].reshape(slots, rows, lane), 'slot', 0, 0, tiled=True)  7.08 us
    pallas_call x2, Pallas kernels, pack(): pl.pallas_call(body, grid_spec=pltpu.PrefetchScalarGridSpec(num_scalar_pr...  6.66 us
    ppermute x1, starting transfers between devices, shards(): lax.ppermute(summed, ('slot', 'ctx'), [(there, home) for home, there in m...  5.44 us
  transfers between devices with their start and end apart: 14, of which 4 were waited for; matrix products, arithmetic and copies ran while one was open for 0% of the time, Pallas kernels for 10%

profile of v6, /device:TPU:6, one launch (start us, length us, event | category | flops | bytes accessed | tf_op | source)
XLA Modules:
  0.0 131.8 jit_solution(1657446355341739755)
XLA Ops:
  0.6 0.0 copy-start.5
  0.6 2.3 %shard_map.87 = f32[3,8,128,128]{3,2,1,0:T(8,128)} custom-call(s32[1]{0:T(128)} %bitcast.me, bf16[128,4096]{1,0:T(8,128)(2,1)} %bitcast.19, bf16[128,4096]{1,0:T(8,128)(2,1)} %bitcast.31, bf16[128,4096]{1,0:T(8,128)(2,1)} %bitcast.43, bf16[128,4096]{1,0:T(8,128)(2,1)} %bitcast.20, bf16[128,4096]{1,0:T(8,128)(2,1)} %bitcast.32, bf16[128,4096]{1,0:T(8,128)(2,1)} %bitcast.44, ...), custom_call_target="tpu_custom_call" | custom-call | bytes 6291456 | tf_op jit(solution)/shard_map/pallas_call | solution.py:76
  2.9 3.3 %collective-permute-start.2 = (f32[3,8,128,128]{3,2,1,0:T(8,128)}, f32[3,8,128,128]{3,2,1,0:T(8,128)}, u32[]{:S(2)}, u32[]{:S(2)}) collective-permute-start(f32[3,8,128,128]{3,2,1,0:T(8,128)} %shard_map.87), channel_id=1, source_target_pairs={{0,2},{1,3},{2,0},{3,1},{4,6},{5,7},{6,4},{7,5},{8,10},{9,11},{10,... | collective-permute-start | bytes 4718600 | tf_op jit(solution)/shard_map/ppermute | solution.py:281
  6.2 0.0 copy-done.5
  6.3 0.0 copy-start.4
  6.3 3.2 %collective-permute-start = (f32[64,128]{1,0:T(8,128)S(1)}, f32[64,128]{1,0:T(8,128)S(1)}, u32[]{:S(2)}, u32[]{:S(2)}) collective-permute-start(f32[64,128]{1,0:T(8,128)S(1)} %bitcast.62), channel_id=1, source_target_pairs={{0,0},{4,1},{2,2},{6,3},{1,4},{5,5},{3,6},{7,7},{8,8},{12,9},{10,1... | collective-permute-start | bytes 98312 | tf_op jit(solution)/shard_map/ppermute | solution.py:277
  9.5 0.0 copy-start
  9.5 0.0 copy-start.1
  9.5 0.0 copy-start.2
  9.5 4.4 %shard_map.86 = (f32[3,6,128,128]{3,2,1,0:T(8,128)}, f32[3,6,128,128]{3,2,1,0:T(8,128)}, f32[3,2,128,128]{3,2,1,0:T(8,128)}, f32[3,2,128,128]{3,2,1,0:T(8,128)}) custom-call(s32[1]{0:T(128)} %bitcast.me, bf16[128,4096]{1,0:T(8,128)(2,1)} %bitcast.23, bf16[128,4096]{1,0:T(8,128)(2,1)} %bitcast.35, bf16[128,4096]{1,0:T(8,128)(2,1)} %bitcast.47, ...), custom_call_target="tpu_custom_call" | custom-call | bytes 6291456 | tf_op jit(solution)/shard_map/pallas_call | solution.py:76
  14.5 0.0 collective-permute-done
  14.6 3.8 %collective-permute-start.7 = (f32[3,6,128,128]{3,2,1,0:T(8,128)}, f32[3,6,128,128]{3,2,1,0:T(8,128)S(1)}, u32[]{:S(2)}, u32[]{:S(2)}) collective-permute-start(f32[3,6,128,128]{3,2,1,0:T(8,128)} %get-tuple-element.30), channel_id=1, source_target_pairs={{0,1},{1,2},{2,3},{3,0},{4,5},{5,6},{6,7},{7,4},{8,9},{9,10},{10,1... | collective-permute-start | bytes 3538952 | tf_op jit(solution)/shard_map/ppermute | solution.py:281
  18.4 2.8 %collective-permute-start.8 = (f32[3,6,128,128]{3,2,1,0:T(8,128)}, f32[3,6,128,128]{3,2,1,0:T(8,128)S(1)}, u32[]{:S(2)}, u32[]{:S(2)}) collective-permute-start(f32[3,6,128,128]{3,2,1,0:T(8,128)} %get-tuple-element.31), channel_id=1, source_target_pairs={{0,3},{1,0},{2,1},{3,2},{4,7},{5,4},{6,5},{7,6},{8,11},{9,8},{10,9... | collective-permute-start | bytes 3538952 | tf_op jit(solution)/shard_map/ppermute | solution.py:281
  21.2 1.9 %collective-permute-start.4 = (f32[1,128]{1,0:T(1,128)S(1)}, f32[1,128]{1,0:T(1,128)S(1)}, u32[]{:S(2)}, u32[]{:S(2)}) collective-permute-start(f32[1,128]{1,0:T(1,128)S(1)} %broadcast_in_dim.12), channel_id=1, source_target_pairs={{0,64},{64,0},{128,192},{192,128},{256,320},{320,256},{384,448},{4... | collective-permute-start | bytes 1544 | tf_op jit(solution)/shard_map/ppermute | solution.py:291
  23.1 1.1 collective-permute-done.4
  24.2 2.7 %collective-permute-start.5 = (f32[1,128]{1,0:T(1,128)S(1)}, f32[1,128]{1,0:T(1,128)S(1)}, u32[]{:S(2)}, u32[]{:S(2)}) collective-permute-start(f32[1,128]{1,0:T(1,128)S(1)} %add.9), channel_id=1, source_target_pairs={{0,128},{64,192},{128,0},{192,64},{256,384},{320,448},{384,256},{4... | collective-permute-start | bytes 1544 | tf_op jit(solution)/shard_map/ppermute | solution.py:291
  26.9 0.1 pad_add_fusion.place
  27.0 2.6 %collective-permute-done.5 = f32[1,128]{1,0:T(1,128)S(1)} collective-permute-done((f32[1,128]{1,0:T(1,128)S(1)}, f32[1,128]{1,0:T(1,128)S(1)}, u32[]{:S(2)}, u32[]{:S(2)}) %collective-permute-start.5) | collective-permute-done | bytes 544 | tf_op jit(solution)/shard_map/ppermute | solution.py:291
  29.6 4.3 %collective-permute-start.6 = (f32[1,128]{1,0:T(1,128)S(1)}, f32[1,128]{1,0:T(1,128)S(1)}, u32[]{:S(2)}, u32[]{:S(2)}) collective-permute-start(f32[1,128]{1,0:T(1,128)S(1)} %add.10), channel_id=1, source_target_pairs={{0,256},{64,320},{128,384},{192,448},{256,0},{320,64},{384,128},{4... | collective-permute-start | bytes 1544 | tf_op jit(solution)/shard_map/ppermute | solution.py:291
  34.6 0.1 pad.2.clone
  34.7 0.1 pad.3.clone
  34.8 4.1 %collective-permute-start.1 = (f32[3,2,128,128]{3,2,1,0:T(8,128)}, f32[3,2,128,128]{3,2,1,0:T(8,128)S(1)}, u32[]{:S(2)}, u32[]{:S(2)}) collective-permute-start(f32[3,2,128,128]{3,2,1,0:T(8,128)} %get-tuple-element.26), channel_id=1, source_target_pairs={{0,1},{1,2},{2,3},{3,0},{4,5},{5,6},{6,7},{7,4},{8,9},{9,10},{10,1... | collective-permute-start | bytes 1179656 | tf_op jit(solution)/shard_map/ppermute | solution.py:281
  38.8 0.0 collective-permute-done.6
  38.9 1.9 %collective-permute-start.3 = (f32[3,2,128,128]{3,2,1,0:T(8,128)}, f32[3,2,128,128]{3,2,1,0:T(8,128)S(1)}, u32[]{:S(2)}, u32[]{:S(2)}) collective-permute-start(f32[3,2,128,128]{3,2,1,0:T(8,128)} %get-tuple-element.27), channel_id=1, source_target_pairs={{0,3},{1,0},{2,1},{3,2},{4,7},{5,4},{6,5},{7,6},{8,11},{9,8},{10,9... | collective-permute-start | bytes 1179656 | tf_op jit(solution)/shard_map/ppermute | solution.py:281
  40.8 0.1 maximum_maximum_fusion
  40.9 39.4 %all-gather = f32[1152,128]{1,0:T(8,128)S(1)} all-gather(f32[72,128]{1,0:T(8,128)S(1)} %maximum_maximum_fusion), channel_id=2, replica_groups=mesh['group'=8,'slot'=16,'ctx'=4] {'slot'}, dimensions={0}, use_global_device_ids=true | all-gather | bytes 626688 | tf_op jit(solution)/shard_map/all_gather | solution.py:295
  80.3 0.0 collective-permute-done.7.refs_6_
  80.3 0.0 collective-permute-done.8.refs_8_
  80.3 0.0 collective-permute-done.2.refs_7_
  80.3 0.0 copy-done.4
  80.3 0.0 copy-done
  80.3 0.0 copy-done.1
  80.3 0.0 copy-done.2
  80.4 7.0 %shard_map.88 = (f32[8,128,128]{2,1,0:T(8,128)}, f32[8,128,128]{2,1,0:T(8,128)}, f32[8,128,128]{2,1,0:T(8,128)}, f32[8,128,128]{2,1,0:T(8,128)}, f32[8,128,128]{2,1,0:T(8,128)}) custom-call(s32[2]{0:T(128)S(1)} %pad_add_fusion.place, f32[32]{0:T(128)S(1)} %copy-done.4, f32[1]{0:T(128)} %bitcast.16.reward, bf16[128,4096]{1,0:T(8,128)(2,1)S(1)} %bitcast.27, ...), custom_call_target="tpu_custom_call" | custom-call | flops 1509949440 | bytes 7864320 | tf_op jit(solution)/shard_map/pallas_call | solution.py:220
  87.4 0.0 collective-permute-done.1.refs_6_
  87.4 0.0 collective-permute-done.3.refs_8_
  87.4 3.8 %shard_map.89 = (f32[8,128,128]{2,1,0:T(8,128)}, f32[8,128,128]{2,1,0:T(8,128)}, f32[8,128,128]{2,1,0:T(8,128)}, f32[8,128,128]{2,1,0:T(8,128)}, f32[8,128,128]{2,1,0:T(8,128)}) custom-call(s32[2]{0:T(128)S(1)} %pad_add_fusion.place, f32[32]{0:T(128)S(1)} %copy-done.4, ...), custom_call_target="tpu_custom_call", output_to_operand_aliasing={{0}: (14, {}), {1}: (15, {}), {2}: (16, {}), {3}: (17, {}),... | custom-call | flops 503316480 | bytes 2621440 | tf_op jit(solution)/shard_map/pallas_call | solution.py:220
  91.2 0.0 copy-start.3
  91.2 7.1 %all-to-all-start = ((f32[16,64,128]{2,1,0:T(8,128)}), f32[16,64,128]{2,1,0:T(8,128)S(1)}, u32[]{:S(2)}, u32[]{:S(2)}) async-start(f32[16,64,128]{2,1,0:T(8,128)} %bitcast.59), calls=%async_computation | async-start | bytes 1048576 | tf_op jit(solution)/shard_map/all_to_all | solution.py:305
  98.3 3.5 %collective-permute-start.9 = (f32[8,128,128]{2,1,0:T(8,128)}, f32[8,128,128]{2,1,0:T(8,128)S(1)}, u32[]{:S(2)}, u32[]{:S(2)}) collective-permute-start(f32[8,128,128]{2,1,0:T(8,128)} %get-tuple-element.38), channel_id=1, source_target_pairs={{0,2},{1,3},{2,0},{3,1},{4,6},{5,7},{6,4},{7,5},{8,10},{9,11},{10,... | collective-permute-start | bytes 1572872 | tf_op jit(solution)/shard_map/ppermute | solution.py:281
  101.9 3.4 %collective-permute-start.10 = (f32[8,128,128]{2,1,0:T(8,128)}, f32[8,128,128]{2,1,0:T(8,128)S(1)}, u32[]{:S(2)}, u32[]{:S(2)}) collective-permute-start(f32[8,128,128]{2,1,0:T(8,128)} %get-tuple-element.39), channel_id=1, source_target_pairs={{0,1},{1,2},{2,3},{3,0},{4,5},{5,6},{6,7},{7,4},{8,9},{9,10},{10,1... | collective-permute-start | bytes 1572872 | tf_op jit(solution)/shard_map/ppermute | solution.py:281
  105.3 2.7 %collective-permute-start.11 = (f32[8,128,128]{2,1,0:T(8,128)}, f32[8,128,128]{2,1,0:T(8,128)S(1)}, u32[]{:S(2)}, u32[]{:S(2)}) collective-permute-start(f32[8,128,128]{2,1,0:T(8,128)} %get-tuple-element.40), channel_id=1, source_target_pairs={{0,3},{1,0},{2,1},{3,2},{4,7},{5,4},{6,5},{7,6},{8,11},{9,8},{10,9... | collective-permute-start | bytes 1572872 | tf_op jit(solution)/shard_map/ppermute | solution.py:281
  107.9 15.8 %all-to-all-done = f32[16,64,128]{2,1,0:T(8,128)S(1)} async-done(((f32[16,64,128]{2,1,0:T(8,128)}), f32[16,64,128]{2,1,0:T(8,128)S(1)}, u32[]{:S(2)}, u32[]{:S(2)}) %all-to-all-start) | async-done | bytes 524320 | tf_op jit(solution)/shard_map/all_to_all | solution.py:305
  123.8 5.4 %collective-permute-start.12 = (f32[1,64,128]{2,1,0:T(8,128)S(1)}, f32[1,64,128]{2,1,0:T(8,128)S(1)}, u32[]{:S(2)}, u32[]{:S(2)}) collective-permute-start(f32[1,64,128]{2,1,0:T(8,128)S(1)} %bitcast.61), channel_id=1, source_target_pairs={{0,0},{1,4},{2,2},{3,6},{4,1},{5,5},{6,3},{7,7},{8,8},{9,12},{10,1... | collective-permute-start | bytes 98312 | tf_op jit(solution)/shard_map/ppermute | solution.py:307
  129.3 0.0 collective-permute-done.9.refs_1_
  129.3 0.0 collective-permute-done.10.refs_2_
  129.3 0.0 collective-permute-done.11.refs_3_
  129.3 0.0 copy-done.3
  129.3 1.7 %shard_map.90 = bf16[128,4096]{1,0:T(8,128)(2,1)} custom-call(s32[2]{0:T(128)S(1)} %pad_add_fusion.place, f32[8,128,128]{2,1,0:T(8,128)S(1)} %copy-done.3, f32[8,128,128]{2,1,0:T(8,128)S(1)} %collective-permute-done.9.refs_1_, f32[8,128,128]{2,1,0:T(8,128)S(1)} %collective-permute-done.10.refs_2_, f32[8,128,128]{2,1,0:T(8,128)S(1)} %collective-permute-done.11.refs_3_), custom_call_target="tpu_custom_call" | custom-call | bytes 3145728 | tf_op jit(solution)/shard_map/pallas_call | solution.py:249
  131.0 0.2 collective-permute-done.12
  131.1 0.6 copy.22
  (6 shorter events, 0.0 us)
Async XLA Ops:
  0.6 5.6 %copy-start.5 = (f32[1,64,128]{2,1,0:T(8,128)S(1)}, f32[1,64,128]{2,1,0:T(8,128)}, u32[]{:S(2)}) copy-start(f32[1,64,128]{2,1,0:T(8,128)} %param.13) | copy-start | bytes 98308
  2.9 77.4 %collective-permute-start.2 = (f32[3,8,128,128]{3,2,1,0:T(8,128)}, f32[3,8,128,128]{3,2,1,0:T(8,128)}, u32[]{:S(2)}, u32[]{:S(2)}) collective-permute-start(f32[3,8,128,128]{3,2,1,0:T(8,128)} %shard_map.87), channel_id=1, source_target_pairs={{0,2},{1,3},{2,0},{3,1},{4,6},{5,7},{6,4},{7,5},{8,10},{9,11},{10,... | collective-permute-start | bytes 4718600 | tf_op jit(solution)/shard_map/ppermute | solution.py:281
  6.3 74.1 %copy-start.4 = (f32[32]{0:T(128)S(1)}, f32[32]{0:T(128)}, u32[]{:S(2)}) copy-start(f32[32]{0:T(128)} %rates.3) | copy-start | bytes 388
  6.3 8.3 %collective-permute-start = (f32[64,128]{1,0:T(8,128)S(1)}, f32[64,128]{1,0:T(8,128)S(1)}, u32[]{:S(2)}, u32[]{:S(2)}) collective-permute-start(f32[64,128]{1,0:T(8,128)S(1)} %bitcast.62), channel_id=1, source_target_pairs={{0,0},{4,1},{2,2},{6,3},{1,4},{5,5},{3,6},{7,7},{8,8},{12,9},{10,1... | collective-permute-start | bytes 98312 | tf_op jit(solution)/shard_map/ppermute | solution.py:277
  9.5 70.9 %copy-start = (bf16[1,1,128,4096]{3,2,1,0:T(8,128)(2,1)S(1)}, bf16[1,1,128,4096]{3,2,1,0:T(8,128)(2,1)}, u32[]{:S(2)}) copy-start(bf16[1,1,128,4096]{3,2,1,0:T(8,128)(2,1)} %param.7) | copy-start | bytes 3145732
  9.5 70.9 %copy-start.1 = (bf16[1,1,128,4096]{3,2,1,0:T(8,128)(2,1)S(1)}, bf16[1,1,128,4096]{3,2,1,0:T(8,128)(2,1)}, u32[]{:S(2)}) copy-start(bf16[1,1,128,4096]{3,2,1,0:T(8,128)(2,1)} %param.8) | copy-start | bytes 3145732
  9.5 70.9 %copy-start.2 = (bf16[1,1,128,4096]{3,2,1,0:T(8,128)(2,1)S(1)}, bf16[1,1,128,4096]{3,2,1,0:T(8,128)(2,1)}, u32[]{:S(2)}) copy-start(bf16[1,1,128,4096]{3,2,1,0:T(8,128)(2,1)} %param.9) | copy-start | bytes 3145732
  14.6 65.8 %collective-permute-start.7 = (f32[3,6,128,128]{3,2,1,0:T(8,128)}, f32[3,6,128,128]{3,2,1,0:T(8,128)S(1)}, u32[]{:S(2)}, u32[]{:S(2)}) collective-permute-start(f32[3,6,128,128]{3,2,1,0:T(8,128)} %get-tuple-element.30), channel_id=1, source_target_pairs={{0,1},{1,2},{2,3},{3,0},{4,5},{5,6},{6,7},{7,4},{8,9},{9,10},{10,1... | collective-permute-start | bytes 3538952 | tf_op jit(solution)/shard_map/ppermute | solution.py:281
  18.4 61.9 %collective-permute-start.8 = (f32[3,6,128,128]{3,2,1,0:T(8,128)}, f32[3,6,128,128]{3,2,1,0:T(8,128)S(1)}, u32[]{:S(2)}, u32[]{:S(2)}) collective-permute-start(f32[3,6,128,128]{3,2,1,0:T(8,128)} %get-tuple-element.31), channel_id=1, source_target_pairs={{0,3},{1,0},{2,1},{3,2},{4,7},{5,4},{6,5},{7,6},{8,11},{9,8},{10,9... | collective-permute-start | bytes 3538952 | tf_op jit(solution)/shard_map/ppermute | solution.py:281
  21.2 3.0 %collective-permute-start.4 = (f32[1,128]{1,0:T(1,128)S(1)}, f32[1,128]{1,0:T(1,128)S(1)}, u32[]{:S(2)}, u32[]{:S(2)}) collective-permute-start(f32[1,128]{1,0:T(1,128)S(1)} %broadcast_in_dim.12), channel_id=1, source_target_pairs={{0,64},{64,0},{128,192},{192,128},{256,320},{320,256},{384,448},{4... | collective-permute-start | bytes 1544 | tf_op jit(solution)/shard_map/ppermute | solution.py:291
  24.2 5.4 %collective-permute-start.5 = (f32[1,128]{1,0:T(1,128)S(1)}, f32[1,128]{1,0:T(1,128)S(1)}, u32[]{:S(2)}, u32[]{:S(2)}) collective-permute-start(f32[1,128]{1,0:T(1,128)S(1)} %add.9), channel_id=1, source_target_pairs={{0,128},{64,192},{128,0},{192,64},{256,384},{320,448},{384,256},{4... | collective-permute-start | bytes 1544 | tf_op jit(solution)/shard_map/ppermute | solution.py:291
  29.6 9.2 %collective-permute-start.6 = (f32[1,128]{1,0:T(1,128)S(1)}, f32[1,128]{1,0:T(1,128)S(1)}, u32[]{:S(2)}, u32[]{:S(2)}) collective-permute-start(f32[1,128]{1,0:T(1,128)S(1)} %add.10), channel_id=1, source_target_pairs={{0,256},{64,320},{128,384},{192,448},{256,0},{320,64},{384,128},{4... | collective-permute-start | bytes 1544 | tf_op jit(solution)/shard_map/ppermute | solution.py:291
  34.8 52.6 %collective-permute-start.1 = (f32[3,2,128,128]{3,2,1,0:T(8,128)}, f32[3,2,128,128]{3,2,1,0:T(8,128)S(1)}, u32[]{:S(2)}, u32[]{:S(2)}) collective-permute-start(f32[3,2,128,128]{3,2,1,0:T(8,128)} %get-tuple-element.26), channel_id=1, source_target_pairs={{0,1},{1,2},{2,3},{3,0},{4,5},{5,6},{6,7},{7,4},{8,9},{9,10},{10,1... | collective-permute-start | bytes 1179656 | tf_op jit(solution)/shard_map/ppermute | solution.py:281
  38.9 48.6 %collective-permute-start.3 = (f32[3,2,128,128]{3,2,1,0:T(8,128)}, f32[3,2,128,128]{3,2,1,0:T(8,128)S(1)}, u32[]{:S(2)}, u32[]{:S(2)}) collective-permute-start(f32[3,2,128,128]{3,2,1,0:T(8,128)} %get-tuple-element.27), channel_id=1, source_target_pairs={{0,3},{1,0},{2,1},{3,2},{4,7},{5,4},{6,5},{7,6},{8,11},{9,8},{10,9... | collective-permute-start | bytes 1179656 | tf_op jit(solution)/shard_map/ppermute | solution.py:281
  91.2 38.1 %copy-start.3 = (f32[8,128,128]{2,1,0:T(8,128)S(1)}, f32[8,128,128]{2,1,0:T(8,128)}, u32[]{:S(2)}) copy-start(f32[8,128,128]{2,1,0:T(8,128)} %get-tuple-element.37.refs_0_) | copy-start | bytes 1572868
  91.2 32.6 %all-to-all-start = ((f32[16,64,128]{2,1,0:T(8,128)}), f32[16,64,128]{2,1,0:T(8,128)S(1)}, u32[]{:S(2)}, u32[]{:S(2)}) async-start(f32[16,64,128]{2,1,0:T(8,128)} %bitcast.59), calls=%async_computation | async-start | bytes 1048576 | tf_op jit(solution)/shard_map/all_to_all | solution.py:305
  98.3 31.0 %collective-permute-start.9 = (f32[8,128,128]{2,1,0:T(8,128)}, f32[8,128,128]{2,1,0:T(8,128)S(1)}, u32[]{:S(2)}, u32[]{:S(2)}) collective-permute-start(f32[8,128,128]{2,1,0:T(8,128)} %get-tuple-element.38), channel_id=1, source_target_pairs={{0,2},{1,3},{2,0},{3,1},{4,6},{5,7},{6,4},{7,5},{8,10},{9,11},{10,... | collective-permute-start | bytes 1572872 | tf_op jit(solution)/shard_map/ppermute | solution.py:281
  101.9 27.4 %collective-permute-start.10 = (f32[8,128,128]{2,1,0:T(8,128)}, f32[8,128,128]{2,1,0:T(8,128)S(1)}, u32[]{:S(2)}, u32[]{:S(2)}) collective-permute-start(f32[8,128,128]{2,1,0:T(8,128)} %get-tuple-element.39), channel_id=1, source_target_pairs={{0,1},{1,2},{2,3},{3,0},{4,5},{5,6},{6,7},{7,4},{8,9},{9,10},{10,1... | collective-permute-start | bytes 1572872 | tf_op jit(solution)/shard_map/ppermute | solution.py:281
  105.3 24.0 %collective-permute-start.11 = (f32[8,128,128]{2,1,0:T(8,128)}, f32[8,128,128]{2,1,0:T(8,128)S(1)}, u32[]{:S(2)}, u32[]{:S(2)}) collective-permute-start(f32[8,128,128]{2,1,0:T(8,128)} %get-tuple-element.40), channel_id=1, source_target_pairs={{0,3},{1,0},{2,1},{3,2},{4,7},{5,4},{6,5},{7,6},{8,11},{9,8},{10,9... | collective-permute-start | bytes 1572872 | tf_op jit(solution)/shard_map/ppermute | solution.py:281
  123.8 7.3 %collective-permute-start.12 = (f32[1,64,128]{2,1,0:T(8,128)S(1)}, f32[1,64,128]{2,1,0:T(8,128)S(1)}, u32[]{:S(2)}, u32[]{:S(2)}) collective-permute-start(f32[1,64,128]{2,1,0:T(8,128)S(1)} %bitcast.61), channel_id=1, source_target_pairs={{0,0},{1,4},{2,2},{3,6},{4,1},{5,5},{6,3},{7,7},{8,8},{9,12},{10,1... | collective-permute-start | bytes 98312 | tf_op jit(solution)/shard_map/ppermute | solution.py:307

commit v7 on v6

--- a/solution.py
+++ b/solution.py
@@ -189,7 +189,7 @@
     )
     for step in steps:
         for turn in range(4):
-            outs[turn][step] = grads[step, (me + turn) % 4]
+            outs[turn][step] = grads[step, (me + turn) % 4].astype(outs[turn].dtype)
         prompt_grad_ref[step] = ends[step]
 
 
@@ -225,7 +225,9 @@
             in_specs=in_specs,
             out_specs=[one] * 5,
         ),
-        out_shape=[pltpu.HBM((total, block_len, lane), f32)] * 5,
+        out_shape=[
+            pltpu.HBM((total, block_len, lane), bf16 if n == 0 else f32) for n in range(5)
+        ],
         input_output_aliases=aliases,
         compiler_params=pltpu.CompilerParams(vmem_limit_bytes=vmem_bytes),
         cost_estimate=pl.CostEstimate(

time: 133 us -> 133 us (level)
  no operation moved by 1% of the time
where the time goes in v7:
time: 133 us; the launch traced here: 132 us
  starting transfers between devices  50.2 us (38%)
  blocking collectives  39.4 us (30%)
  waiting for transfers between devices  19.8 us (15%)
  Pallas kernels  19.1 us (14%)
  between operations  2.21 us (2%)
    all_gather x1, blocking collectives, shards(): prompt = lax.all_gather(jnp.concatenate([piece, scalars], 0), 'slot')  39.4 us
    ppermute x8, starting transfers between devices, turned(): return lax.ppermute(part, 'ctx', rings[turn])  25.5 us
    all_to_all x1, waiting for transfers between devices, shards(): lax.all_to_all(out[4].reshape(slots, rows, lane), 'slot', 0, 0, tiled=True)  15.8 us
    pallas_call x2, Pallas kernels, main(): pl.pallas_call(functools.partial(main_body, start, heads, scale, len(so_f...  10.8 us
    ppermute x3, starting transfers between devices, shards(): lax.ppermute(tokens, 'group', [(i, i ^ step) for i in range(groups)])  8.96 us
    all_to_all x1, starting transfers between devices, shards(): lax.all_to_all(out[4].reshape(slots, rows, lane), 'slot', 0, 0, tiled=True)  7.08 us
    pallas_call x2, Pallas kernels, pack(): pl.pallas_call(body, grid_spec=pltpu.PrefetchScalarGridSpec(num_scalar_pr...  6.66 us
    ppermute x1, starting transfers between devices, shards(): lax.ppermute(summed, ('slot', 'ctx'), [(there, home) for home, there in m...  5.43 us
  transfers between devices with their start and end apart: 14, of which 4 were waited for; matrix products, arithmetic and copies ran while one was open for 0% of the time, Pallas kernels for 10%

profile of v7, /device:TPU:6, one launch (start us, length us, event | category | flops | bytes accessed | tf_op | source)
XLA Modules:
  0.0 131.7 jit_solution(6044071790766642612)
XLA Ops:
  0.6 0.0 copy-start.5
  0.6 2.3 %shard_map.87 = f32[3,8,128,128]{3,2,1,0:T(8,128)} custom-call(s32[1]{0:T(128)} %bitcast.me, bf16[128,4096]{1,0:T(8,128)(2,1)} %bitcast.19, bf16[128,4096]{1,0:T(8,128)(2,1)} %bitcast.31, bf16[128,4096]{1,0:T(8,128)(2,1)} %bitcast.43, bf16[128,4096]{1,0:T(8,128)(2,1)} %bitcast.20, bf16[128,4096]{1,0:T(8,128)(2,1)} %bitcast.32, bf16[128,4096]{1,0:T(8,128)(2,1)} %bitcast.44, ...), custom_call_target="tpu_custom_call" | custom-call | bytes 6291456 | tf_op jit(solution)/shard_map/pallas_call | solution.py:76
  2.9 3.3 %collective-permute-start.2 = (f32[3,8,128,128]{3,2,1,0:T(8,128)}, f32[3,8,128,128]{3,2,1,0:T(8,128)}, u32[]{:S(2)}, u32[]{:S(2)}) collective-permute-start(f32[3,8,128,128]{3,2,1,0:T(8,128)} %shard_map.87), channel_id=1, source_target_pairs={{0,2},{1,3},{2,0},{3,1},{4,6},{5,7},{6,4},{7,5},{8,10},{9,11},{10,... | collective-permute-start | bytes 4718600 | tf_op jit(solution)/shard_map/ppermute | solution.py:283
  6.2 0.0 copy-done.5
  6.3 0.0 copy-start.4
  6.3 3.2 %collective-permute-start = (f32[64,128]{1,0:T(8,128)S(1)}, f32[64,128]{1,0:T(8,128)S(1)}, u32[]{:S(2)}, u32[]{:S(2)}) collective-permute-start(f32[64,128]{1,0:T(8,128)S(1)} %bitcast.62), channel_id=1, source_target_pairs={{0,0},{4,1},{2,2},{6,3},{1,4},{5,5},{3,6},{7,7},{8,8},{12,9},{10,1... | collective-permute-start | bytes 98312 | tf_op jit(solution)/shard_map/ppermute | solution.py:279
  9.5 0.0 copy-start
  9.5 0.0 copy-start.1
  9.5 0.0 copy-start.2
  9.5 4.4 %shard_map.86 = (f32[3,6,128,128]{3,2,1,0:T(8,128)}, f32[3,6,128,128]{3,2,1,0:T(8,128)}, f32[3,2,128,128]{3,2,1,0:T(8,128)}, f32[3,2,128,128]{3,2,1,0:T(8,128)}) custom-call(s32[1]{0:T(128)} %bitcast.me, bf16[128,4096]{1,0:T(8,128)(2,1)} %bitcast.23, bf16[128,4096]{1,0:T(8,128)(2,1)} %bitcast.35, bf16[128,4096]{1,0:T(8,128)(2,1)} %bitcast.47, ...), custom_call_target="tpu_custom_call" | custom-call | bytes 6291456 | tf_op jit(solution)/shard_map/pallas_call | solution.py:76
  14.5 0.0 collective-permute-done
  14.6 3.8 %collective-permute-start.7 = (f32[3,6,128,128]{3,2,1,0:T(8,128)}, f32[3,6,128,128]{3,2,1,0:T(8,128)S(1)}, u32[]{:S(2)}, u32[]{:S(2)}) collective-permute-start(f32[3,6,128,128]{3,2,1,0:T(8,128)} %get-tuple-element.30), channel_id=1, source_target_pairs={{0,1},{1,2},{2,3},{3,0},{4,5},{5,6},{6,7},{7,4},{8,9},{9,10},{10,1... | collective-permute-start | bytes 3538952 | tf_op jit(solution)/shard_map/ppermute | solution.py:283
  18.4 2.8 %collective-permute-start.8 = (f32[3,6,128,128]{3,2,1,0:T(8,128)}, f32[3,6,128,128]{3,2,1,0:T(8,128)S(1)}, u32[]{:S(2)}, u32[]{:S(2)}) collective-permute-start(f32[3,6,128,128]{3,2,1,0:T(8,128)} %get-tuple-element.31), channel_id=1, source_target_pairs={{0,3},{1,0},{2,1},{3,2},{4,7},{5,4},{6,5},{7,6},{8,11},{9,8},{10,9... | collective-permute-start | bytes 3538952 | tf_op jit(solution)/shard_map/ppermute | solution.py:283
  21.2 1.9 %collective-permute-start.4 = (f32[1,128]{1,0:T(1,128)S(1)}, f32[1,128]{1,0:T(1,128)S(1)}, u32[]{:S(2)}, u32[]{:S(2)}) collective-permute-start(f32[1,128]{1,0:T(1,128)S(1)} %broadcast_in_dim.12), channel_id=1, source_target_pairs={{0,64},{64,0},{128,192},{192,128},{256,320},{320,256},{384,448},{4... | collective-permute-start | bytes 1544 | tf_op jit(solution)/shard_map/ppermute | solution.py:293
  23.1 1.1 collective-permute-done.4
  24.2 2.7 %collective-permute-start.5 = (f32[1,128]{1,0:T(1,128)S(1)}, f32[1,128]{1,0:T(1,128)S(1)}, u32[]{:S(2)}, u32[]{:S(2)}) collective-permute-start(f32[1,128]{1,0:T(1,128)S(1)} %add.9), channel_id=1, source_target_pairs={{0,128},{64,192},{128,0},{192,64},{256,384},{320,448},{384,256},{4... | collective-permute-start | bytes 1544 | tf_op jit(solution)/shard_map/ppermute | solution.py:293
  26.9 0.1 pad_add_fusion.place
  27.0 2.6 %collective-permute-done.5 = f32[1,128]{1,0:T(1,128)S(1)} collective-permute-done((f32[1,128]{1,0:T(1,128)S(1)}, f32[1,128]{1,0:T(1,128)S(1)}, u32[]{:S(2)}, u32[]{:S(2)}) %collective-permute-start.5) | collective-permute-done | bytes 544 | tf_op jit(solution)/shard_map/ppermute | solution.py:293
  29.6 4.3 %collective-permute-start.6 = (f32[1,128]{1,0:T(1,128)S(1)}, f32[1,128]{1,0:T(1,128)S(1)}, u32[]{:S(2)}, u32[]{:S(2)}) collective-permute-start(f32[1,128]{1,0:T(1,128)S(1)} %add.10), channel_id=1, source_target_pairs={{0,256},{64,320},{128,384},{192,448},{256,0},{320,64},{384,128},{4... | collective-permute-start | bytes 1544 | tf_op jit(solution)/shard_map/ppermute | solution.py:293
  34.6 0.1 pad.2.clone
  34.7 0.1 pad.3.clone
  34.8 4.1 %collective-permute-start.1 = (f32[3,2,128,128]{3,2,1,0:T(8,128)}, f32[3,2,128,128]{3,2,1,0:T(8,128)S(1)}, u32[]{:S(2)}, u32[]{:S(2)}) collective-permute-start(f32[3,2,128,128]{3,2,1,0:T(8,128)} %get-tuple-element.26), channel_id=1, source_target_pairs={{0,1},{1,2},{2,3},{3,0},{4,5},{5,6},{6,7},{7,4},{8,9},{9,10},{10,1... | collective-permute-start | bytes 1179656 | tf_op jit(solution)/shard_map/ppermute | solution.py:283
  38.8 0.0 collective-permute-done.6
  38.9 1.9 %collective-permute-start.3 = (f32[3,2,128,128]{3,2,1,0:T(8,128)}, f32[3,2,128,128]{3,2,1,0:T(8,128)S(1)}, u32[]{:S(2)}, u32[]{:S(2)}) collective-permute-start(f32[3,2,128,128]{3,2,1,0:T(8,128)} %get-tuple-element.27), channel_id=1, source_target_pairs={{0,3},{1,0},{2,1},{3,2},{4,7},{5,4},{6,5},{7,6},{8,11},{9,8},{10,9... | collective-permute-start | bytes 1179656 | tf_op jit(solution)/shard_map/ppermute | solution.py:283
  40.8 0.1 maximum_maximum_fusion
  40.9 39.4 %all-gather = f32[1152,128]{1,0:T(8,128)S(1)} all-gather(f32[72,128]{1,0:T(8,128)S(1)} %maximum_maximum_fusion), channel_id=2, replica_groups=mesh['group'=8,'slot'=16,'ctx'=4] {'slot'}, dimensions={0}, use_global_device_ids=true | all-gather | bytes 626688 | tf_op jit(solution)/shard_map/all_gather | solution.py:297
  80.3 0.0 collective-permute-done.7.refs_6_
  80.3 0.0 collective-permute-done.8.refs_8_
  80.3 0.0 collective-permute-done.2.refs_7_
  80.3 0.0 copy-done.4
  80.3 0.0 copy-done
  80.3 0.0 copy-done.1
  80.3 0.0 copy-done.2
  80.4 7.0 %shard_map.88 = (bf16[8,128,128]{2,1,0:T(8,128)(2,1)}, f32[8,128,128]{2,1,0:T(8,128)}, f32[8,128,128]{2,1,0:T(8,128)}, f32[8,128,128]{2,1,0:T(8,128)}, f32[8,128,128]{2,1,0:T(8,128)}) custom-call(s32[2]{0:T(128)S(1)} %pad_add_fusion.place, f32[32]{0:T(128)S(1)} %copy-done.4, f32[1]{0:T(128)} %bitcast.16.reward, bf16[128,4096]{1,0:T(8,128)(2,1)S(1)} %bitcast.27, ...), custom_call_target="tpu_custom_call" | custom-call | flops 1509949440 | bytes 7864320 | tf_op jit(solution)/shard_map/pallas_call | solution.py:220
  87.4 0.0 collective-permute-done.1.refs_6_
  87.4 0.0 collective-permute-done.3.refs_8_
  87.4 3.8 %shard_map.89 = (bf16[8,128,128]{2,1,0:T(8,128)(2,1)}, f32[8,128,128]{2,1,0:T(8,128)}, f32[8,128,128]{2,1,0:T(8,128)}, f32[8,128,128]{2,1,0:T(8,128)}, f32[8,128,128]{2,1,0:T(8,128)}) custom-call(s32[2]{0:T(128)S(1)} %pad_add_fusion.place, f32[32]{0:T(128)S(1)} %copy-done.4, ...), custom_call_target="tpu_custom_call", output_to_operand_aliasing={{0}: (14, {}), {1}: (15, {}), {2}: (16, {}), {3}: (17, {}),... | custom-call | flops 503316480 | bytes 2621440 | tf_op jit(solution)/shard_map/pallas_call | solution.py:220
  91.2 0.0 copy-start.3
  91.2 7.1 %all-to-all-start = ((f32[16,64,128]{2,1,0:T(8,128)}), f32[16,64,128]{2,1,0:T(8,128)S(1)}, u32[]{:S(2)}, u32[]{:S(2)}) async-start(f32[16,64,128]{2,1,0:T(8,128)} %bitcast.59), calls=%async_computation | async-start | bytes 1048576 | tf_op jit(solution)/shard_map/all_to_all | solution.py:307
  98.3 3.5 %collective-permute-start.9 = (f32[8,128,128]{2,1,0:T(8,128)}, f32[8,128,128]{2,1,0:T(8,128)S(1)}, u32[]{:S(2)}, u32[]{:S(2)}) collective-permute-start(f32[8,128,128]{2,1,0:T(8,128)} %get-tuple-element.38), channel_id=1, source_target_pairs={{0,2},{1,3},{2,0},{3,1},{4,6},{5,7},{6,4},{7,5},{8,10},{9,11},{10,... | collective-permute-start | bytes 1572872 | tf_op jit(solution)/shard_map/ppermute | solution.py:283
  101.8 3.4 %collective-permute-start.10 = (f32[8,128,128]{2,1,0:T(8,128)}, f32[8,128,128]{2,1,0:T(8,128)S(1)}, u32[]{:S(2)}, u32[]{:S(2)}) collective-permute-start(f32[8,128,128]{2,1,0:T(8,128)} %get-tuple-element.39), channel_id=1, source_target_pairs={{0,1},{1,2},{2,3},{3,0},{4,5},{5,6},{6,7},{7,4},{8,9},{9,10},{10,1... | collective-permute-start | bytes 1572872 | tf_op jit(solution)/shard_map/ppermute | solution.py:283
  105.2 2.7 %collective-permute-start.11 = (f32[8,128,128]{2,1,0:T(8,128)}, f32[8,128,128]{2,1,0:T(8,128)S(1)}, u32[]{:S(2)}, u32[]{:S(2)}) collective-permute-start(f32[8,128,128]{2,1,0:T(8,128)} %get-tuple-element.40), channel_id=1, source_target_pairs={{0,3},{1,0},{2,1},{3,2},{4,7},{5,4},{6,5},{7,6},{8,11},{9,8},{10,9... | collective-permute-start | bytes 1572872 | tf_op jit(solution)/shard_map/ppermute | solution.py:283
  107.9 15.8 %all-to-all-done = f32[16,64,128]{2,1,0:T(8,128)S(1)} async-done(((f32[16,64,128]{2,1,0:T(8,128)}), f32[16,64,128]{2,1,0:T(8,128)S(1)}, u32[]{:S(2)}, u32[]{:S(2)}) %all-to-all-start) | async-done | bytes 524320 | tf_op jit(solution)/shard_map/all_to_all | solution.py:307
  123.8 5.4 %collective-permute-start.12 = (f32[1,64,128]{2,1,0:T(8,128)S(1)}, f32[1,64,128]{2,1,0:T(8,128)S(1)}, u32[]{:S(2)}, u32[]{:S(2)}) collective-permute-start(f32[1,64,128]{2,1,0:T(8,128)S(1)} %bitcast.61), channel_id=1, source_target_pairs={{0,0},{1,4},{2,2},{3,6},{4,1},{5,5},{6,3},{7,7},{8,8},{9,12},{10,1... | collective-permute-start | bytes 98312 | tf_op jit(solution)/shard_map/ppermute | solution.py:309
  129.2 0.0 collective-permute-done.9.refs_1_
  129.2 0.0 collective-permute-done.10.refs_2_
  129.3 0.0 collective-permute-done.11.refs_3_
  129.3 0.0 copy-done.3
  129.3 1.7 %shard_map.90 = bf16[128,4096]{1,0:T(8,128)(2,1)} custom-call(s32[2]{0:T(128)S(1)} %pad_add_fusion.place, bf16[8,128,128]{2,1,0:T(8,128)(2,1)S(1)} %copy-done.3, f32[8,128,128]{2,1,0:T(8,128)S(1)} %collective-permute-done.9.refs_1_, f32[8,128,128]{2,1,0:T(8,128)S(1)} %collective-permute-done.10.refs_2_, f32[8,128,128]{2,1,0:T(8,128)S(1)} %collective-permute-done.11.refs_3_), custom_call_target="tpu_custom_call" | custom-call | bytes 3145728 | tf_op jit(solution)/shard_map/pallas_call | solution.py:251
  130.9 0.2 collective-permute-done.12
  131.1 0.6 copy.22
  (6 shorter events, 0.0 us)
Async XLA Ops:
  0.6 5.6 %copy-start.5 = (f32[1,64,128]{2,1,0:T(8,128)S(1)}, f32[1,64,128]{2,1,0:T(8,128)}, u32[]{:S(2)}) copy-start(f32[1,64,128]{2,1,0:T(8,128)} %param.13) | copy-start | bytes 98308
  2.9 77.4 %collective-permute-start.2 = (f32[3,8,128,128]{3,2,1,0:T(8,128)}, f32[3,8,128,128]{3,2,1,0:T(8,128)}, u32[]{:S(2)}, u32[]{:S(2)}) collective-permute-start(f32[3,8,128,128]{3,2,1,0:T(8,128)} %shard_map.87), channel_id=1, source_target_pairs={{0,2},{1,3},{2,0},{3,1},{4,6},{5,7},{6,4},{7,5},{8,10},{9,11},{10,... | collective-permute-start | bytes 4718600 | tf_op jit(solution)/shard_map/ppermute | solution.py:283
  6.3 74.1 %copy-start.4 = (f32[32]{0:T(128)S(1)}, f32[32]{0:T(128)}, u32[]{:S(2)}) copy-start(f32[32]{0:T(128)} %rates.3) | copy-start | bytes 388
  6.3 8.3 %collective-permute-start = (f32[64,128]{1,0:T(8,128)S(1)}, f32[64,128]{1,0:T(8,128)S(1)}, u32[]{:S(2)}, u32[]{:S(2)}) collective-permute-start(f32[64,128]{1,0:T(8,128)S(1)} %bitcast.62), channel_id=1, source_target_pairs={{0,0},{4,1},{2,2},{6,3},{1,4},{5,5},{3,6},{7,7},{8,8},{12,9},{10,1... | collective-permute-start | bytes 98312 | tf_op jit(solution)/shard_map/ppermute | solution.py:279
  9.5 70.9 %copy-start = (bf16[1,1,128,4096]{3,2,1,0:T(8,128)(2,1)S(1)}, bf16[1,1,128,4096]{3,2,1,0:T(8,128)(2,1)}, u32[]{:S(2)}) copy-start(bf16[1,1,128,4096]{3,2,1,0:T(8,128)(2,1)} %param.7) | copy-start | bytes 3145732
  9.5 70.9 %copy-start.1 = (bf16[1,1,128,4096]{3,2,1,0:T(8,128)(2,1)S(1)}, bf16[1,1,128,4096]{3,2,1,0:T(8,128)(2,1)}, u32[]{:S(2)}) copy-start(bf16[1,1,128,4096]{3,2,1,0:T(8,128)(2,1)} %param.8) | copy-start | bytes 3145732
  9.5 70.9 %copy-start.2 = (bf16[1,1,128,4096]{3,2,1,0:T(8,128)(2,1)S(1)}, bf16[1,1,128,4096]{3,2,1,0:T(8,128)(2,1)}, u32[]{:S(2)}) copy-start(bf16[1,1,128,4096]{3,2,1,0:T(8,128)(2,1)} %param.9) | copy-start | bytes 3145732
  14.6 65.8 %collective-permute-start.7 = (f32[3,6,128,128]{3,2,1,0:T(8,128)}, f32[3,6,128,128]{3,2,1,0:T(8,128)S(1)}, u32[]{:S(2)}, u32[]{:S(2)}) collective-permute-start(f32[3,6,128,128]{3,2,1,0:T(8,128)} %get-tuple-element.30), channel_id=1, source_target_pairs={{0,1},{1,2},{2,3},{3,0},{4,5},{5,6},{6,7},{7,4},{8,9},{9,10},{10,1... | collective-permute-start | bytes 3538952 | tf_op jit(solution)/shard_map/ppermute | solution.py:283
  18.4 61.9 %collective-permute-start.8 = (f32[3,6,128,128]{3,2,1,0:T(8,128)}, f32[3,6,128,128]{3,2,1,0:T(8,128)S(1)}, u32[]{:S(2)}, u32[]{:S(2)}) collective-permute-start(f32[3,6,128,128]{3,2,1,0:T(8,128)} %get-tuple-element.31), channel_id=1, source_target_pairs={{0,3},{1,0},{2,1},{3,2},{4,7},{5,4},{6,5},{7,6},{8,11},{9,8},{10,9... | collective-permute-start | bytes 3538952 | tf_op jit(solution)/shard_map/ppermute | solution.py:283
  21.2 3.0 %collective-permute-start.4 = (f32[1,128]{1,0:T(1,128)S(1)}, f32[1,128]{1,0:T(1,128)S(1)}, u32[]{:S(2)}, u32[]{:S(2)}) collective-permute-start(f32[1,128]{1,0:T(1,128)S(1)} %broadcast_in_dim.12), channel_id=1, source_target_pairs={{0,64},{64,0},{128,192},{192,128},{256,320},{320,256},{384,448},{4... | collective-permute-start | bytes 1544 | tf_op jit(solution)/shard_map/ppermute | solution.py:293
  24.2 5.4 %collective-permute-start.5 = (f32[1,128]{1,0:T(1,128)S(1)}, f32[1,128]{1,0:T(1,128)S(1)}, u32[]{:S(2)}, u32[]{:S(2)}) collective-permute-start(f32[1,128]{1,0:T(1,128)S(1)} %add.9), channel_id=1, source_target_pairs={{0,128},{64,192},{128,0},{192,64},{256,384},{320,448},{384,256},{4... | collective-permute-start | bytes 1544 | tf_op jit(solution)/shard_map/ppermute | solution.py:293
  29.6 9.2 %collective-permute-start.6 = (f32[1,128]{1,0:T(1,128)S(1)}, f32[1,128]{1,0:T(1,128)S(1)}, u32[]{:S(2)}, u32[]{:S(2)}) collective-permute-start(f32[1,128]{1,0:T(1,128)S(1)} %add.10), channel_id=1, source_target_pairs={{0,256},{64,320},{128,384},{192,448},{256,0},{320,64},{384,128},{4... | collective-permute-start | bytes 1544 | tf_op jit(solution)/shard_map/ppermute | solution.py:293
  34.8 52.6 %collective-permute-start.1 = (f32[3,2,128,128]{3,2,1,0:T(8,128)}, f32[3,2,128,128]{3,2,1,0:T(8,128)S(1)}, u32[]{:S(2)}, u32[]{:S(2)}) collective-permute-start(f32[3,2,128,128]{3,2,1,0:T(8,128)} %get-tuple-element.26), channel_id=1, source_target_pairs={{0,1},{1,2},{2,3},{3,0},{4,5},{5,6},{6,7},{7,4},{8,9},{9,10},{10,1... | collective-permute-start | bytes 1179656 | tf_op jit(solution)/shard_map/ppermute | solution.py:283
  38.9 48.5 %collective-permute-start.3 = (f32[3,2,128,128]{3,2,1,0:T(8,128)}, f32[3,2,128,128]{3,2,1,0:T(8,128)S(1)}, u32[]{:S(2)}, u32[]{:S(2)}) collective-permute-start(f32[3,2,128,128]{3,2,1,0:T(8,128)} %get-tuple-element.27), channel_id=1, source_target_pairs={{0,3},{1,0},{2,1},{3,2},{4,7},{5,4},{6,5},{7,6},{8,11},{9,8},{10,9... | collective-permute-start | bytes 1179656 | tf_op jit(solution)/shard_map/ppermute | solution.py:283
  91.2 38.1 %copy-start.3 = (bf16[8,128,128]{2,1,0:T(8,128)(2,1)S(1)}, bf16[8,128,128]{2,1,0:T(8,128)(2,1)}, u32[]{:S(2)}) copy-start(bf16[8,128,128]{2,1,0:T(8,128)(2,1)} %get-tuple-element.37.refs_0_) | copy-start | bytes 786436
  91.2 32.6 %all-to-all-start = ((f32[16,64,128]{2,1,0:T(8,128)}), f32[16,64,128]{2,1,0:T(8,128)S(1)}, u32[]{:S(2)}, u32[]{:S(2)}) async-start(f32[16,64,128]{2,1,0:T(8,128)} %bitcast.59), calls=%async_computation | async-start | bytes 1048576 | tf_op jit(solution)/shard_map/all_to_all | solution.py:307
  98.3 31.0 %collective-permute-start.9 = (f32[8,128,128]{2,1,0:T(8,128)}, f32[8,128,128]{2,1,0:T(8,128)S(1)}, u32[]{:S(2)}, u32[]{:S(2)}) collective-permute-start(f32[8,128,128]{2,1,0:T(8,128)} %get-tuple-element.38), channel_id=1, source_target_pairs={{0,2},{1,3},{2,0},{3,1},{4,6},{5,7},{6,4},{7,5},{8,10},{9,11},{10,... | collective-permute-start | bytes 1572872 | tf_op jit(solution)/shard_map/ppermute | solution.py:283
  101.8 27.4 %collective-permute-start.10 = (f32[8,128,128]{2,1,0:T(8,128)}, f32[8,128,128]{2,1,0:T(8,128)S(1)}, u32[]{:S(2)}, u32[]{:S(2)}) collective-permute-start(f32[8,128,128]{2,1,0:T(8,128)} %get-tuple-element.39), channel_id=1, source_target_pairs={{0,1},{1,2},{2,3},{3,0},{4,5},{5,6},{6,7},{7,4},{8,9},{9,10},{10,1... | collective-permute-start | bytes 1572872 | tf_op jit(solution)/shard_map/ppermute | solution.py:283
  105.2 24.0 %collective-permute-start.11 = (f32[8,128,128]{2,1,0:T(8,128)}, f32[8,128,128]{2,1,0:T(8,128)S(1)}, u32[]{:S(2)}, u32[]{:S(2)}) collective-permute-start(f32[8,128,128]{2,1,0:T(8,128)} %get-tuple-element.40), channel_id=1, source_target_pairs={{0,3},{1,0},{2,1},{3,2},{4,7},{5,4},{6,5},{7,6},{8,11},{9,8},{10,9... | collective-permute-start | bytes 1572872 | tf_op jit(solution)/shard_map/ppermute | solution.py:283
  123.8 7.3 %collective-permute-start.12 = (f32[1,64,128]{2,1,0:T(8,128)S(1)}, f32[1,64,128]{2,1,0:T(8,128)S(1)}, u32[]{:S(2)}, u32[]{:S(2)}) collective-permute-start(f32[1,64,128]{2,1,0:T(8,128)S(1)} %bitcast.61), channel_id=1, source_target_pairs={{0,0},{1,4},{2,2},{3,6},{4,1},{5,5},{6,3},{7,7},{8,8},{9,12},{10,1... | collective-permute-start | bytes 98312 | tf_op jit(solution)/shard_map/ppermute | solution.py:309
